TPU v7x, 32 devices: a whole 2x2x4 slice. The times are simulated.
32 devices in a mesh: row: 8 (over z, core), col: 4 (over y, x).
Axes of the slice: x: 2, y: 2, z: 4, core: 2. Of those that a mesh axis runs over, the one named last changes fastest.
Arguments:
- queries: bfloat16 [1024, 2048], P('row'), may hold values from -18 to 18
- keys: bfloat16 [1024, 1024], P(('row', 'col')), may hold values from -6 to 6
- values: bfloat16 [1024, 1024], P(('row', 'col')), may hold values from -6 to 6
Outputs:
- attended: bfloat16 [1024, 2048], P(('row', 'col'))
All inputs are finite; a program needn't handle non-finite values.
Results may differ from a plain program's by a relative error of at most 0.0095.
Values may be sent and summed in bfloat16 or wider, within the bound.
No kernel may reach another device: no remote copies, remote signals or barrier semaphores. Data moves between devices by JAX's collectives and lax.ppermute only.
A program may use at most 64 MiB of HBM per device.

v0:
```python
import jax
import jax.numpy as jnp
from jax import lax
from jax.sharding import PartitionSpec as P

HEAD_SIZE = 256


SCALE = 0.0625
CAP = 50.0


def per_device(queries, keys, values):
    blk = keys.shape[0]
    feat = queries.shape[1]
    heads_q = feat // HEAD_SIZE
    heads_kv = keys.shape[1] // HEAD_SIZE
    head_group = heads_q // heads_kv
    n_row = lax.axis_size("row")
    n_col = lax.axis_size("col")
    row = lax.axis_index("row")
    col = lax.axis_index("col")
    half = n_col // 2
    rows_all = n_col * blk
    rows_half = half * blk
    key_all, value_all = (
        lax.all_gather(keys, "row", axis=0, tiled=True),
        lax.all_gather(values, "row", axis=0, tiled=True),
    )
    index_q = jnp.arange(rows_all, dtype=jnp.int32)
    col_block = index_q // blk
    span = jnp.where(col_block < half, row, row)
    query_pos = (span * n_col + col_block) * blk + index_q % blk
    index_k = jnp.arange(n_row * blk, dtype=jnp.int32)
    key_pos = (index_k // blk * n_col + col) * blk + index_k % blk
    tile = 8 * blk
    tiles = n_row // 8
    numer_parts = []
    denom_parts = []
    for which in range(2):
        query_half = queries[which * rows_half : (which + 1) * rows_half].reshape(
            rows_half, heads_kv, head_group, HEAD_SIZE
        )
        pos_half = query_pos[which * rows_half : (which + 1) * rows_half]
        latest = pos_half[rows_half - 1]

        def attend(carry, start, query_half=query_half, pos_half=pos_half):
            numer, denom = carry
            key_tile = lax.dynamic_slice_in_dim(key_all, start, tile, 0).reshape(
                tile, heads_kv, HEAD_SIZE
            )
            value_tile = lax.dynamic_slice_in_dim(value_all, start, tile, 0).reshape(
                tile, heads_kv, HEAD_SIZE
            )
            pos_tile = lax.dynamic_slice_in_dim(key_pos, start, tile, 0)
            scores = (
                jnp.einsum(
                    "qkgd,nkd->kgqn", query_half, key_tile, preferred_element_type=jnp.float32
                )
                * SCALE
            )
            capped = CAP * jnp.tanh(scores / CAP)
            allowed = pos_tile[None, :] <= pos_half[:, None]
            weights = jnp.where(allowed[None, None], jnp.exp(capped), jnp.float32(0.0))
            denom = denom + jnp.sum(weights, axis=-1)
            rounded_length = weights.astype(jnp.bfloat16)
            contrib = jnp.einsum(
                "kgqn,nkd->qkgd", rounded_length, value_tile, preferred_element_type=jnp.float32
            )
            return (numer + contrib.reshape(rows_half, feat), denom)

        def step(turn, carry, attend=attend, latest=latest):
            start = (turn * tile).astype(jnp.int32)
            needed = key_pos[start] <= latest
            return lax.cond(needed, lambda c: attend(c, start), lambda c: c, carry)

        start_carry = (
            jnp.zeros((rows_half, feat), jnp.float32),
            jnp.zeros((heads_kv, head_group, rows_half), jnp.float32),
        )
        numer_half, denom_half = lax.fori_loop(0, tiles, step, start_carry)
        numer_parts.append(numer_half)
        denom_parts.append(denom_half)
    numer_all = jnp.concatenate(numer_parts, axis=0)
    denom_all = jnp.transpose(jnp.concatenate(denom_parts, axis=2), (2, 0, 1)).reshape(
        rows_all, heads_q
    )
    numer_mine = lax.psum_scatter(
        numer_all.astype(jnp.bfloat16), "col", scatter_dimension=0, tiled=True
    ).astype(jnp.float32)
    denom_total = lax.psum(denom_all, "col")
    denom_mine = lax.dynamic_slice_in_dim(denom_total, col * blk, blk, 0)
    result = (
        (numer_mine.reshape(blk, heads_q, HEAD_SIZE) / denom_mine[:, :, None])
        .reshape(blk, feat)
        .astype(jnp.bfloat16)
    )
    return result


def solution(mesh):
    return jax.shard_map(
        per_device,
        mesh=mesh,
        in_specs=(P("row", None), P(("row", "col"), None), P(("row", "col"), None)),
        out_specs=P(("row", "col"), None),
        check_vma=False,
    )
```

profile of v0, /device:TPU:0, one launch (start us, length us, event | category | flops | bytes accessed | tf_op | source)
XLA Modules:
  0.0 83.4 jit_solution(8258094161155596511)
XLA Ops:
  6.6 0.5 dynamic_slice.10
  7.1 0.6 fusion.29
  10.3 16.9 %all_gather.6 = bf16[256,1024]{1,0:T(8,128)(2,1)S(1)} all-gather(bf16[32,1024]{1,0:T(8,128)(2,1)} %param.8), channel_id=1, replica_groups=mesh['row'=8,'col'=4] {'row'}, dimensions={0}, use_global_device_ids=true | all-gather | bytes 589824 | tf_op jit(solution)/shard_map/all_gather | solution.py:27
  27.2 14.8 %all_gather.7 = bf16[256,1024]{1,0:T(8,128)(2,1)S(1)} all-gather(bf16[32,1024]{1,0:T(8,128)(2,1)S(1)} %copy-done.1), channel_id=1, replica_groups=mesh['row'=8,'col'=4] {'row'}, dimensions={0}, use_global_device_ids=true | all-gather | bytes 589824 | tf_op jit(solution)/shard_map/all_gather | solution.py:28
  42.1 2.8 %conditional.3 = (f32[4,2,64]{2,1,0:T(2,128)S(1)}, f32[64,2048]{1,0:T(8,128)S(1)}) conditional(s32[]{:T(128)} %bitcast.9, (f32[64,2048]{1,0:T(8,128)S(1)}, f32[4,2,64]{2,1,0:T(2,128)S(1)}) %tuple.27, (s32[256]{0:T(256)S(1)}, s32[128]{0:T(128)S(1)}, bf16[256,1024]{1,0:T(8,128)(2,1)S(1)}, bf16[128,2048]{1,0:T(8,128)(2,1)S(1)}, ...), branch_computations={%region_3.4_spmd, %region_4.6_spmd} | conditional | flops 135020544 | bytes 9217808 | solution.py:75
  42.3 0.2 reshape.95
  42.5 0.4 reshape.94
  42.9 0.4 fusion.28
  43.4 0.4 reshape.96
  43.7 0.2 convolution_bitcast_fusion.1
  44.0 0.4 copy.16
  44.4 0.4 reshape.97
  44.9 2.7 %conditional.2 = (f32[4,2,64]{2,1,0:T(2,128)S(1)}, f32[64,2048]{1,0:T(8,128)S(1)}) conditional(s32[]{:T(128)} %bitcast.8, (f32[64,2048]{1,0:T(8,128)S(1)}, f32[4,2,64]{2,1,0:T(2,128)S(1)}) %tuple.27, (s32[256]{0:T(256)S(1)}, s32[128]{0:T(128)S(1)}, bf16[256,1024]{1,0:T(8,128)(2,1)S(1)}, bf16[128,2048]{1,0:T(8,128)(2,1)S(1)}, ...), branch_computations={%region_0.1_spmd, %region_1.3_spmd} | conditional | flops 135020544 | bytes 9217296 | solution.py:75
  45.1 0.2 reshape.91
  45.3 0.4 reshape.90
  45.6 0.4 fusion.27
  46.1 0.4 reshape.92
  46.5 0.2 convolution_bitcast_fusion
  46.7 0.4 copy.12
  47.1 0.4 reshape.93
  47.8 0.8 pad_maximum_fusion
  48.7 8.9 %psum.7 = f32[128,8]{0,1:T(8,128)S(1)} all-reduce(f32[128,8]{0,1:T(8,128)S(1)} %bitcast.32), channel_id=1, replica_groups=mesh['row'=8,'col'=4] {'col'}, use_global_device_ids=true, to_apply=%region_7.8 | all-reduce | flops 1024 | bytes 8192 | tf_op jit(solution)/shard_map/psum | solution.py:91
  58.0 17.0 %reduce-scatter.2.cloned.1.call-done = bf16[32,2048]{1,0:T(8,128)(2,1)} async-done(((bf16[128,2048]{1,0:T(8,128)(2,1)}), bf16[32,2048]{1,0:T(8,128)(2,1)}) %reduce-scatter.2.cloned.1.call-update) | async-done | bytes 131088 | tf_op jit(solution)/shard_map/reduce_scatter | solution.py:88
  75.0 1.6 %divide_convert_fusion = bf16[32,2048]{1,0:T(8,128)(2,1)} fusion(f32[32,2048]{1,0:T(8,128)S(1)} %bitcast.28, bf16[32,2048]{1,0:T(8,128)(2,1)} %reduce-scatter.2.cloned.1.call-done), kind=kLoop, calls=%fused_computation.25 | loop fusion | flops 196608 | bytes 524288 | tf_op jit(solution)/shard_map/convert_element_type | solution.py:96
  (26 shorter events, 1.1 us)
Async XLA Ops:
  6.5 68.4 %reduce-scatter.2.cloned.1.call-start = ((), (), s32[]{:S(2)}) async-start(), calls=%async_computation.1 | async-start | bytes 655360 | tf_op jit(solution)/shard_map/reduce_scatter | solution.py:88
  10.3 16.9 %copy-start.1 = (bf16[32,1024]{1,0:T(8,128)(2,1)S(1)}, bf16[32,1024]{1,0:T(8,128)(2,1)}, u32[]{:S(2)}) copy-start(bf16[32,1024]{1,0:T(8,128)(2,1)} %param.9) | copy-start | bytes 196612
  27.2 14.9 %copy-start = (bf16[128,2048]{1,0:T(8,128)(2,1)S(1)}, bf16[128,2048]{1,0:T(8,128)(2,1)}, u32[]{:S(2)}) copy-start(bf16[128,2048]{1,0:T(8,128)(2,1)} %param.7) | copy-start | bytes 1572868
Sparse Core Ops, SparseCore 0:
  48.7 26.1 reduce-scatter.1
where the time goes:
time: 83.7 us; the launch traced here: 83.4 us
  blocking collectives  40.7 us (49%)
  waiting for transfers between devices  17 us (20%)
  between operations  16 us (19%)
  local copies, waits for them, and re-layouts  5.17 us (6%)
  other arithmetic  2.99 us (4%)
  matrix products  1.34 us (2%)
    reduce_scatter x1, waiting for transfers between devices, per_device(): lax.psum_scatter(numer_all.astype(jnp.bfloat16), 'col', scatter_dimension...  17 us
    all_gather x1, blocking collectives, per_device(): lax.all_gather(keys, 'row', axis=0, tiled=True)  16.9 us
    all_gather x1, blocking collectives, per_device(): lax.all_gather(values, 'row', axis=0, tiled=True)  14.8 us
    psum x1, blocking collectives, per_device(): denom_total = lax.psum(denom_all, 'col')  8.94 us
  transfers between devices with their start and end apart: 1, of which 1 were waited for; matrix products, arithmetic and copies ran while one was open for 0% of the time, Pallas kernels for 0%

commit v1 on v0

v1 whole, which is shorter than its diff:
```python
import math

import jax
import jax.numpy as jnp
from jax import lax
from jax.experimental import pallas as pl
from jax.experimental.pallas import tpu as pltpu
from jax.sharding import PartitionSpec as P

HEAD = 256
SCALE = 0.0625
CAP = 50.0
LANES = 128


def attend_kernel(order, blk, n_col, q_ref, *refs):
    n_src = len(order)
    srcs, outs = refs[:n_src], refs[n_src : n_src + n_col]
    k_all, v_all = refs[n_src + n_col :]
    row, col = lax.axis_index("row"), lax.axis_index("col")
    feat_q, feat_k = q_ref.shape[1], srcs[0].shape[1]
    kv_heads = feat_k // HEAD
    group = feat_q // feat_k
    span = n_col * blk
    n_keys = n_src * blk
    for t, src in enumerate(srcs):
        k_all[t * blk : (t + 1) * blk, :] = src[:blk, :]
        v_all[t * blk : (t + 1) * blk, :] = src[blk:, :]
    lane = lax.broadcasted_iota(jnp.int32, (1, n_keys), 1)
    key_pos = jnp.zeros((1, n_keys), jnp.int32)
    for t, mask in enumerate(order):
        start = ((row ^ mask) * n_col + col) * blk
        key_pos = jnp.where(lane // blk == t, start + lane % blk, key_pos)
    chunk = min(n_col, 4)
    for base in range(0, n_col, chunk):
        parts = [pl.ds(pl.multiple_of((col ^ j) * blk, blk), blk) for j in range(base, base + chunk)]
        sub = lax.broadcasted_iota(jnp.int32, (blk, 1), 0)
        pos = jnp.concatenate(
            [row * span + (col ^ j) * blk + sub for j in range(base, base + chunk)], axis=0
        )
        rows = chunk * blk
        keep = jnp.where(key_pos <= pos, 1.0, 0.0).astype(jnp.float32)
        tail_lane = lax.broadcasted_iota(jnp.int32, (rows, LANES), 1)
        high = jnp.zeros((rows, LANES), jnp.float32)
        low = jnp.zeros((rows, LANES), jnp.float32)
        for kv in range(kv_heads):
            k_head = k_all[:, kv * HEAD : (kv + 1) * HEAD]
            v_head = v_all[:, kv * HEAD : (kv + 1) * HEAD]
            for g in range(group):
                h = kv * group + g
                q_head = jnp.concatenate(
                    [q_ref[part, h * HEAD : (h + 1) * HEAD] for part in parts], axis=0
                )
                scores = lax.dot_general(
                    q_head, k_head, (((1,), (1,)), ((), ())), preferred_element_type=jnp.float32
                )
                capped = jnp.tanh(scores * (SCALE / CAP)) * (CAP / math.log(2.0))
                weights = jnp.exp2(capped) * keep
                denom = jnp.sum(weights, axis=1, keepdims=True)
                numer = jnp.dot(
                    weights.astype(jnp.bfloat16), v_head, preferred_element_type=jnp.float32
                ).astype(jnp.bfloat16)
                for i in range(chunk):
                    outs[base + i][:, h * HEAD : (h + 1) * HEAD] = numer[i * blk : (i + 1) * blk]
                rounded = denom.astype(jnp.bfloat16).astype(jnp.float32)
                high = jnp.where(tail_lane == h, rounded, high)
                low = jnp.where(tail_lane == h, denom - rounded, low)
        for i in range(chunk):
            part = slice(i * blk, (i + 1) * blk)
            outs[base + i][:, feat_q : feat_q + LANES] = high[part].astype(jnp.bfloat16)
            outs[base + i][:, feat_q + LANES :] = low[part].astype(jnp.bfloat16)


def combine_kernel(*refs):
    parts, out_ref = refs[:-1], refs[-1]
    feat_q = out_ref.shape[1]
    tail = sum(p[:, feat_q:].astype(jnp.float32) for p in parts)
    denom = tail[:, :LANES] + tail[:, LANES:]
    for h in range(feat_q // HEAD):
        cut = slice(h * HEAD, (h + 1) * HEAD)
        numer = sum(p[:, cut].astype(jnp.float32) for p in parts)
        out_ref[:, cut] = (numer / denom[:, h : h + 1]).astype(jnp.bfloat16)


def per_device(queries, keys, values):
    blk, feat_k = keys.shape
    feat_q = queries.shape[1]
    n_row = lax.axis_size("row")
    n_col = lax.axis_size("col")

    def swap_row(x, mask):
        return lax.ppermute(x, "row", [(i, i ^ mask) for i in range(n_row)])

    def swap_col(x, mask):
        return lax.ppermute(x, "col", [(i, i ^ mask) for i in range(n_col)])

    own = jnp.concatenate([keys, values], axis=0)
    blocks = {0: own}
    for mask in range(2, n_row, 2):
        blocks[mask] = swap_row(own, mask)
    for mask in range(0, n_row, 2):
        blocks[mask ^ 1] = swap_row(blocks[mask], 1)
    order = sorted(blocks)
    n_keys = n_row * blk
    vmem = pl.BlockSpec(memory_space=pltpu.VMEM)
    wide = feat_q + 2 * LANES
    messages = pl.pallas_call(
        lambda *refs: attend_kernel(order, blk, n_col, *refs),
        out_shape=[jax.ShapeDtypeStruct((blk, wide), jnp.bfloat16)] * n_col,
        in_specs=[vmem] * (1 + n_row),
        out_specs=[vmem] * n_col,
        scratch_shapes=[
            pltpu.VMEM((n_keys, feat_k), jnp.bfloat16),
            pltpu.VMEM((n_keys, feat_k), jnp.bfloat16),
        ],
        compiler_params=pltpu.CompilerParams(vmem_limit_bytes=40 * 2**20),
        name="attend",
    )(queries, *[blocks[m] for m in order])
    received = [messages[0]] + [swap_col(messages[j], j) for j in range(1, n_col)]
    return pl.pallas_call(
        combine_kernel,
        out_shape=jax.ShapeDtypeStruct((blk, feat_q), jnp.bfloat16),
        in_specs=[vmem] * n_col,
        out_specs=vmem,
        name="combine",
    )(*received)


def solution(mesh):
    return jax.shard_map(
        per_device,
        mesh=mesh,
        in_specs=(P("row", None), P(("row", "col"), None), P(("row", "col"), None)),
        out_specs=P(("row", "col"), None),
        check_vma=False,
    )
```

time: 83.7 us -> 35.4 us (0.42)
  blocking collectives: 40.7 us -> 0 us
  between operations: 16 us -> 0.04 us
  starting transfers between devices: 0.01 us -> 9.76 us
  Pallas kernels: 0 us -> 3.67 us
  other arithmetic: 2.99 us -> 0 us
  local copies, waits for them, and re-layouts: 5.17 us -> 3.27 us
  waiting for transfers between devices: 17 us -> 18.4 us
  matrix products: 1.34 us -> 0 us
    all_gather x2 -> x0, blocking collectives: 31.8 us -> none  [the longest x1 16.9 us: per_device(): lax.all_gather(keys, 'row', axis=0, tiled=True)]
    ppermute x0 -> x10, waiting for transfers between devices: none -> 18.4 us  [the longest x7 11.4 us: swap_row(): return lax.ppermute(x, 'row', [(i, i ^ mask) for i in range(n_row)])]
    reduce_scatter x1 -> x0, waiting for transfers between devices: 17 us -> none  [per_device(): lax.psum_scatter(numer_all.astype(jnp.bfloat16), 'col', scatter_dimension...]
    ppermute x0 -> x10, starting transfers between devices: none -> 9.76 us  [the longest x7 6.27 us: swap_row(): return lax.ppermute(x, 'row', [(i, i ^ mask) for i in range(n_row)])]
    psum x1 -> x0, blocking collectives: 8.94 us -> none  [per_device(): denom_total = lax.psum(denom_all, 'col')]
    pallas_call x0 -> x2, Pallas kernels: none -> 3.67 us  [the longest x1 1.9 us: per_device(): pl.pallas_call(combine_kernel, out_shape=jax.ShapeDtypeStruct((blk, feat_...]
    unnamed x5 -> x13, local copies, waits for them, and re-layouts: 0.09 us -> 3.27 us
    reshape x8 -> x0, local copies, waits for them, and re-layouts: 2.71 us -> none  [the longest x2 0.84 us: attend(): return (numer + contrib.reshape(rows_half, feat), denom)]
  transfers between devices with their start and end apart: 1 -> 10, of which waited for: 1 -> 6; matrix products, arithmetic and copies ran while one was open for 0% -> 0% of each run, Pallas kernels for 0% -> 0%
where the time goes in v1:
time: 35.4 us; the launch traced here: 35.2 us
  waiting for transfers between devices  18.4 us (52%)
  starting transfers between devices  9.76 us (28%)
  Pallas kernels  3.67 us (10%)
  local copies, waits for them, and re-layouts  3.27 us (9%)
    ppermute x7, waiting for transfers between devices, swap_row(): return lax.ppermute(x, 'row', [(i, i ^ mask) for i in range(n_row)])  11.4 us
    ppermute x3, waiting for transfers between devices, swap_col(): return lax.ppermute(x, 'col', [(i, i ^ mask) for i in range(n_col)])  6.96 us
    ppermute x7, starting transfers between devices, swap_row(): return lax.ppermute(x, 'row', [(i, i ^ mask) for i in range(n_row)])  6.27 us
    ppermute x3, starting transfers between devices, swap_col(): return lax.ppermute(x, 'col', [(i, i ^ mask) for i in range(n_col)])  3.49 us
    unnamed x13, local copies, waits for them, and re-layouts  3.27 us
    pallas_call x1, Pallas kernels, per_device(): pl.pallas_call(combine_kernel, out_shape=jax.ShapeDtypeStruct((blk, feat_...  1.9 us
    pallas_call x1, Pallas kernels, per_device(): pl.pallas_call(lambda *refs: attend_kernel(order, blk, n_col, *refs), out...  1.77 us
  transfers between devices with their start and end apart: 10, of which 6 were waited for; matrix products, arithmetic and copies ran while one was open for 0% of the time, Pallas kernels for 0%

profile of v1, /device:TPU:0, one launch (start us, length us, event | category | flops | bytes accessed | tf_op | source)
XLA Modules:
  0.0 35.2 jit_solution(14448635734442759120)
XLA Ops:
  0.0 0.9 %constant_dynamic-update-slice_fusion.1 = bf16[64,1024]{1,0:T(8,128)(2,1)S(1)} fusion(bf16[32,1024]{1,0:T(8,128)(2,1)} %param.4), kind=kLoop, calls=%fused_computation.1 | loop fusion | bytes 131072
  0.9 5.1 %collective-permute-start.5 = (bf16[64,1024]{1,0:T(8,128)(2,1)S(1)}, bf16[64,1024]{1,0:T(8,128)(2,1)S(1)}, u32[]{:S(2)}, u32[]{:S(2)}) collective-permute-start(bf16[64,1024]{1,0:T(8,128)(2,1)S(1)} %constant_dynamic-update-slice_fusion.refs_1_), channel_id=1, source_target_pairs={{0,24},{4,28},{8,16},{12,20},{16,8},{20,12},{24,0},{28,4},{1,25},{... | collective-permute-start | bytes 393224 | tf_op jit(solution)/shard_map/ppermute | solution.py:92
  6.0 0.6 %collective-permute-start.1 = (bf16[64,1024]{1,0:T(8,128)(2,1)S(1)}, bf16[64,1024]{1,0:T(8,128)(2,1)S(1)}, u32[]{:S(2)}, u32[]{:S(2)}) collective-permute-start(bf16[64,1024]{1,0:T(8,128)(2,1)S(1)} %constant_dynamic-update-slice_fusion.refs_1_), channel_id=1, source_target_pairs={{0,8},{4,12},{8,0},{12,4},{16,24},{20,28},{24,16},{28,20},{1,9},{5... | collective-permute-start | bytes 393224 | tf_op jit(solution)/shard_map/ppermute | solution.py:92
  6.7 3.8 %collective-permute-done.5.refs_7_ = bf16[64,1024]{1,0:T(8,128)(2,1)S(1)} collective-permute-done((bf16[64,1024]{1,0:T(8,128)(2,1)S(1)}, bf16[64,1024]{1,0:T(8,128)(2,1)S(1)}, u32[]{:S(2)}, u32[]{:S(2)}) %collective-permute-start.5) | collective-permute-done | bytes 131104 | tf_op jit(solution)/shard_map/ppermute | solution.py:92
  10.4 0.0 collective-permute-start.6
  10.4 6.6 %collective-permute-done.3.refs_5_ = bf16[64,1024]{1,0:T(8,128)(2,1)S(1)} collective-permute-done((bf16[64,1024]{1,0:T(8,128)(2,1)S(1)}, bf16[64,1024]{1,0:T(8,128)(2,1)S(1)}, u32[]{:S(2)}, u32[]{:S(2)}) %collective-permute-start.3) | collective-permute-done | bytes 131104 | tf_op jit(solution)/shard_map/ppermute | solution.py:92
  17.1 0.0 collective-permute-start.4
  17.1 0.0 collective-permute-done.1.refs_3_
  17.1 0.5 %collective-permute-start.2 = (bf16[64,1024]{1,0:T(8,128)(2,1)S(1)}, bf16[64,1024]{1,0:T(8,128)(2,1)S(1)}, u32[]{:S(2)}, u32[]{:S(2)}) collective-permute-start(bf16[64,1024]{1,0:T(8,128)(2,1)S(1)} %collective-permute-done.1.refs_3_), channel_id=1, source_target_pairs={{0,4},{4,0},{8,12},{12,8},{16,20},{20,16},{24,28},{28,24},{1,5},{5... | collective-permute-start | bytes 393224 | tf_op jit(solution)/shard_map/ppermute | solution.py:92
  17.6 0.0 collective-permute-done.refs_2_
  17.6 0.0 collective-permute-done.6.refs_8_
  17.6 0.8 %collective-permute-done.4.refs_6_ = bf16[64,1024]{1,0:T(8,128)(2,1)S(1)} collective-permute-done((bf16[64,1024]{1,0:T(8,128)(2,1)S(1)}, bf16[64,1024]{1,0:T(8,128)(2,1)S(1)}, u32[]{:S(2)}, u32[]{:S(2)}) %collective-permute-start.4) | collective-permute-done | bytes 131104 | tf_op jit(solution)/shard_map/ppermute | solution.py:92
  18.4 0.2 collective-permute-done.2.refs_4_
  18.6 1.0 %copy-done = bf16[128,2048]{1,0:T(8,128)(2,1)S(1)} copy-done((bf16[128,2048]{1,0:T(8,128)(2,1)S(1)}, bf16[128,2048]{1,0:T(8,128)(2,1)}, u32[]{:S(2)}) %copy-start) | copy-done | bytes 524312
  19.7 1.8 %attend.1 = (bf16[32,2304]{1,0:T(8,128)(2,1)S(1)}, bf16[32,2304]{1,0:T(8,128)(2,1)S(1)}, bf16[32,2304]{1,0:T(8,128)(2,1)S(1)}, bf16[32,2304]{1,0:T(8,128)(2,1)S(1)}) custom-call(bf16[128,2048]{1,0:T(8,128)(2,1)S(1)} %copy-done, bf16[64,1024]{1,0:T(8,128)(2,1)S(1)} %constant_dynamic-update-slice_fusion.refs_1_, ...), custom_call_target="tpu_custom_call" | custom-call | tf_op jit(solution)/shard_map/attend/pallas_call | solution.py:107
  21.4 0.7 %copy-done.1 = bf16[32,2304]{1,0:T(8,128)(2,1)} copy-done((bf16[32,2304]{1,0:T(8,128)(2,1)}, bf16[32,2304]{1,0:T(8,128)(2,1)S(1)}, u32[]{:S(2)}) %copy-start.1) | copy-done | bytes 147480
  22.1 1.5 %collective-permute-start.7 = (bf16[32,2304]{1,0:T(8,128)(2,1)S(1)}, bf16[32,2304]{1,0:T(8,128)(2,1)S(1)}, u32[]{:S(2)}, u32[]{:S(2)}) collective-permute-start(bf16[32,2304]{1,0:T(8,128)(2,1)S(1)} %get-tuple-element.10), channel_id=1, source_target_pairs={{0,1},{1,0},{2,3},{3,2},{4,5},{5,4},{6,7},{7,6},{8,9},{9,8},{10,11... | collective-permute-start | bytes 442376 | tf_op jit(solution)/shard_map/ppermute | solution.py:95
  23.6 1.5 %collective-permute-start.8 = (bf16[32,2304]{1,0:T(8,128)(2,1)S(1)}, bf16[32,2304]{1,0:T(8,128)(2,1)S(1)}, u32[]{:S(2)}, u32[]{:S(2)}) collective-permute-start(bf16[32,2304]{1,0:T(8,128)(2,1)S(1)} %get-tuple-element.11), channel_id=1, source_target_pairs={{0,2},{1,3},{2,0},{3,1},{4,6},{5,7},{6,4},{7,5},{8,10},{9,11},{10,... | collective-permute-start | bytes 442376 | tf_op jit(solution)/shard_map/ppermute | solution.py:95
  25.1 0.5 %collective-permute-start.9 = (bf16[32,2304]{1,0:T(8,128)(2,1)S(1)}, bf16[32,2304]{1,0:T(8,128)(2,1)S(1)}, u32[]{:S(2)}, u32[]{:S(2)}) collective-permute-start(bf16[32,2304]{1,0:T(8,128)(2,1)S(1)} %get-tuple-element.12), channel_id=1, source_target_pairs={{0,3},{1,2},{2,1},{3,0},{4,7},{5,6},{6,5},{7,4},{8,11},{9,10},{10,... | collective-permute-start | bytes 442376 | tf_op jit(solution)/shard_map/ppermute | solution.py:95
  25.6 3.2 %collective-permute-done.7.refs_1_ = bf16[32,2304]{1,0:T(8,128)(2,1)S(1)} collective-permute-done((bf16[32,2304]{1,0:T(8,128)(2,1)S(1)}, bf16[32,2304]{1,0:T(8,128)(2,1)S(1)}, u32[]{:S(2)}, u32[]{:S(2)}) %collective-permute-start.7) | collective-permute-done | bytes 147488 | tf_op jit(solution)/shard_map/ppermute | solution.py:95
  28.8 3.8 %collective-permute-done.8.refs_2_ = bf16[32,2304]{1,0:T(8,128)(2,1)S(1)} collective-permute-done((bf16[32,2304]{1,0:T(8,128)(2,1)S(1)}, bf16[32,2304]{1,0:T(8,128)(2,1)S(1)}, u32[]{:S(2)}, u32[]{:S(2)}) %collective-permute-start.8) | collective-permute-done | bytes 147488 | tf_op jit(solution)/shard_map/ppermute | solution.py:95
  32.6 0.6 %copy-done.3 = bf16[32,2304]{1,0:T(8,128)(2,1)} copy-done((bf16[32,2304]{1,0:T(8,128)(2,1)}, bf16[32,2304]{1,0:T(8,128)(2,1)S(1)}, u32[]{:S(2)}) %copy-start.3) | copy-done | bytes 147480
  33.2 0.1 copy-done.4
  33.3 1.9 %combine.1 = bf16[32,2048]{1,0:T(8,128)(2,1)} custom-call(bf16[32,2304]{1,0:T(8,128)(2,1)} %copy-done.1, bf16[32,2304]{1,0:T(8,128)(2,1)} %copy-done.2, bf16[32,2304]{1,0:T(8,128)(2,1)} %copy-done.3, bf16[32,2304]{1,0:T(8,128)(2,1)} %copy-done.4), custom_call_target="tpu_custom_call" | custom-call | tf_op jit(solution)/shard_map/combine/pallas_call | solution.py:120
  (12 shorter events, 0.0 us)
Async XLA Ops:
  0.0 0.9 %copy-start.5 = (bf16[32,1024]{1,0:T(8,128)(2,1)S(1)}, bf16[32,1024]{1,0:T(8,128)(2,1)}, u32[]{:S(2)}) copy-start(bf16[32,1024]{1,0:T(8,128)(2,1)} %param.5) | copy-start | bytes 196612
  0.9 9.5 %collective-permute-start.5 = (bf16[64,1024]{1,0:T(8,128)(2,1)S(1)}, bf16[64,1024]{1,0:T(8,128)(2,1)S(1)}, u32[]{:S(2)}, u32[]{:S(2)}) collective-permute-start(bf16[64,1024]{1,0:T(8,128)(2,1)S(1)} %constant_dynamic-update-slice_fusion.refs_1_), channel_id=1, source_target_pairs={{0,24},{4,28},{8,16},{12,20},{16,8},{20,12},{24,0},{28,4},{1,25},{... | collective-permute-start | bytes 393224 | tf_op jit(solution)/shard_map/ppermute | solution.py:92
  6.0 11.1 %collective-permute-start.3 = (bf16[64,1024]{1,0:T(8,128)(2,1)S(1)}, bf16[64,1024]{1,0:T(8,128)(2,1)S(1)}, u32[]{:S(2)}, u32[]{:S(2)}) collective-permute-start(bf16[64,1024]{1,0:T(8,128)(2,1)S(1)} %constant_dynamic-update-slice_fusion.refs_1_), channel_id=1, source_target_pairs={{0,16},{4,20},{8,24},{12,28},{16,0},{20,4},{24,8},{28,12},{1,17},{... | collective-permute-start | bytes 393224 | tf_op jit(solution)/shard_map/ppermute | solution.py:92
  6.0 11.1 %collective-permute-start.1 = (bf16[64,1024]{1,0:T(8,128)(2,1)S(1)}, bf16[64,1024]{1,0:T(8,128)(2,1)S(1)}, u32[]{:S(2)}, u32[]{:S(2)}) collective-permute-start(bf16[64,1024]{1,0:T(8,128)(2,1)S(1)} %constant_dynamic-update-slice_fusion.refs_1_), channel_id=1, source_target_pairs={{0,8},{4,12},{8,0},{12,4},{16,24},{20,28},{24,16},{28,20},{1,9},{5... | collective-permute-start | bytes 393224 | tf_op jit(solution)/shard_map/ppermute | solution.py:92
  6.6 10.9 %collective-permute-start = (bf16[64,1024]{1,0:T(8,128)(2,1)S(1)}, bf16[64,1024]{1,0:T(8,128)(2,1)S(1)}, u32[]{:S(2)}, u32[]{:S(2)}) collective-permute-start(bf16[64,1024]{1,0:T(8,128)(2,1)S(1)} %constant_dynamic-update-slice_fusion.refs_1_), channel_id=1, source_target_pairs={{0,4},{4,0},{8,12},{12,8},{16,20},{20,16},{24,28},{28,24},{1,5},{5... | collective-permute-start | bytes 393224 | tf_op jit(solution)/shard_map/ppermute | solution.py:92
  10.4 7.2 %collective-permute-start.6 = (bf16[64,1024]{1,0:T(8,128)(2,1)S(1)}, bf16[64,1024]{1,0:T(8,128)(2,1)S(1)}, u32[]{:S(2)}, u32[]{:S(2)}) collective-permute-start(bf16[64,1024]{1,0:T(8,128)(2,1)S(1)} %collective-permute-done.5.refs_7_), channel_id=1, source_target_pairs={{0,4},{4,0},{8,12},{12,8},{16,20},{20,16},{24,28},{28,24},{1,5},{5... | collective-permute-start | bytes 393224 | tf_op jit(solution)/shard_map/ppermute | solution.py:92
  17.1 1.3 %collective-permute-start.4 = (bf16[64,1024]{1,0:T(8,128)(2,1)S(1)}, bf16[64,1024]{1,0:T(8,128)(2,1)S(1)}, u32[]{:S(2)}, u32[]{:S(2)}) collective-permute-start(bf16[64,1024]{1,0:T(8,128)(2,1)S(1)} %collective-permute-done.3.refs_5_), channel_id=1, source_target_pairs={{0,4},{4,0},{8,12},{12,8},{16,20},{20,16},{24,28},{28,24},{1,5},{5... | collective-permute-start | bytes 393224 | tf_op jit(solution)/shard_map/ppermute | solution.py:92
  17.1 1.5 %collective-permute-start.2 = (bf16[64,1024]{1,0:T(8,128)(2,1)S(1)}, bf16[64,1024]{1,0:T(8,128)(2,1)S(1)}, u32[]{:S(2)}, u32[]{:S(2)}) collective-permute-start(bf16[64,1024]{1,0:T(8,128)(2,1)S(1)} %collective-permute-done.1.refs_3_), channel_id=1, source_target_pairs={{0,4},{4,0},{8,12},{12,8},{16,20},{20,16},{24,28},{28,24},{1,5},{5... | collective-permute-start | bytes 393224 | tf_op jit(solution)/shard_map/ppermute | solution.py:92
  18.6 1.0 %copy-start = (bf16[128,2048]{1,0:T(8,128)(2,1)S(1)}, bf16[128,2048]{1,0:T(8,128)(2,1)}, u32[]{:S(2)}) copy-start(bf16[128,2048]{1,0:T(8,128)(2,1)} %refs_0_.1) | copy-start | bytes 1572868
  21.4 0.7 %copy-start.1 = (bf16[32,2304]{1,0:T(8,128)(2,1)}, bf16[32,2304]{1,0:T(8,128)(2,1)S(1)}, u32[]{:S(2)}) copy-start(bf16[32,2304]{1,0:T(8,128)(2,1)S(1)} %get-tuple-element.9.refs_0_) | copy-start | bytes 442372
  22.1 6.7 %collective-permute-start.7 = (bf16[32,2304]{1,0:T(8,128)(2,1)S(1)}, bf16[32,2304]{1,0:T(8,128)(2,1)S(1)}, u32[]{:S(2)}, u32[]{:S(2)}) collective-permute-start(bf16[32,2304]{1,0:T(8,128)(2,1)S(1)} %get-tuple-element.10), channel_id=1, source_target_pairs={{0,1},{1,0},{2,3},{3,2},{4,5},{5,4},{6,7},{7,6},{8,9},{9,8},{10,11... | collective-permute-start | bytes 442376 | tf_op jit(solution)/shard_map/ppermute | solution.py:95
  23.6 9.0 %collective-permute-start.8 = (bf16[32,2304]{1,0:T(8,128)(2,1)S(1)}, bf16[32,2304]{1,0:T(8,128)(2,1)S(1)}, u32[]{:S(2)}, u32[]{:S(2)}) collective-permute-start(bf16[32,2304]{1,0:T(8,128)(2,1)S(1)} %get-tuple-element.11), channel_id=1, source_target_pairs={{0,2},{1,3},{2,0},{3,1},{4,6},{5,7},{6,4},{7,5},{8,10},{9,11},{10,... | collective-permute-start | bytes 442376 | tf_op jit(solution)/shard_map/ppermute | solution.py:95
  25.1 7.4 %collective-permute-start.9 = (bf16[32,2304]{1,0:T(8,128)(2,1)S(1)}, bf16[32,2304]{1,0:T(8,128)(2,1)S(1)}, u32[]{:S(2)}, u32[]{:S(2)}) collective-permute-start(bf16[32,2304]{1,0:T(8,128)(2,1)S(1)} %get-tuple-element.12), channel_id=1, source_target_pairs={{0,3},{1,2},{2,1},{3,0},{4,7},{5,6},{6,5},{7,4},{8,11},{9,10},{10,... | collective-permute-start | bytes 442376 | tf_op jit(solution)/shard_map/ppermute | solution.py:95
  28.8 3.8 %copy-start.2 = (bf16[32,2304]{1,0:T(8,128)(2,1)}, bf16[32,2304]{1,0:T(8,128)(2,1)S(1)}, u32[]{:S(2)}) copy-start(bf16[32,2304]{1,0:T(8,128)(2,1)S(1)} %collective-permute-done.7.refs_1_) | copy-start | bytes 442372
  32.5 0.7 %copy-start.3 = (bf16[32,2304]{1,0:T(8,128)(2,1)}, bf16[32,2304]{1,0:T(8,128)(2,1)S(1)}, u32[]{:S(2)}) copy-start(bf16[32,2304]{1,0:T(8,128)(2,1)S(1)} %collective-permute-done.8.refs_2_) | copy-start | bytes 442372
  32.6 0.7 %copy-start.4 = (bf16[32,2304]{1,0:T(8,128)(2,1)}, bf16[32,2304]{1,0:T(8,128)(2,1)S(1)}, u32[]{:S(2)}) copy-start(bf16[32,2304]{1,0:T(8,128)(2,1)S(1)} %collective-permute-done.9.refs_3_) | copy-start | bytes 442372

commit v2 on v1

v2 whole, which is shorter than its diff:
```python
import functools
import math

import jax
import jax.numpy as jnp
from jax import lax
from jax.experimental import pallas as pl
from jax.experimental.pallas import tpu as pltpu
from jax.sharding import PartitionSpec as P

HEAD = 256
SCALE = 0.0625
CAP = 50.0
LANES = 128
VMEM = pl.BlockSpec(memory_space=pltpu.VMEM)


def stack_blocks(srcs, k_all, v_all, blk):
    for t, src in enumerate(srcs):
        k_all[t * blk : (t + 1) * blk, :] = src[:blk, :]
        v_all[t * blk : (t + 1) * blk, :] = src[blk:, :]


def group_sums(masks, blk, n_col, dests, q_ref, k_all, v_all, emit):
    row, col = lax.axis_index("row"), lax.axis_index("col")
    kv_heads = k_all.shape[1] // HEAD
    group = q_ref.shape[1] // k_all.shape[1]
    n_keys = len(masks) * blk
    lane = lax.broadcasted_iota(jnp.int32, (1, n_keys), 1)
    key_pos = jnp.zeros((1, n_keys), jnp.int32)
    for t, mask in enumerate(masks):
        start = ((row ^ mask) * n_col + col) * blk
        key_pos = jnp.where(lane // blk == t, start + lane % blk, key_pos)
    sub = lax.broadcasted_iota(jnp.int32, (blk, 1), 0)
    parts = [pl.ds(pl.multiple_of((col ^ d) * blk, blk), blk) for d in dests]
    pos = jnp.concatenate([(row * n_col + (col ^ d)) * blk + sub for d in dests], axis=0)
    keep = jnp.where(key_pos <= pos, 1.0, 0.0).astype(jnp.float32)
    for kv in range(kv_heads):
        k_head = k_all[:, kv * HEAD : (kv + 1) * HEAD]
        v_head = v_all[:, kv * HEAD : (kv + 1) * HEAD]
        for h in range(kv * group, (kv + 1) * group):
            q_head = jnp.concatenate([q_ref[p, h * HEAD : (h + 1) * HEAD] for p in parts], axis=0)
            scores = lax.dot_general(
                q_head, k_head, (((1,), (1,)), ((), ())), preferred_element_type=jnp.float32
            )
            capped = jnp.tanh(scores * (SCALE / CAP)) * (CAP / math.log(2.0))
            weights = jnp.exp2(capped) * keep
            denom = jnp.sum(weights, axis=1, keepdims=True)
            numer = jnp.dot(
                weights.astype(jnp.bfloat16), v_head, preferred_element_type=jnp.float32
            )
            emit(h, numer, denom)


def chunks_of(n_col):
    size = min(n_col, 4)
    return [range(base, base + size) for base in range(0, n_col, size)]


def sums_kernel(masks, sums_in, last, blk, n_col, q_ref, *refs):
    before, refs = refs[: 2 * sums_in], refs[2 * sums_in :]
    n_src = len(masks)
    srcs, outs, (k_all, v_all) = refs[:n_src], refs[n_src:-2], refs[-2:]
    feat_q = q_ref.shape[1]
    stack_blocks(srcs, k_all, v_all, blk)
    for dests in chunks_of(n_col):
        rows = slice(dests[0] * blk, (dests[-1] + 1) * blk)
        lanes = lax.broadcasted_iota(jnp.int32, (len(dests) * blk, LANES), 1)
        total = [before[1][rows, :] if sums_in else jnp.zeros(lanes.shape, jnp.float32)]

        def emit(h, numer, denom, dests=dests, rows=rows, lanes=lanes, total=total):
            cut = slice(h * HEAD, (h + 1) * HEAD)
            if sums_in:
                numer = numer + before[0][rows, cut]
            if last:
                numer = numer.astype(jnp.bfloat16)
                for i, d in enumerate(dests):
                    outs[d][:, cut] = numer[i * blk : (i + 1) * blk]
            else:
                outs[0][rows, cut] = numer
            total[0] = total[0] + jnp.where(lanes % (LANES // 2) == h, denom, 0.0)

        group_sums(masks, blk, n_col, dests, q_ref, k_all, v_all, emit)
        if last:
            high = total[0].astype(jnp.bfloat16).astype(jnp.float32)
            tail = jnp.where(lanes < LANES // 2, high, total[0] - high).astype(jnp.bfloat16)
            for i, d in enumerate(dests):
                outs[d][:, feat_q:] = tail[i * blk : (i + 1) * blk]
        else:
            outs[1][rows, :] = total[0]


def combine_kernel(*refs):
    parts, out_ref = refs[:-1], refs[-1]
    feat_q = out_ref.shape[1]
    tail = sum(p[:, feat_q:].astype(jnp.float32) for p in parts)
    inverse = 1.0 / (tail + pltpu.roll(tail, LANES // 2, 1))
    for h in range(feat_q // HEAD):
        cut = slice(h * HEAD, (h + 1) * HEAD)
        numer = sum(p[:, cut].astype(jnp.float32) for p in parts)
        out_ref[:, cut] = (numer * inverse[:, h : h + 1]).astype(jnp.bfloat16)


def per_device(queries, keys, values):
    blk, feat_k = keys.shape
    span, feat_q = queries.shape
    n_row = lax.axis_size("row")
    n_col = lax.axis_size("col")

    def swap_row(x, mask):
        return lax.ppermute(x, "row", [(i, i ^ mask) for i in range(n_row)])

    def swap_col(x, mask):
        return lax.ppermute(x, "col", [(i, i ^ mask) for i in range(n_col)])

    def sums(masks, before, last, name):
        message = jax.ShapeDtypeStruct((blk, feat_q + LANES), jnp.bfloat16)
        totals = [
            jax.ShapeDtypeStruct((span, feat_q), jnp.float32),
            jax.ShapeDtypeStruct((span, LANES), jnp.float32),
        ]
        out_shape = [message] * n_col if last else totals
        args = [queries, *before, *[blocks[m] for m in masks]]
        return pl.pallas_call(
            functools.partial(sums_kernel, masks, len(before) // 2, last, blk, n_col),
            out_shape=out_shape,
            in_specs=[VMEM] * len(args),
            out_specs=[VMEM] * len(out_shape),
            scratch_shapes=[pltpu.VMEM((len(masks) * blk, feat_k), jnp.bfloat16)] * 2,
            compiler_params=pltpu.CompilerParams(vmem_limit_bytes=limit),
            name=name,
        )(*args)

    limit = 16 * 2**20 if span * n_row <= 4096 else 40 * 2**20
    own = jnp.concatenate([keys, values], axis=0)
    blocks = {0: own, 1: swap_row(own, 1)}
    far = list(range(2, n_row, 2))
    for mask in far:
        blocks[mask] = swap_row(own, mask)
    totals = sums([0, 1], [], False, "own_chip")
    *totals, arrived = lax.optimization_barrier((*totals, [blocks[m] for m in far]))
    blocks.update(zip(far, arrived))
    for mask in far:
        blocks[mask ^ 1] = swap_row(blocks[mask], 1)
    totals = sums(far, totals, False, "far_same_core")
    messages = sums([m ^ 1 for m in far], totals, True, "far_other_core")
    received = [messages[0]] + [swap_col(messages[j], j) for j in range(1, n_col)]
    return pl.pallas_call(
        combine_kernel,
        out_shape=jax.ShapeDtypeStruct((blk, feat_q), jnp.bfloat16),
        in_specs=[VMEM] * n_col,
        out_specs=VMEM,
        compiler_params=pltpu.CompilerParams(vmem_limit_bytes=8 * 2**20),
        name="combine",
    )(*received)


def solution(mesh):
    return jax.shard_map(
        per_device,
        mesh=mesh,
        in_specs=(P("row", None), P(("row", "col"), None), P(("row", "col"), None)),
        out_specs=P(("row", "col"), None),
        check_vma=False,
    )
```

time: 35.4 us -> 31.4 us (0.89)
  waiting for transfers between devices: 18.4 us -> 16.5 us
  local copies, waits for them, and re-layouts: 3.27 us -> 1.93 us
  Pallas kernels: 3.67 us -> 2.87 us
    ppermute x7, waiting for transfers between devices: 11.4 us -> 9.99 us  [swap_row(): return lax.ppermute(x, 'row', [(i, i ^ mask) for i in range(n_row)])]
    unnamed x13 -> x5, local copies, waits for them, and re-layouts: 3.27 us -> 1.92 us
    pallas_call x1, Pallas kernels: 1.9 us -> 0.85 us  [per_device(): pl.pallas_call(combine_kernel, out_shape=jax.ShapeDtypeStruct((blk, feat_...]
    ppermute x3, waiting for transfers between devices: 6.96 us -> 6.47 us  [swap_col(): return lax.ppermute(x, 'col', [(i, i ^ mask) for i in range(n_col)])]
    pallas_call x1 -> x3, Pallas kernels: 1.77 us -> 2.02 us  [sums(): pl.pallas_call(functools.partial(sums_kernel, masks, len(before) // 2, la...]
  transfers between devices with their start and end apart: 10 -> 10, of which waited for: 6 -> 7; matrix products, arithmetic and copies ran while one was open for 0% -> 0% of each run, Pallas kernels for 0% -> 4%
where the time goes in v2:
time: 31.4 us; the launch traced here: 31.2 us
  waiting for transfers between devices  16.5 us (53%)
  starting transfers between devices  9.9 us (32%)
  Pallas kernels  2.87 us (9%)
  local copies, waits for them, and re-layouts  1.93 us (6%)
    ppermute x7, waiting for transfers between devices, swap_row(): return lax.ppermute(x, 'row', [(i, i ^ mask) for i in range(n_row)])  9.99 us
    ppermute x3, waiting for transfers between devices, swap_col(): return lax.ppermute(x, 'col', [(i, i ^ mask) for i in range(n_col)])  6.47 us
    ppermute x7, starting transfers between devices, swap_row(): return lax.ppermute(x, 'row', [(i, i ^ mask) for i in range(n_row)])  6.35 us
    ppermute x3, starting transfers between devices, swap_col(): return lax.ppermute(x, 'col', [(i, i ^ mask) for i in range(n_col)])  3.55 us
    pallas_call x3, Pallas kernels, sums(): pl.pallas_call(functools.partial(sums_kernel, masks, len(before) // 2, la...  2.02 us
    unnamed x5, local copies, waits for them, and re-layouts  1.92 us
    pallas_call x1, Pallas kernels, per_device(): pl.pallas_call(combine_kernel, out_shape=jax.ShapeDtypeStruct((blk, feat_...  0.85 us
  transfers between devices with their start and end apart: 10, of which 7 were waited for; matrix products, arithmetic and copies ran while one was open for 0% of the time, Pallas kernels for 4%

profile of v2, /device:TPU:0, one launch (start us, length us, event | category | flops | bytes accessed | tf_op | source)
XLA Modules:
  0.0 31.2 jit_solution(13809562716362085062)
XLA Ops:
  0.0 0.9 %constant_dynamic-update-slice_fusion.1 = bf16[64,1024]{1,0:T(8,128)(2,1)S(1)} fusion(bf16[32,1024]{1,0:T(8,128)(2,1)} %param.4), kind=kLoop, calls=%fused_computation.1 | loop fusion | bytes 131072
  0.9 0.5 %collective-permute-start = (bf16[64,1024]{1,0:T(8,128)(2,1)S(1)}, bf16[64,1024]{1,0:T(8,128)(2,1)S(1)}, u32[]{:S(2)}, u32[]{:S(2)}) collective-permute-start(bf16[64,1024]{1,0:T(8,128)(2,1)S(1)} %constant_dynamic-update-slice_fusion.refs_0_), channel_id=1, source_target_pairs={{0,4},{4,0},{8,12},{12,8},{16,20},{20,16},{24,28},{28,24},{1,5},{5... | collective-permute-start | bytes 393224 | tf_op jit(solution)/shard_map/ppermute | solution.py:111
  1.4 4.7 %collective-permute-start.3 = (bf16[64,1024]{1,0:T(8,128)(2,1)S(1)}, bf16[64,1024]{1,0:T(8,128)(2,1)S(1)}, u32[]{:S(2)}, u32[]{:S(2)}) collective-permute-start(bf16[64,1024]{1,0:T(8,128)(2,1)S(1)} %constant_dynamic-update-slice_fusion.refs_0_), channel_id=1, source_target_pairs={{0,24},{4,28},{8,16},{12,20},{16,8},{20,12},{24,0},{28,4},{1,25},{... | collective-permute-start | bytes 393224 | tf_op jit(solution)/shard_map/ppermute | solution.py:111
  6.1 0.0 collective-permute-start.2
  6.1 0.6 %collective-permute-start.1 = (bf16[64,1024]{1,0:T(8,128)(2,1)S(1)}, bf16[64,1024]{1,0:T(8,128)(2,1)S(1)}, u32[]{:S(2)}, u32[]{:S(2)}) collective-permute-start(bf16[64,1024]{1,0:T(8,128)(2,1)S(1)} %constant_dynamic-update-slice_fusion.refs_0_), channel_id=1, source_target_pairs={{0,8},{4,12},{8,0},{12,4},{16,24},{20,28},{24,16},{28,20},{1,9},{5... | collective-permute-start | bytes 393224 | tf_op jit(solution)/shard_map/ppermute | solution.py:111
  6.7 0.0 collective-permute-done.refs_1_
  6.7 1.0 %copy-done = bf16[128,2048]{1,0:T(8,128)(2,1)S(1)} copy-done((bf16[128,2048]{1,0:T(8,128)(2,1)S(1)}, bf16[128,2048]{1,0:T(8,128)(2,1)}, u32[]{:S(2)}) %copy-start) | copy-done | bytes 524312
  7.8 0.7 %own_chip.1 = (f32[128,2048]{1,0:T(8,128)S(1)}, f32[128,128]{1,0:T(8,128)S(1)}) custom-call(bf16[128,2048]{1,0:T(8,128)(2,1)S(1)} %copy-done, bf16[64,1024]{1,0:T(8,128)(2,1)S(1)} %constant_dynamic-update-slice_fusion.refs_0_, bf16[64,1024]{1,0:T(8,128)(2,1)S(1)} %collective-permute-done.refs_1_), custom_call_target="tpu_custom_call" | custom-call | tf_op jit(solution)/shard_map/own_chip/pallas_call | solution.py:124
  8.4 2.1 %collective-permute-done.3.refs_4_ = bf16[64,1024]{1,0:T(8,128)(2,1)S(1)} collective-permute-done((bf16[64,1024]{1,0:T(8,128)(2,1)S(1)}, bf16[64,1024]{1,0:T(8,128)(2,1)S(1)}, u32[]{:S(2)}, u32[]{:S(2)}) %collective-permute-start.3) | collective-permute-done | bytes 131104 | tf_op jit(solution)/shard_map/ppermute | solution.py:111
  10.5 7.2 %collective-permute-done.2.refs_3_ = bf16[64,1024]{1,0:T(8,128)(2,1)S(1)} collective-permute-done((bf16[64,1024]{1,0:T(8,128)(2,1)S(1)}, bf16[64,1024]{1,0:T(8,128)(2,1)S(1)}, u32[]{:S(2)}, u32[]{:S(2)}) %collective-permute-start.2) | collective-permute-done | bytes 131104 | tf_op jit(solution)/shard_map/ppermute | solution.py:111
  17.8 0.0 collective-permute-start.4
  17.8 0.5 %collective-permute-start.5 = (bf16[64,1024]{1,0:T(8,128)(2,1)S(1)}, bf16[64,1024]{1,0:T(8,128)(2,1)S(1)}, u32[]{:S(2)}, u32[]{:S(2)}) collective-permute-start(bf16[64,1024]{1,0:T(8,128)(2,1)S(1)} %collective-permute-done.2.refs_3_), channel_id=1, source_target_pairs={{0,4},{4,0},{8,12},{12,8},{16,20},{20,16},{24,28},{28,24},{1,5},{5... | collective-permute-start | bytes 393224 | tf_op jit(solution)/shard_map/ppermute | solution.py:111
  18.3 0.0 collective-permute-start.6
  18.3 0.7 %far_same_core.1 = (f32[128,2048]{1,0:T(8,128)S(1)}, f32[128,128]{1,0:T(8,128)S(1)}) custom-call(bf16[128,2048]{1,0:T(8,128)(2,1)S(1)} %copy-done, f32[128,2048]{1,0:T(8,128)S(1)} %get-tuple-element.20.refs_0_, f32[128,128]{1,0:T(8,128)S(1)} %get-tuple-element.21.refs_1_, bf16[64,1024]{1,0:T(8,128)(2,1)S(1)} %collective-permute-done.1.refs_2_, ...), custom_call_target="tpu_custom_call" | custom-call | tf_op jit(solution)/shard_map/far_same_core/pallas_call | solution.py:124
  19.0 0.2 collective-permute-done.4.refs_2_
  19.1 0.2 collective-permute-done.5.refs_3_
  19.3 0.3 %collective-permute-done.6.refs_4_ = bf16[64,1024]{1,0:T(8,128)(2,1)S(1)} collective-permute-done((bf16[64,1024]{1,0:T(8,128)(2,1)S(1)}, bf16[64,1024]{1,0:T(8,128)(2,1)S(1)}, u32[]{:S(2)}, u32[]{:S(2)}) %collective-permute-start.6) | collective-permute-done | bytes 131104 | tf_op jit(solution)/shard_map/ppermute | solution.py:111
  19.6 0.7 %far_other_core.1 = (bf16[32,2176]{1,0:T(8,128)(2,1)S(1)}, bf16[32,2176]{1,0:T(8,128)(2,1)S(1)}, bf16[32,2176]{1,0:T(8,128)(2,1)S(1)}, bf16[32,2176]{1,0:T(8,128)(2,1)S(1)}) custom-call(bf16[128,2048]{1,0:T(8,128)(2,1)S(1)} %copy-done, f32[128,2048]{1,0:T(8,128)S(1)} %get-tuple-element.25.refs_0_, f32[128,128]{1,0:T(8,128)S(1)} %get-tuple-element.26.refs_1_, ...), custom_call_target="tpu_custom_call" | custom-call | tf_op jit(solution)/shard_map/far_other_core/pallas_call | solution.py:124
  20.3 1.6 %collective-permute-start.7 = (bf16[32,2176]{1,0:T(8,128)(2,1)S(1)}, bf16[32,2176]{1,0:T(8,128)(2,1)S(1)}, u32[]{:S(2)}, u32[]{:S(2)}) collective-permute-start(bf16[32,2176]{1,0:T(8,128)(2,1)S(1)} %get-tuple-element.28), channel_id=1, source_target_pairs={{0,1},{1,0},{2,3},{3,2},{4,5},{5,4},{6,7},{7,6},{8,9},{9,8},{10,11... | collective-permute-start | bytes 417800 | tf_op jit(solution)/shard_map/ppermute | solution.py:114
  21.9 1.5 %collective-permute-start.8 = (bf16[32,2176]{1,0:T(8,128)(2,1)S(1)}, bf16[32,2176]{1,0:T(8,128)(2,1)S(1)}, u32[]{:S(2)}, u32[]{:S(2)}) collective-permute-start(bf16[32,2176]{1,0:T(8,128)(2,1)S(1)} %get-tuple-element.29), channel_id=1, source_target_pairs={{0,2},{1,3},{2,0},{3,1},{4,6},{5,7},{6,4},{7,5},{8,10},{9,11},{10,... | collective-permute-start | bytes 417800 | tf_op jit(solution)/shard_map/ppermute | solution.py:114
  23.4 0.5 %collective-permute-start.9 = (bf16[32,2176]{1,0:T(8,128)(2,1)S(1)}, bf16[32,2176]{1,0:T(8,128)(2,1)S(1)}, u32[]{:S(2)}, u32[]{:S(2)}) collective-permute-start(bf16[32,2176]{1,0:T(8,128)(2,1)S(1)} %get-tuple-element.30), channel_id=1, source_target_pairs={{0,3},{1,2},{2,1},{3,0},{4,7},{5,6},{6,5},{7,4},{8,11},{9,10},{10,... | collective-permute-start | bytes 417800 | tf_op jit(solution)/shard_map/ppermute | solution.py:114
  23.9 2.8 %collective-permute-done.7.refs_1_ = bf16[32,2176]{1,0:T(8,128)(2,1)S(1)} collective-permute-done((bf16[32,2176]{1,0:T(8,128)(2,1)S(1)}, bf16[32,2176]{1,0:T(8,128)(2,1)S(1)}, u32[]{:S(2)}, u32[]{:S(2)}) %collective-permute-start.7) | collective-permute-done | bytes 139296 | tf_op jit(solution)/shard_map/ppermute | solution.py:114
  26.7 3.7 %collective-permute-done.8.refs_2_ = bf16[32,2176]{1,0:T(8,128)(2,1)S(1)} collective-permute-done((bf16[32,2176]{1,0:T(8,128)(2,1)S(1)}, bf16[32,2176]{1,0:T(8,128)(2,1)S(1)}, u32[]{:S(2)}, u32[]{:S(2)}) %collective-permute-start.8) | collective-permute-done | bytes 139296 | tf_op jit(solution)/shard_map/ppermute | solution.py:114
  30.3 0.9 %combine.1 = bf16[32,2048]{1,0:T(8,128)(2,1)} custom-call(bf16[32,2176]{1,0:T(8,128)(2,1)S(1)} %get-tuple-element.27.refs_0_, bf16[32,2176]{1,0:T(8,128)(2,1)S(1)} %collective-permute-done.7.refs_1_, bf16[32,2176]{1,0:T(8,128)(2,1)S(1)} %collective-permute-done.8.refs_2_, bf16[32,2176]{1,0:T(8,128)(2,1)S(1)} %collective-permute-done.9.refs_3_), custom_call_target="tpu_custom_call" | custom-call | tf_op jit(solution)/shard_map/combine/pallas_call | solution.py:148
  (6 shorter events, 0.0 us)
Async XLA Ops:
  0.0 0.9 %copy-start.1 = (bf16[32,1024]{1,0:T(8,128)(2,1)S(1)}, bf16[32,1024]{1,0:T(8,128)(2,1)}, u32[]{:S(2)}) copy-start(bf16[32,1024]{1,0:T(8,128)(2,1)} %param.5) | copy-start | bytes 196612
  0.9 5.8 %collective-permute-start = (bf16[64,1024]{1,0:T(8,128)(2,1)S(1)}, bf16[64,1024]{1,0:T(8,128)(2,1)S(1)}, u32[]{:S(2)}, u32[]{:S(2)}) collective-permute-start(bf16[64,1024]{1,0:T(8,128)(2,1)S(1)} %constant_dynamic-update-slice_fusion.refs_0_), channel_id=1, source_target_pairs={{0,4},{4,0},{8,12},{12,8},{16,20},{20,16},{24,28},{28,24},{1,5},{5... | collective-permute-start | bytes 393224 | tf_op jit(solution)/shard_map/ppermute | solution.py:111
  1.4 9.1 %collective-permute-start.3 = (bf16[64,1024]{1,0:T(8,128)(2,1)S(1)}, bf16[64,1024]{1,0:T(8,128)(2,1)S(1)}, u32[]{:S(2)}, u32[]{:S(2)}) collective-permute-start(bf16[64,1024]{1,0:T(8,128)(2,1)S(1)} %constant_dynamic-update-slice_fusion.refs_0_), channel_id=1, source_target_pairs={{0,24},{4,28},{8,16},{12,20},{16,8},{20,12},{24,0},{28,4},{1,25},{... | collective-permute-start | bytes 393224 | tf_op jit(solution)/shard_map/ppermute | solution.py:111
  6.1 11.7 %collective-permute-start.2 = (bf16[64,1024]{1,0:T(8,128)(2,1)S(1)}, bf16[64,1024]{1,0:T(8,128)(2,1)S(1)}, u32[]{:S(2)}, u32[]{:S(2)}) collective-permute-start(bf16[64,1024]{1,0:T(8,128)(2,1)S(1)} %constant_dynamic-update-slice_fusion.refs_0_), channel_id=1, source_target_pairs={{0,16},{4,20},{8,24},{12,28},{16,0},{20,4},{24,8},{28,12},{1,17},{... | collective-permute-start | bytes 393224 | tf_op jit(solution)/shard_map/ppermute | solution.py:111
  6.1 11.7 %collective-permute-start.1 = (bf16[64,1024]{1,0:T(8,128)(2,1)S(1)}, bf16[64,1024]{1,0:T(8,128)(2,1)S(1)}, u32[]{:S(2)}, u32[]{:S(2)}) collective-permute-start(bf16[64,1024]{1,0:T(8,128)(2,1)S(1)} %constant_dynamic-update-slice_fusion.refs_0_), channel_id=1, source_target_pairs={{0,8},{4,12},{8,0},{12,4},{16,24},{20,28},{24,16},{28,20},{1,9},{5... | collective-permute-start | bytes 393224 | tf_op jit(solution)/shard_map/ppermute | solution.py:111
  6.7 1.0 %copy-start = (bf16[128,2048]{1,0:T(8,128)(2,1)S(1)}, bf16[128,2048]{1,0:T(8,128)(2,1)}, u32[]{:S(2)}) copy-start(bf16[128,2048]{1,0:T(8,128)(2,1)} %q_ref.5) | copy-start | bytes 1572868
  17.8 1.3 %collective-permute-start.4 = (bf16[64,1024]{1,0:T(8,128)(2,1)S(1)}, bf16[64,1024]{1,0:T(8,128)(2,1)S(1)}, u32[]{:S(2)}, u32[]{:S(2)}) collective-permute-start(bf16[64,1024]{1,0:T(8,128)(2,1)S(1)} %collective-permute-done.1.refs_2_), channel_id=1, source_target_pairs={{0,4},{4,0},{8,12},{12,8},{16,20},{20,16},{24,28},{28,24},{1,5},{5... | collective-permute-start | bytes 393224 | tf_op jit(solution)/shard_map/ppermute | solution.py:111
  17.8 1.5 %collective-permute-start.5 = (bf16[64,1024]{1,0:T(8,128)(2,1)S(1)}, bf16[64,1024]{1,0:T(8,128)(2,1)S(1)}, u32[]{:S(2)}, u32[]{:S(2)}) collective-permute-start(bf16[64,1024]{1,0:T(8,128)(2,1)S(1)} %collective-permute-done.2.refs_3_), channel_id=1, source_target_pairs={{0,4},{4,0},{8,12},{12,8},{16,20},{20,16},{24,28},{28,24},{1,5},{5... | collective-permute-start | bytes 393224 | tf_op jit(solution)/shard_map/ppermute | solution.py:111
  18.3 1.3 %collective-permute-start.6 = (bf16[64,1024]{1,0:T(8,128)(2,1)S(1)}, bf16[64,1024]{1,0:T(8,128)(2,1)S(1)}, u32[]{:S(2)}, u32[]{:S(2)}) collective-permute-start(bf16[64,1024]{1,0:T(8,128)(2,1)S(1)} %collective-permute-done.3.refs_4_), channel_id=1, source_target_pairs={{0,4},{4,0},{8,12},{12,8},{16,20},{20,16},{24,28},{28,24},{1,5},{5... | collective-permute-start | bytes 393224 | tf_op jit(solution)/shard_map/ppermute | solution.py:111
  20.3 6.4 %collective-permute-start.7 = (bf16[32,2176]{1,0:T(8,128)(2,1)S(1)}, bf16[32,2176]{1,0:T(8,128)(2,1)S(1)}, u32[]{:S(2)}, u32[]{:S(2)}) collective-permute-start(bf16[32,2176]{1,0:T(8,128)(2,1)S(1)} %get-tuple-element.28), channel_id=1, source_target_pairs={{0,1},{1,0},{2,3},{3,2},{4,5},{5,4},{6,7},{7,6},{8,9},{9,8},{10,11... | collective-permute-start | bytes 417800 | tf_op jit(solution)/shard_map/ppermute | solution.py:114
  21.9 8.5 %collective-permute-start.8 = (bf16[32,2176]{1,0:T(8,128)(2,1)S(1)}, bf16[32,2176]{1,0:T(8,128)(2,1)S(1)}, u32[]{:S(2)}, u32[]{:S(2)}) collective-permute-start(bf16[32,2176]{1,0:T(8,128)(2,1)S(1)} %get-tuple-element.29), channel_id=1, source_target_pairs={{0,2},{1,3},{2,0},{3,1},{4,6},{5,7},{6,4},{7,5},{8,10},{9,11},{10,... | collective-permute-start | bytes 417800 | tf_op jit(solution)/shard_map/ppermute | solution.py:114
  23.4 7.0 %collective-permute-start.9 = (bf16[32,2176]{1,0:T(8,128)(2,1)S(1)}, bf16[32,2176]{1,0:T(8,128)(2,1)S(1)}, u32[]{:S(2)}, u32[]{:S(2)}) collective-permute-start(bf16[32,2176]{1,0:T(8,128)(2,1)S(1)} %get-tuple-element.30), channel_id=1, source_target_pairs={{0,3},{1,2},{2,1},{3,0},{4,7},{5,6},{6,5},{7,4},{8,11},{9,10},{10,... | collective-permute-start | bytes 417800 | tf_op jit(solution)/shard_map/ppermute | solution.py:114

commit v3 on v2

--- a/solution.py
+++ b/solution.py
@@ -15,14 +15,24 @@
 VMEM = pl.BlockSpec(memory_space=pltpu.VMEM)
 
 
+def turned(mask, n_col):
+    half = (n_col.bit_length() - 1) // 2
+    return mask >> half | (mask & (1 << half) - 1) << half if 1 << 2 * half == n_col else mask
+
+
 def stack_blocks(srcs, k_all, v_all, blk):
+    first = lax.axis_index("row") % 2 == 0
     for t, src in enumerate(srcs):
-        k_all[t * blk : (t + 1) * blk, :] = src[:blk, :]
-        v_all[t * blk : (t + 1) * blk, :] = src[blk:, :]
+        for part, into in (slice(0, blk), k_all), (slice(blk, 2 * blk), v_all):
+            value = src[0][part, :]
+            if len(src) == 2:
+                value = jnp.where(first, value, src[1][part, :])
+            into[t * blk : (t + 1) * blk, :] = value
 
 
 def group_sums(masks, blk, n_col, dests, q_ref, k_all, v_all, emit):
     row, col = lax.axis_index("row"), lax.axis_index("col")
+    columns = [col ^ jnp.where(row % 2 == 0, d, turned(d, n_col)) for d in dests]
     kv_heads = k_all.shape[1] // HEAD
     group = q_ref.shape[1] // k_all.shape[1]
     n_keys = len(masks) * blk
@@ -32,8 +42,8 @@
         start = ((row ^ mask) * n_col + col) * blk
         key_pos = jnp.where(lane // blk == t, start + lane % blk, key_pos)
     sub = lax.broadcasted_iota(jnp.int32, (blk, 1), 0)
-    parts = [pl.ds(pl.multiple_of((col ^ d) * blk, blk), blk) for d in dests]
-    pos = jnp.concatenate([(row * n_col + (col ^ d)) * blk + sub for d in dests], axis=0)
+    parts = [pl.ds(pl.multiple_of(c * blk, blk), blk) for c in columns]
+    pos = jnp.concatenate([(row * n_col + c) * blk + sub for c in columns], axis=0)
     keep = jnp.where(key_pos <= pos, 1.0, 0.0).astype(jnp.float32)
     for kv in range(kv_heads):
         k_head = k_all[:, kv * HEAD : (kv + 1) * HEAD]
@@ -57,10 +67,13 @@
     return [range(base, base + size) for base in range(0, n_col, size)]
 
 
-def sums_kernel(masks, sums_in, last, blk, n_col, q_ref, *refs):
+def sums_kernel(masks, widths, sums_in, last, blk, n_col, q_ref, *refs):
     before, refs = refs[: 2 * sums_in], refs[2 * sums_in :]
-    n_src = len(masks)
-    srcs, outs, (k_all, v_all) = refs[:n_src], refs[n_src:-2], refs[-2:]
+    srcs = []
+    for width in widths:
+        srcs.append(refs[:width])
+        refs = refs[width:]
+    outs, (k_all, v_all) = refs[:-2], refs[-2:]
     feat_q = q_ref.shape[1]
     stack_blocks(srcs, k_all, v_all, blk)
     for dests in chunks_of(n_col):
@@ -110,8 +123,20 @@
     def swap_row(x, mask):
         return lax.ppermute(x, "row", [(i, i ^ mask) for i in range(n_row)])
 
+    def send_up(x, block, hops):
+        pairs = []
+        for r in range(n_row):
+            hop = hops[r % 2]
+            if hop is not None and (r ^ hop ^ block) < r ^ hop:
+                pairs += [(r * n_col + c, (r ^ hop) * n_col + c) for c in range(n_col)]
+        return lax.ppermute(x, ("row", "col"), pairs)
+
     def swap_col(x, mask):
-        return lax.ppermute(x, "col", [(i, i ^ mask) for i in range(n_col)])
+        masks = [mask, turned(mask, n_col)]
+        pairs = [
+            (r * n_col + c, r * n_col + (c ^ masks[r % 2])) for r in range(n_row) for c in range(n_col)
+        ]
+        return lax.ppermute(x, ("row", "col"), pairs)
 
     def sums(masks, before, last, name):
         message = jax.ShapeDtypeStruct((blk, feat_q + LANES), jnp.bfloat16)
@@ -120,9 +145,10 @@
             jax.ShapeDtypeStruct((span, LANES), jnp.float32),
         ]
         out_shape = [message] * n_col if last else totals
-        args = [queries, *before, *[blocks[m] for m in masks]]
+        widths = [len(blocks[m]) for m in masks]
+        args = [queries, *before, *[x for m in masks for x in blocks[m]]]
         return pl.pallas_call(
-            functools.partial(sums_kernel, masks, len(before) // 2, last, blk, n_col),
+            functools.partial(sums_kernel, masks, widths, len(before) // 2, last, blk, n_col),
             out_shape=out_shape,
             in_specs=[VMEM] * len(args),
             out_specs=[VMEM] * len(out_shape),
@@ -133,15 +159,20 @@
 
     limit = 16 * 2**20 if span * n_row <= 4096 else 40 * 2**20
     own = jnp.concatenate([keys, values], axis=0)
-    blocks = {0: own, 1: swap_row(own, 1)}
-    far = list(range(2, n_row, 2))
+    blocks = {0: [own], 1: [swap_row(own, 1)]}
+    far = sorted(range(2, n_row, 2), key=lambda m: (m & n_row // 2 == 0, m & 2 == 0))
     for mask in far:
-        blocks[mask] = swap_row(own, mask)
+        if mask & n_row // 2 and not mask & 2:
+            direct = send_up(own, mask, (mask, None))
+            relayed = send_up(blocks[mask ^ 2][0], mask, (None, 2))
+            blocks[mask] = [direct, relayed]
+        else:
+            blocks[mask] = [swap_row(own, mask)]
     totals = sums([0, 1], [], False, "own_chip")
     *totals, arrived = lax.optimization_barrier((*totals, [blocks[m] for m in far]))
     blocks.update(zip(far, arrived))
     for mask in far:
-        blocks[mask ^ 1] = swap_row(blocks[mask], 1)
+        blocks[mask ^ 1] = [swap_row(x, 1) for x in blocks[mask]][::-1]
     totals = sums(far, totals, False, "far_same_core")
     messages = sums([m ^ 1 for m in far], totals, True, "far_other_core")
     received = [messages[0]] + [swap_col(messages[j], j) for j in range(1, n_col)]

time: 31.4 us -> 27 us (0.86)
  waiting for transfers between devices: 16.5 us -> 8.89 us
  starting transfers between devices: 9.9 us -> 13 us
    ppermute x7, waiting for transfers between devices: 9.99 us -> 2.07 us  [swap_row(): return lax.ppermute(x, 'row', [(i, i ^ mask) for i in range(n_row)])]
    ppermute x3 -> x5, starting transfers between devices: 3.55 us -> 6.83 us  [the longest x3 3.55 us: swap_col(): return lax.ppermute(x, ('row', 'col'), pairs)]
    ppermute x3 -> x5, waiting for transfers between devices: 6.47 us -> 6.82 us  [the longest x3 6.58 us: swap_col(): return lax.ppermute(x, ('row', 'col'), pairs)]
  transfers between devices with their start and end apart: 10 -> 12, of which waited for: 7 -> 7; matrix products, arithmetic and copies ran while one was open for 0% -> 0% of each run, Pallas kernels for 4% -> 5%
where the time goes in v3:
time: 27 us; the launch traced here: 26.7 us
  starting transfers between devices  13 us (48%)
  waiting for transfers between devices  8.89 us (33%)
  Pallas kernels  2.88 us (11%)
  local copies, waits for them, and re-layouts  1.92 us (7%)
    ppermute x3, waiting for transfers between devices, swap_col(): return lax.ppermute(x, ('row', 'col'), pairs)  6.58 us
    ppermute x7, starting transfers between devices, swap_row(): return lax.ppermute(x, 'row', [(i, i ^ mask) for i in range(n_row)])  6.14 us
    ppermute x3, starting transfers between devices, swap_col(): return lax.ppermute(x, ('row', 'col'), pairs)  3.55 us
    ppermute x2, starting transfers between devices, send_up(): return lax.ppermute(x, ('row', 'col'), pairs)  3.27 us
    ppermute x7, waiting for transfers between devices, swap_row(): return lax.ppermute(x, 'row', [(i, i ^ mask) for i in range(n_row)])  2.07 us
    pallas_call x3, Pallas kernels, sums(): pl.pallas_call(functools.partial(sums_kernel, masks, widths, len(before)...  2.03 us
    unnamed x5, local copies, waits for them, and re-layouts  1.92 us
    pallas_call x1, Pallas kernels, per_device(): pl.pallas_call(combine_kernel, out_shape=jax.ShapeDtypeStruct((blk, feat_...  0.85 us
  transfers between devices with their start and end apart: 12, of which 7 were waited for; matrix products, arithmetic and copies ran while one was open for 0% of the time, Pallas kernels for 5%

profile of v3, /device:TPU:0, one launch (start us, length us, event | category | flops | bytes accessed | tf_op | source)
XLA Modules:
  0.0 26.7 jit_solution(1486981240044665219)
XLA Ops:
  0.0 0.9 %constant_dynamic-update-slice_fusion.1 = bf16[64,1024]{1,0:T(8,128)(2,1)S(1)} fusion(bf16[32,1024]{1,0:T(8,128)(2,1)} %param.4), kind=kLoop, calls=%fused_computation.1 | loop fusion | bytes 131072
  0.9 5.1 %collective-permute-start.1 = (bf16[64,1024]{1,0:T(8,128)(2,1)S(1)}, bf16[64,1024]{1,0:T(8,128)(2,1)S(1)}, u32[]{:S(2)}, u32[]{:S(2)}) collective-permute-start(bf16[64,1024]{1,0:T(8,128)(2,1)S(1)} %constant_dynamic-update-slice_fusion.refs_0_), channel_id=1, source_target_pairs={{0,24},{4,28},{8,16},{12,20},{16,8},{20,12},{24,0},{28,4},{1,25},{... | collective-permute-start | bytes 393224 | tf_op jit(solution)/shard_map/ppermute | solution.py:124
  6.0 2.6 %collective-permute-start.2 = (bf16[64,1024]{1,0:T(8,128)(2,1)S(1)}, bf16[64,1024]{1,0:T(8,128)(2,1)S(1)}, u32[]{:S(2)}, u32[]{:S(2)}) collective-permute-start(bf16[64,1024]{1,0:T(8,128)(2,1)S(1)} %constant_dynamic-update-slice_fusion.refs_0_), channel_id=1, source_target_pairs={{0,16},{1,17},{2,18},{3,19},{8,24},{9,25},{10,26},{11,27}} | collective-permute-start | bytes 393224 | tf_op jit(solution)/shard_map/ppermute | solution.py:132
  8.6 1.7 %collective-permute-done.1.refs_2_ = bf16[64,1024]{1,0:T(8,128)(2,1)S(1)} collective-permute-done((bf16[64,1024]{1,0:T(8,128)(2,1)S(1)}, bf16[64,1024]{1,0:T(8,128)(2,1)S(1)}, u32[]{:S(2)}, u32[]{:S(2)}) %collective-permute-start.1) | collective-permute-done | bytes 131104 | tf_op jit(solution)/shard_map/ppermute | solution.py:124
  10.4 0.7 %collective-permute-start.3 = (bf16[64,1024]{1,0:T(8,128)(2,1)S(1)}, bf16[64,1024]{1,0:T(8,128)(2,1)S(1)}, u32[]{:S(2)}, u32[]{:S(2)}) collective-permute-start(bf16[64,1024]{1,0:T(8,128)(2,1)S(1)} %collective-permute-done.1.refs_2_), channel_id=1, source_target_pairs={{20,28},{21,29},{22,30},{23,31},{28,20},{29,21},{30,22},{31,23}} | collective-permute-start | bytes 393224 | tf_op jit(solution)/shard_map/ppermute | solution.py:132
  11.0 0.0 collective-permute-done.refs_1_
  11.1 0.0 copy-start
  11.1 1.0 %copy-done = bf16[128,2048]{1,0:T(8,128)(2,1)S(1)} copy-done((bf16[128,2048]{1,0:T(8,128)(2,1)S(1)}, bf16[128,2048]{1,0:T(8,128)(2,1)}, u32[]{:S(2)}) %copy-start) | copy-done | bytes 524312
  12.1 0.7 %own_chip.1 = (f32[128,2048]{1,0:T(8,128)S(1)}, f32[128,128]{1,0:T(8,128)S(1)}) custom-call(bf16[128,2048]{1,0:T(8,128)(2,1)S(1)} %copy-done, bf16[64,1024]{1,0:T(8,128)(2,1)S(1)} %constant_dynamic-update-slice_fusion.refs_0_, bf16[64,1024]{1,0:T(8,128)(2,1)S(1)} %collective-permute-done.refs_1_), custom_call_target="tpu_custom_call" | custom-call | tf_op jit(solution)/shard_map/own_chip/pallas_call | solution.py:150
  12.8 0.2 collective-permute-done.2.refs_3_
  13.0 0.5 %collective-permute-start.7 = (bf16[64,1024]{1,0:T(8,128)(2,1)S(1)}, bf16[64,1024]{1,0:T(8,128)(2,1)S(1)}, u32[]{:S(2)}, u32[]{:S(2)}) collective-permute-start(bf16[64,1024]{1,0:T(8,128)(2,1)S(1)} %collective-permute-done.2.refs_3_), channel_id=1, source_target_pairs={{0,4},{4,0},{8,12},{12,8},{16,20},{20,16},{24,28},{28,24},{1,5},{5... | collective-permute-start | bytes 393224 | tf_op jit(solution)/shard_map/ppermute | solution.py:124
  13.5 0.0 collective-permute-start.6
  13.5 0.5 %collective-permute-start.8 = (bf16[64,1024]{1,0:T(8,128)(2,1)S(1)}, bf16[64,1024]{1,0:T(8,128)(2,1)S(1)}, u32[]{:S(2)}, u32[]{:S(2)}) collective-permute-start(bf16[64,1024]{1,0:T(8,128)(2,1)S(1)} %collective-permute-done.4.refs_5_), channel_id=1, source_target_pairs={{0,4},{4,0},{8,12},{12,8},{16,20},{20,16},{24,28},{28,24},{1,5},{5... | collective-permute-start | bytes 393224 | tf_op jit(solution)/shard_map/ppermute | solution.py:124
  14.0 0.7 %far_same_core.1 = (f32[128,2048]{1,0:T(8,128)S(1)}, f32[128,128]{1,0:T(8,128)S(1)}) custom-call(bf16[128,2048]{1,0:T(8,128)(2,1)S(1)} %copy-done, f32[128,2048]{1,0:T(8,128)S(1)} %get-tuple-element.21.refs_0_, f32[128,128]{1,0:T(8,128)S(1)} %get-tuple-element.22.refs_1_, bf16[64,1024]{1,0:T(8,128)(2,1)S(1)} %collective-permute-done.1.refs_2_, ...), custom_call_target="tpu_custom_call" | custom-call | tf_op jit(solution)/shard_map/far_same_core/pallas_call | solution.py:150
  14.8 0.1 collective-permute-done.6.refs_3_
  14.9 0.2 collective-permute-done.8.refs_5_
  15.1 0.7 %far_other_core.1 = (bf16[32,2176]{1,0:T(8,128)(2,1)S(1)}, bf16[32,2176]{1,0:T(8,128)(2,1)S(1)}, bf16[32,2176]{1,0:T(8,128)(2,1)S(1)}, bf16[32,2176]{1,0:T(8,128)(2,1)S(1)}) custom-call(bf16[128,2048]{1,0:T(8,128)(2,1)S(1)} %copy-done, f32[128,2048]{1,0:T(8,128)S(1)} %get-tuple-element.27.refs_0_, f32[128,128]{1,0:T(8,128)S(1)} %get-tuple-element.28.refs_1_, ...), custom_call_target="tpu_custom_call" | custom-call | tf_op jit(solution)/shard_map/far_other_core/pallas_call | solution.py:150
  15.8 1.6 %collective-permute-start.9 = (bf16[32,2176]{1,0:T(8,128)(2,1)S(1)}, bf16[32,2176]{1,0:T(8,128)(2,1)S(1)}, u32[]{:S(2)}, u32[]{:S(2)}) collective-permute-start(bf16[32,2176]{1,0:T(8,128)(2,1)S(1)} %get-tuple-element.30), channel_id=1, source_target_pairs={{0,1},{1,0},{2,3},{3,2},{4,6},{5,7},{6,4},{7,5},{8,9},{9,8},{10,11... | collective-permute-start | bytes 417800 | tf_op jit(solution)/shard_map/ppermute | solution.py:139
  17.4 1.5 %collective-permute-start.10 = (bf16[32,2176]{1,0:T(8,128)(2,1)S(1)}, bf16[32,2176]{1,0:T(8,128)(2,1)S(1)}, u32[]{:S(2)}, u32[]{:S(2)}) collective-permute-start(bf16[32,2176]{1,0:T(8,128)(2,1)S(1)} %get-tuple-element.31), channel_id=1, source_target_pairs={{0,2},{1,3},{2,0},{3,1},{4,5},{5,4},{6,7},{7,6},{8,10},{9,11},{10,... | collective-permute-start | bytes 417800 | tf_op jit(solution)/shard_map/ppermute | solution.py:139
  18.9 0.4 %collective-permute-start.11 = (bf16[32,2176]{1,0:T(8,128)(2,1)S(1)}, bf16[32,2176]{1,0:T(8,128)(2,1)S(1)}, u32[]{:S(2)}, u32[]{:S(2)}) collective-permute-start(bf16[32,2176]{1,0:T(8,128)(2,1)S(1)} %get-tuple-element.32), channel_id=1, source_target_pairs={{0,3},{1,2},{2,1},{3,0},{4,7},{5,6},{6,5},{7,4},{8,11},{9,10},{10,... | collective-permute-start | bytes 417800 | tf_op jit(solution)/shard_map/ppermute | solution.py:139
  19.3 2.5 %collective-permute-done.9.refs_1_ = bf16[32,2176]{1,0:T(8,128)(2,1)S(1)} collective-permute-done((bf16[32,2176]{1,0:T(8,128)(2,1)S(1)}, bf16[32,2176]{1,0:T(8,128)(2,1)S(1)}, u32[]{:S(2)}, u32[]{:S(2)}) %collective-permute-start.9) | collective-permute-done | bytes 139296 | tf_op jit(solution)/shard_map/ppermute | solution.py:139
  21.8 0.6 %collective-permute-done.10.refs_2_ = bf16[32,2176]{1,0:T(8,128)(2,1)S(1)} collective-permute-done((bf16[32,2176]{1,0:T(8,128)(2,1)S(1)}, bf16[32,2176]{1,0:T(8,128)(2,1)S(1)}, u32[]{:S(2)}, u32[]{:S(2)}) %collective-permute-start.10) | collective-permute-done | bytes 139296 | tf_op jit(solution)/shard_map/ppermute | solution.py:139
  22.4 3.5 %collective-permute-done.11.refs_3_ = bf16[32,2176]{1,0:T(8,128)(2,1)S(1)} collective-permute-done((bf16[32,2176]{1,0:T(8,128)(2,1)S(1)}, bf16[32,2176]{1,0:T(8,128)(2,1)S(1)}, u32[]{:S(2)}, u32[]{:S(2)}) %collective-permute-start.11) | collective-permute-done | bytes 139296 | tf_op jit(solution)/shard_map/ppermute | solution.py:139
  25.9 0.9 %combine.1 = bf16[32,2048]{1,0:T(8,128)(2,1)} custom-call(bf16[32,2176]{1,0:T(8,128)(2,1)S(1)} %get-tuple-element.29.refs_0_, bf16[32,2176]{1,0:T(8,128)(2,1)S(1)} %collective-permute-done.9.refs_1_, bf16[32,2176]{1,0:T(8,128)(2,1)S(1)} %collective-permute-done.10.refs_2_, bf16[32,2176]{1,0:T(8,128)(2,1)S(1)} %collective-permute-done.11.refs_3_), custom_call_target="tpu_custom_call" | custom-call | tf_op jit(solution)/shard_map/combine/pallas_call | solution.py:179
  (10 shorter events, 0.0 us)
Async XLA Ops:
  0.0 0.9 %copy-start.1 = (bf16[32,1024]{1,0:T(8,128)(2,1)S(1)}, bf16[32,1024]{1,0:T(8,128)(2,1)}, u32[]{:S(2)}) copy-start(bf16[32,1024]{1,0:T(8,128)(2,1)} %param.5) | copy-start | bytes 196612
  0.9 9.5 %collective-permute-start.1 = (bf16[64,1024]{1,0:T(8,128)(2,1)S(1)}, bf16[64,1024]{1,0:T(8,128)(2,1)S(1)}, u32[]{:S(2)}, u32[]{:S(2)}) collective-permute-start(bf16[64,1024]{1,0:T(8,128)(2,1)S(1)} %constant_dynamic-update-slice_fusion.refs_0_), channel_id=1, source_target_pairs={{0,24},{4,28},{8,16},{12,20},{16,8},{20,12},{24,0},{28,4},{1,25},{... | collective-permute-start | bytes 393224 | tf_op jit(solution)/shard_map/ppermute | solution.py:124
  6.0 5.0 %collective-permute-start = (bf16[64,1024]{1,0:T(8,128)(2,1)S(1)}, bf16[64,1024]{1,0:T(8,128)(2,1)S(1)}, u32[]{:S(2)}, u32[]{:S(2)}) collective-permute-start(bf16[64,1024]{1,0:T(8,128)(2,1)S(1)} %constant_dynamic-update-slice_fusion.refs_0_), channel_id=1, source_target_pairs={{0,4},{4,0},{8,12},{12,8},{16,20},{20,16},{24,28},{28,24},{1,5},{5... | collective-permute-start | bytes 393224 | tf_op jit(solution)/shard_map/ppermute | solution.py:124
  6.0 6.8 %collective-permute-start.4 = (bf16[64,1024]{1,0:T(8,128)(2,1)S(1)}, bf16[64,1024]{1,0:T(8,128)(2,1)S(1)}, u32[]{:S(2)}, u32[]{:S(2)}) collective-permute-start(bf16[64,1024]{1,0:T(8,128)(2,1)S(1)} %constant_dynamic-update-slice_fusion.refs_0_), channel_id=1, source_target_pairs={{0,8},{4,12},{8,0},{12,4},{16,24},{20,28},{24,16},{28,20},{1,9},{5... | collective-permute-start | bytes 393224 | tf_op jit(solution)/shard_map/ppermute | solution.py:124
  6.0 7.0 %collective-permute-start.2 = (bf16[64,1024]{1,0:T(8,128)(2,1)S(1)}, bf16[64,1024]{1,0:T(8,128)(2,1)S(1)}, u32[]{:S(2)}, u32[]{:S(2)}) collective-permute-start(bf16[64,1024]{1,0:T(8,128)(2,1)S(1)} %constant_dynamic-update-slice_fusion.refs_0_), channel_id=1, source_target_pairs={{0,16},{1,17},{2,18},{3,19},{8,24},{9,25},{10,26},{11,27}} | collective-permute-start | bytes 393224 | tf_op jit(solution)/shard_map/ppermute | solution.py:132
  10.4 2.6 %collective-permute-start.3 = (bf16[64,1024]{1,0:T(8,128)(2,1)S(1)}, bf16[64,1024]{1,0:T(8,128)(2,1)S(1)}, u32[]{:S(2)}, u32[]{:S(2)}) collective-permute-start(bf16[64,1024]{1,0:T(8,128)(2,1)S(1)} %collective-permute-done.1.refs_2_), channel_id=1, source_target_pairs={{20,28},{21,29},{22,30},{23,31},{28,20},{29,21},{30,22},{31,23}} | collective-permute-start | bytes 393224 | tf_op jit(solution)/shard_map/ppermute | solution.py:132
  11.1 1.0 %copy-start = (bf16[128,2048]{1,0:T(8,128)(2,1)S(1)}, bf16[128,2048]{1,0:T(8,128)(2,1)}, u32[]{:S(2)}) copy-start(bf16[128,2048]{1,0:T(8,128)(2,1)} %q_ref.5) | copy-start | bytes 1572868
  13.0 1.7 %collective-permute-start.5 = (bf16[64,1024]{1,0:T(8,128)(2,1)S(1)}, bf16[64,1024]{1,0:T(8,128)(2,1)S(1)}, u32[]{:S(2)}, u32[]{:S(2)}) collective-permute-start(bf16[64,1024]{1,0:T(8,128)(2,1)S(1)} %collective-permute-done.1.refs_2_), channel_id=1, source_target_pairs={{0,4},{4,0},{8,12},{12,8},{16,20},{20,16},{24,28},{28,24},{1,5},{5... | collective-permute-start | bytes 393224 | tf_op jit(solution)/shard_map/ppermute | solution.py:124
  13.0 1.7 %collective-permute-start.7 = (bf16[64,1024]{1,0:T(8,128)(2,1)S(1)}, bf16[64,1024]{1,0:T(8,128)(2,1)S(1)}, u32[]{:S(2)}, u32[]{:S(2)}) collective-permute-start(bf16[64,1024]{1,0:T(8,128)(2,1)S(1)} %collective-permute-done.2.refs_3_), channel_id=1, source_target_pairs={{0,4},{4,0},{8,12},{12,8},{16,20},{20,16},{24,28},{28,24},{1,5},{5... | collective-permute-start | bytes 393224 | tf_op jit(solution)/shard_map/ppermute | solution.py:124
  13.5 1.3 %collective-permute-start.6 = (bf16[64,1024]{1,0:T(8,128)(2,1)S(1)}, bf16[64,1024]{1,0:T(8,128)(2,1)S(1)}, u32[]{:S(2)}, u32[]{:S(2)}) collective-permute-start(bf16[64,1024]{1,0:T(8,128)(2,1)S(1)} %collective-permute-done.3.refs_4_), channel_id=1, source_target_pairs={{0,4},{4,0},{8,12},{12,8},{16,20},{20,16},{24,28},{28,24},{1,5},{5... | collective-permute-start | bytes 393224 | tf_op jit(solution)/shard_map/ppermute | solution.py:124
  13.5 1.5 %collective-permute-start.8 = (bf16[64,1024]{1,0:T(8,128)(2,1)S(1)}, bf16[64,1024]{1,0:T(8,128)(2,1)S(1)}, u32[]{:S(2)}, u32[]{:S(2)}) collective-permute-start(bf16[64,1024]{1,0:T(8,128)(2,1)S(1)} %collective-permute-done.4.refs_5_), channel_id=1, source_target_pairs={{0,4},{4,0},{8,12},{12,8},{16,20},{20,16},{24,28},{28,24},{1,5},{5... | collective-permute-start | bytes 393224 | tf_op jit(solution)/shard_map/ppermute | solution.py:124
  15.8 6.0 %collective-permute-start.9 = (bf16[32,2176]{1,0:T(8,128)(2,1)S(1)}, bf16[32,2176]{1,0:T(8,128)(2,1)S(1)}, u32[]{:S(2)}, u32[]{:S(2)}) collective-permute-start(bf16[32,2176]{1,0:T(8,128)(2,1)S(1)} %get-tuple-element.30), channel_id=1, source_target_pairs={{0,1},{1,0},{2,3},{3,2},{4,6},{5,7},{6,4},{7,5},{8,9},{9,8},{10,11... | collective-permute-start | bytes 417800 | tf_op jit(solution)/shard_map/ppermute | solution.py:139
  17.4 5.1 %collective-permute-start.10 = (bf16[32,2176]{1,0:T(8,128)(2,1)S(1)}, bf16[32,2176]{1,0:T(8,128)(2,1)S(1)}, u32[]{:S(2)}, u32[]{:S(2)}) collective-permute-start(bf16[32,2176]{1,0:T(8,128)(2,1)S(1)} %get-tuple-element.31), channel_id=1, source_target_pairs={{0,2},{1,3},{2,0},{3,1},{4,5},{5,4},{6,7},{7,6},{8,10},{9,11},{10,... | collective-permute-start | bytes 417800 | tf_op jit(solution)/shard_map/ppermute | solution.py:139
  18.9 7.0 %collective-permute-start.11 = (bf16[32,2176]{1,0:T(8,128)(2,1)S(1)}, bf16[32,2176]{1,0:T(8,128)(2,1)S(1)}, u32[]{:S(2)}, u32[]{:S(2)}) collective-permute-start(bf16[32,2176]{1,0:T(8,128)(2,1)S(1)} %get-tuple-element.32), channel_id=1, source_target_pairs={{0,3},{1,2},{2,1},{3,0},{4,7},{5,6},{6,5},{7,4},{8,11},{9,10},{10,... | collective-permute-start | bytes 417800 | tf_op jit(solution)/shard_map/ppermute | solution.py:139

commit v4 on v3

--- a/solution.py
+++ b/solution.py
@@ -159,22 +159,25 @@
 
     limit = 16 * 2**20 if span * n_row <= 4096 else 40 * 2**20
     own = jnp.concatenate([keys, values], axis=0)
-    blocks = {0: [own], 1: [swap_row(own, 1)]}
-    far = sorted(range(2, n_row, 2), key=lambda m: (m & n_row // 2 == 0, m & 2 == 0))
-    for mask in far:
-        if mask & n_row // 2 and not mask & 2:
-            direct = send_up(own, mask, (mask, None))
-            relayed = send_up(blocks[mask ^ 2][0], mask, (None, 2))
-            blocks[mask] = [direct, relayed]
-        else:
-            blocks[mask] = [swap_row(own, mask)]
-    totals = sums([0, 1], [], False, "own_chip")
-    *totals, arrived = lax.optimization_barrier((*totals, [blocks[m] for m in far]))
-    blocks.update(zip(far, arrived))
-    for mask in far:
+    top = n_row // 2
+    near = list(range(2, top, 2))
+    once = [m for m in range(top, n_row, 2) if m & 2]
+    split = [m for m in range(top, n_row, 2) if not m & 2]
+    blocks = {0: [own]}
+    for mask in once + near:
+        blocks[mask] = [swap_row(own, mask)]
+    totals = sums([0], [], False, "own_block")
+    for mask in split:
+        blocks[mask] = [send_up(own, mask, (mask, None))]
+    *totals, arrived = lax.optimization_barrier((*totals, [blocks[m] for m in once]))
+    blocks.update(zip(once, arrived))
+    for mask in split:
+        blocks[mask].append(send_up(blocks[mask ^ 2][0], mask, (None, 2)))
+    far = split + once + near
+    for mask in [0] + far:
         blocks[mask ^ 1] = [swap_row(x, 1) for x in blocks[mask]][::-1]
     totals = sums(far, totals, False, "far_same_core")
-    messages = sums([m ^ 1 for m in far], totals, True, "far_other_core")
+    messages = sums([m ^ 1 for m in [0] + far], totals, True, "far_other_core")
     received = [messages[0]] + [swap_col(messages[j], j) for j in range(1, n_col)]
     return pl.pallas_call(
         combine_kernel,

time: 27 us -> 26 us (0.963)
  waiting for transfers between devices: 8.89 us -> 7.79 us
    ppermute x7, starting transfers between devices: 6.14 us -> 7.49 us  [swap_row(): return lax.ppermute(x, 'row', [(i, i ^ mask) for i in range(n_row)])]
    ppermute x2, starting transfers between devices: 3.27 us -> 1.99 us  [send_up(): return lax.ppermute(x, ('row', 'col'), pairs)]
    ppermute x3, waiting for transfers between devices: 6.58 us -> 6.06 us  [swap_col(): return lax.ppermute(x, ('row', 'col'), pairs)]
    ppermute x7, waiting for transfers between devices: 2.07 us -> 1.73 us  [swap_row(): return lax.ppermute(x, 'row', [(i, i ^ mask) for i in range(n_row)])]
where the time goes in v4:
time: 26 us; the launch traced here: 25.7 us
  starting transfers between devices  13 us (50%)
  waiting for transfers between devices  7.79 us (30%)
  Pallas kernels  2.89 us (11%)
  local copies, waits for them, and re-layouts  1.93 us (7%)
    ppermute x7, starting transfers between devices, swap_row(): return lax.ppermute(x, 'row', [(i, i ^ mask) for i in range(n_row)])  7.49 us
    ppermute x3, waiting for transfers between devices, swap_col(): return lax.ppermute(x, ('row', 'col'), pairs)  6.06 us
    ppermute x3, starting transfers between devices, swap_col(): return lax.ppermute(x, ('row', 'col'), pairs)  3.55 us
    pallas_call x3, Pallas kernels, sums(): pl.pallas_call(functools.partial(sums_kernel, masks, widths, len(before)...  2.04 us
    ppermute x2, starting transfers between devices, send_up(): return lax.ppermute(x, ('row', 'col'), pairs)  1.99 us
    unnamed x5, local copies, waits for them, and re-layouts  1.92 us
    ppermute x7, waiting for transfers between devices, swap_row(): return lax.ppermute(x, 'row', [(i, i ^ mask) for i in range(n_row)])  1.73 us
    pallas_call x1, Pallas kernels, per_device(): pl.pallas_call(combine_kernel, out_shape=jax.ShapeDtypeStruct((blk, feat_...  0.85 us
  transfers between devices with their start and end apart: 12, of which 7 were waited for; matrix products, arithmetic and copies ran while one was open for 0% of the time, Pallas kernels for 5%

profile of v4, /device:TPU:0, one launch (start us, length us, event | category | flops | bytes accessed | tf_op | source)
XLA Modules:
  0.0 25.7 jit_solution(10830631048868354906)
XLA Ops:
  0.0 0.9 %constant_dynamic-update-slice_fusion.1 = bf16[64,1024]{1,0:T(8,128)(2,1)S(1)} fusion(bf16[32,1024]{1,0:T(8,128)(2,1)} %param.4), kind=kLoop, calls=%fused_computation.1 | loop fusion | bytes 131072
  0.9 5.1 %collective-permute-start = (bf16[64,1024]{1,0:T(8,128)(2,1)S(1)}, bf16[64,1024]{1,0:T(8,128)(2,1)S(1)}, u32[]{:S(2)}, u32[]{:S(2)}) collective-permute-start(bf16[64,1024]{1,0:T(8,128)(2,1)S(1)} %constant_dynamic-update-slice_fusion.refs_0_), channel_id=1, source_target_pairs={{0,24},{4,28},{8,16},{12,20},{16,8},{20,12},{24,0},{28,4},{1,25},{... | collective-permute-start | bytes 393224 | tf_op jit(solution)/shard_map/ppermute | solution.py:124
  6.0 1.3 %collective-permute-start.1 = (bf16[64,1024]{1,0:T(8,128)(2,1)S(1)}, bf16[64,1024]{1,0:T(8,128)(2,1)S(1)}, u32[]{:S(2)}, u32[]{:S(2)}) collective-permute-start(bf16[64,1024]{1,0:T(8,128)(2,1)S(1)} %constant_dynamic-update-slice_fusion.refs_0_), channel_id=1, source_target_pairs={{0,16},{1,17},{2,18},{3,19},{8,24},{9,25},{10,26},{11,27}} | collective-permute-start | bytes 393224 | tf_op jit(solution)/shard_map/ppermute | solution.py:132
  7.3 1.2 %collective-permute-start.3 = (bf16[64,1024]{1,0:T(8,128)(2,1)S(1)}, bf16[64,1024]{1,0:T(8,128)(2,1)S(1)}, u32[]{:S(2)}, u32[]{:S(2)}) collective-permute-start(bf16[64,1024]{1,0:T(8,128)(2,1)S(1)} %constant_dynamic-update-slice_fusion.refs_0_), channel_id=1, source_target_pairs={{0,8},{4,12},{8,0},{12,4},{16,24},{20,28},{24,16},{28,20},{1,9},{5... | collective-permute-start | bytes 393224 | tf_op jit(solution)/shard_map/ppermute | solution.py:124
  8.6 1.0 %copy-done = bf16[128,2048]{1,0:T(8,128)(2,1)S(1)} copy-done((bf16[128,2048]{1,0:T(8,128)(2,1)S(1)}, bf16[128,2048]{1,0:T(8,128)(2,1)}, u32[]{:S(2)}) %copy-start) | copy-done | bytes 524312
  9.6 0.7 %own_block.1 = (f32[128,2048]{1,0:T(8,128)S(1)}, f32[128,128]{1,0:T(8,128)S(1)}) custom-call(bf16[128,2048]{1,0:T(8,128)(2,1)S(1)} %copy-done, bf16[64,1024]{1,0:T(8,128)(2,1)S(1)} %constant_dynamic-update-slice_fusion.refs_0_), custom_call_target="tpu_custom_call" | custom-call | tf_op jit(solution)/shard_map/own_block/pallas_call | solution.py:150
  10.3 0.1 collective-permute-done.refs_4_
  10.4 0.7 %collective-permute-start.2 = (bf16[64,1024]{1,0:T(8,128)(2,1)S(1)}, bf16[64,1024]{1,0:T(8,128)(2,1)S(1)}, u32[]{:S(2)}, u32[]{:S(2)}) collective-permute-start(bf16[64,1024]{1,0:T(8,128)(2,1)S(1)} %collective-permute-done.refs_4_), channel_id=1, source_target_pairs={{20,28},{21,29},{22,30},{23,31},{28,20},{29,21},{30,22},{31,23}} | collective-permute-start | bytes 393224 | tf_op jit(solution)/shard_map/ppermute | solution.py:132
  11.0 0.1 collective-permute-start.4
  11.1 0.5 %collective-permute-start.7 = (bf16[64,1024]{1,0:T(8,128)(2,1)S(1)}, bf16[64,1024]{1,0:T(8,128)(2,1)S(1)}, u32[]{:S(2)}, u32[]{:S(2)}) collective-permute-start(bf16[64,1024]{1,0:T(8,128)(2,1)S(1)} %collective-permute-done.refs_4_), channel_id=1, source_target_pairs={{0,4},{4,0},{8,12},{12,8},{16,20},{20,16},{24,28},{28,24},{1,5},{5... | collective-permute-start | bytes 393224 | tf_op jit(solution)/shard_map/ppermute | solution.py:124
  11.6 0.1 collective-permute-start.6
  11.7 1.3 %collective-permute-done.3.refs_5_ = bf16[64,1024]{1,0:T(8,128)(2,1)S(1)} collective-permute-done((bf16[64,1024]{1,0:T(8,128)(2,1)S(1)}, bf16[64,1024]{1,0:T(8,128)(2,1)S(1)}, u32[]{:S(2)}, u32[]{:S(2)}) %collective-permute-start.3) | collective-permute-done | bytes 131104 | tf_op jit(solution)/shard_map/ppermute | solution.py:124
  13.0 0.5 %collective-permute-start.5 = (bf16[64,1024]{1,0:T(8,128)(2,1)S(1)}, bf16[64,1024]{1,0:T(8,128)(2,1)S(1)}, u32[]{:S(2)}, u32[]{:S(2)}) collective-permute-start(bf16[64,1024]{1,0:T(8,128)(2,1)S(1)} %collective-permute-done.2.refs_3_), channel_id=1, source_target_pairs={{0,4},{4,0},{8,12},{12,8},{16,20},{20,16},{24,28},{28,24},{1,5},{5... | collective-permute-start | bytes 393224 | tf_op jit(solution)/shard_map/ppermute | solution.py:124
  13.5 0.7 %far_same_core.1 = (f32[128,2048]{1,0:T(8,128)S(1)}, f32[128,128]{1,0:T(8,128)S(1)}) custom-call(bf16[128,2048]{1,0:T(8,128)(2,1)S(1)} %copy-done, f32[128,2048]{1,0:T(8,128)S(1)} %get-tuple-element.18.refs_0_, f32[128,128]{1,0:T(8,128)S(1)} %get-tuple-element.19.refs_1_, bf16[64,1024]{1,0:T(8,128)(2,1)S(1)} %collective-permute-done.1.refs_2_, ...), custom_call_target="tpu_custom_call" | custom-call | tf_op jit(solution)/shard_map/far_same_core/pallas_call | solution.py:150
  14.3 0.1 collective-permute-done.8.refs_6_
  14.4 0.2 collective-permute-done.5.refs_3_
  14.6 0.7 %far_other_core.1 = (bf16[32,2176]{1,0:T(8,128)(2,1)S(1)}, bf16[32,2176]{1,0:T(8,128)(2,1)S(1)}, bf16[32,2176]{1,0:T(8,128)(2,1)S(1)}, bf16[32,2176]{1,0:T(8,128)(2,1)S(1)}) custom-call(bf16[128,2048]{1,0:T(8,128)(2,1)S(1)} %copy-done, f32[128,2048]{1,0:T(8,128)S(1)} %get-tuple-element.21.refs_0_, f32[128,128]{1,0:T(8,128)S(1)} %get-tuple-element.22.refs_1_, ...), custom_call_target="tpu_custom_call" | custom-call | tf_op jit(solution)/shard_map/far_other_core/pallas_call | solution.py:150
  15.3 1.6 %collective-permute-start.10 = (bf16[32,2176]{1,0:T(8,128)(2,1)S(1)}, bf16[32,2176]{1,0:T(8,128)(2,1)S(1)}, u32[]{:S(2)}, u32[]{:S(2)}) collective-permute-start(bf16[32,2176]{1,0:T(8,128)(2,1)S(1)} %get-tuple-element.25), channel_id=1, source_target_pairs={{0,2},{1,3},{2,0},{3,1},{4,5},{5,4},{6,7},{7,6},{8,10},{9,11},{10,... | collective-permute-start | bytes 417800 | tf_op jit(solution)/shard_map/ppermute | solution.py:139
  16.8 1.4 %collective-permute-start.11 = (bf16[32,2176]{1,0:T(8,128)(2,1)S(1)}, bf16[32,2176]{1,0:T(8,128)(2,1)S(1)}, u32[]{:S(2)}, u32[]{:S(2)}) collective-permute-start(bf16[32,2176]{1,0:T(8,128)(2,1)S(1)} %get-tuple-element.26), channel_id=1, source_target_pairs={{0,3},{1,2},{2,1},{3,0},{4,7},{5,6},{6,5},{7,4},{8,11},{9,10},{10,... | collective-permute-start | bytes 417800 | tf_op jit(solution)/shard_map/ppermute | solution.py:139
  18.3 0.5 %collective-permute-start.9 = (bf16[32,2176]{1,0:T(8,128)(2,1)S(1)}, bf16[32,2176]{1,0:T(8,128)(2,1)S(1)}, u32[]{:S(2)}, u32[]{:S(2)}) collective-permute-start(bf16[32,2176]{1,0:T(8,128)(2,1)S(1)} %get-tuple-element.24), channel_id=1, source_target_pairs={{0,1},{1,0},{2,3},{3,2},{4,6},{5,7},{6,4},{7,5},{8,9},{9,8},{10,11... | collective-permute-start | bytes 417800 | tf_op jit(solution)/shard_map/ppermute | solution.py:139
  18.8 4.2 %collective-permute-done.10.refs_2_ = bf16[32,2176]{1,0:T(8,128)(2,1)S(1)} collective-permute-done((bf16[32,2176]{1,0:T(8,128)(2,1)S(1)}, bf16[32,2176]{1,0:T(8,128)(2,1)S(1)}, u32[]{:S(2)}, u32[]{:S(2)}) %collective-permute-start.10) | collective-permute-done | bytes 139296 | tf_op jit(solution)/shard_map/ppermute | solution.py:139
  23.0 0.8 %collective-permute-done.11.refs_3_ = bf16[32,2176]{1,0:T(8,128)(2,1)S(1)} collective-permute-done((bf16[32,2176]{1,0:T(8,128)(2,1)S(1)}, bf16[32,2176]{1,0:T(8,128)(2,1)S(1)}, u32[]{:S(2)}, u32[]{:S(2)}) %collective-permute-start.11) | collective-permute-done | bytes 139296 | tf_op jit(solution)/shard_map/ppermute | solution.py:139
  23.8 1.1 %collective-permute-done.9.refs_1_ = bf16[32,2176]{1,0:T(8,128)(2,1)S(1)} collective-permute-done((bf16[32,2176]{1,0:T(8,128)(2,1)S(1)}, bf16[32,2176]{1,0:T(8,128)(2,1)S(1)}, u32[]{:S(2)}, u32[]{:S(2)}) %collective-permute-start.9) | collective-permute-done | bytes 139296 | tf_op jit(solution)/shard_map/ppermute | solution.py:139
  24.9 0.9 %combine.1 = bf16[32,2048]{1,0:T(8,128)(2,1)} custom-call(bf16[32,2176]{1,0:T(8,128)(2,1)S(1)} %get-tuple-element.23.refs_0_, bf16[32,2176]{1,0:T(8,128)(2,1)S(1)} %collective-permute-done.9.refs_1_, bf16[32,2176]{1,0:T(8,128)(2,1)S(1)} %collective-permute-done.10.refs_2_, bf16[32,2176]{1,0:T(8,128)(2,1)S(1)} %collective-permute-done.11.refs_3_), custom_call_target="tpu_custom_call" | custom-call | tf_op jit(solution)/shard_map/combine/pallas_call | solution.py:182
  (10 shorter events, 0.0 us)
Async XLA Ops:
  0.0 0.9 %copy-start.1 = (bf16[32,1024]{1,0:T(8,128)(2,1)S(1)}, bf16[32,1024]{1,0:T(8,128)(2,1)}, u32[]{:S(2)}) copy-start(bf16[32,1024]{1,0:T(8,128)(2,1)} %param.5) | copy-start | bytes 196612
  0.9 9.5 %collective-permute-start = (bf16[64,1024]{1,0:T(8,128)(2,1)S(1)}, bf16[64,1024]{1,0:T(8,128)(2,1)S(1)}, u32[]{:S(2)}, u32[]{:S(2)}) collective-permute-start(bf16[64,1024]{1,0:T(8,128)(2,1)S(1)} %constant_dynamic-update-slice_fusion.refs_0_), channel_id=1, source_target_pairs={{0,24},{4,28},{8,16},{12,20},{16,8},{20,12},{24,0},{28,4},{1,25},{... | collective-permute-start | bytes 393224 | tf_op jit(solution)/shard_map/ppermute | solution.py:124
  6.0 5.6 %collective-permute-start.1 = (bf16[64,1024]{1,0:T(8,128)(2,1)S(1)}, bf16[64,1024]{1,0:T(8,128)(2,1)S(1)}, u32[]{:S(2)}, u32[]{:S(2)}) collective-permute-start(bf16[64,1024]{1,0:T(8,128)(2,1)S(1)} %constant_dynamic-update-slice_fusion.refs_0_), channel_id=1, source_target_pairs={{0,16},{1,17},{2,18},{3,19},{8,24},{9,25},{10,26},{11,27}} | collective-permute-start | bytes 393224 | tf_op jit(solution)/shard_map/ppermute | solution.py:132
  7.3 5.7 %collective-permute-start.3 = (bf16[64,1024]{1,0:T(8,128)(2,1)S(1)}, bf16[64,1024]{1,0:T(8,128)(2,1)S(1)}, u32[]{:S(2)}, u32[]{:S(2)}) collective-permute-start(bf16[64,1024]{1,0:T(8,128)(2,1)S(1)} %constant_dynamic-update-slice_fusion.refs_0_), channel_id=1, source_target_pairs={{0,8},{4,12},{8,0},{12,4},{16,24},{20,28},{24,16},{28,20},{1,9},{5... | collective-permute-start | bytes 393224 | tf_op jit(solution)/shard_map/ppermute | solution.py:124
  8.6 1.0 %copy-start = (bf16[128,2048]{1,0:T(8,128)(2,1)S(1)}, bf16[128,2048]{1,0:T(8,128)(2,1)}, u32[]{:S(2)}) copy-start(bf16[128,2048]{1,0:T(8,128)(2,1)} %q_ref.5) | copy-start | bytes 1572868
  10.4 2.6 %collective-permute-start.2 = (bf16[64,1024]{1,0:T(8,128)(2,1)S(1)}, bf16[64,1024]{1,0:T(8,128)(2,1)S(1)}, u32[]{:S(2)}, u32[]{:S(2)}) collective-permute-start(bf16[64,1024]{1,0:T(8,128)(2,1)S(1)} %collective-permute-done.refs_4_), channel_id=1, source_target_pairs={{20,28},{21,29},{22,30},{23,31},{28,20},{29,21},{30,22},{31,23}} | collective-permute-start | bytes 393224 | tf_op jit(solution)/shard_map/ppermute | solution.py:132
  11.0 3.2 %collective-permute-start.4 = (bf16[64,1024]{1,0:T(8,128)(2,1)S(1)}, bf16[64,1024]{1,0:T(8,128)(2,1)S(1)}, u32[]{:S(2)}, u32[]{:S(2)}) collective-permute-start(bf16[64,1024]{1,0:T(8,128)(2,1)S(1)} %constant_dynamic-update-slice_fusion.refs_0_), channel_id=1, source_target_pairs={{0,4},{4,0},{8,12},{12,8},{16,20},{20,16},{24,28},{28,24},{1,5},{5... | collective-permute-start | bytes 393224 | tf_op jit(solution)/shard_map/ppermute | solution.py:124
  11.1 3.1 %collective-permute-start.7 = (bf16[64,1024]{1,0:T(8,128)(2,1)S(1)}, bf16[64,1024]{1,0:T(8,128)(2,1)S(1)}, u32[]{:S(2)}, u32[]{:S(2)}) collective-permute-start(bf16[64,1024]{1,0:T(8,128)(2,1)S(1)} %collective-permute-done.refs_4_), channel_id=1, source_target_pairs={{0,4},{4,0},{8,12},{12,8},{16,20},{20,16},{24,28},{28,24},{1,5},{5... | collective-permute-start | bytes 393224 | tf_op jit(solution)/shard_map/ppermute | solution.py:124
  11.6 2.6 %collective-permute-start.6 = (bf16[64,1024]{1,0:T(8,128)(2,1)S(1)}, bf16[64,1024]{1,0:T(8,128)(2,1)S(1)}, u32[]{:S(2)}, u32[]{:S(2)}) collective-permute-start(bf16[64,1024]{1,0:T(8,128)(2,1)S(1)} %collective-permute-done.1.refs_2_), channel_id=1, source_target_pairs={{0,4},{4,0},{8,12},{12,8},{16,20},{20,16},{24,28},{28,24},{1,5},{5... | collective-permute-start | bytes 393224 | tf_op jit(solution)/shard_map/ppermute | solution.py:124
  13.0 1.3 %collective-permute-start.8 = (bf16[64,1024]{1,0:T(8,128)(2,1)S(1)}, bf16[64,1024]{1,0:T(8,128)(2,1)S(1)}, u32[]{:S(2)}, u32[]{:S(2)}) collective-permute-start(bf16[64,1024]{1,0:T(8,128)(2,1)S(1)} %collective-permute-done.3.refs_5_), channel_id=1, source_target_pairs={{0,4},{4,0},{8,12},{12,8},{16,20},{20,16},{24,28},{28,24},{1,5},{5... | collective-permute-start | bytes 393224 | tf_op jit(solution)/shard_map/ppermute | solution.py:124
  13.0 1.5 %collective-permute-start.5 = (bf16[64,1024]{1,0:T(8,128)(2,1)S(1)}, bf16[64,1024]{1,0:T(8,128)(2,1)S(1)}, u32[]{:S(2)}, u32[]{:S(2)}) collective-permute-start(bf16[64,1024]{1,0:T(8,128)(2,1)S(1)} %collective-permute-done.2.refs_3_), channel_id=1, source_target_pairs={{0,4},{4,0},{8,12},{12,8},{16,20},{20,16},{24,28},{28,24},{1,5},{5... | collective-permute-start | bytes 393224 | tf_op jit(solution)/shard_map/ppermute | solution.py:124
  15.3 7.8 %collective-permute-start.10 = (bf16[32,2176]{1,0:T(8,128)(2,1)S(1)}, bf16[32,2176]{1,0:T(8,128)(2,1)S(1)}, u32[]{:S(2)}, u32[]{:S(2)}) collective-permute-start(bf16[32,2176]{1,0:T(8,128)(2,1)S(1)} %get-tuple-element.25), channel_id=1, source_target_pairs={{0,2},{1,3},{2,0},{3,1},{4,5},{5,4},{6,7},{7,6},{8,10},{9,11},{10,... | collective-permute-start | bytes 417800 | tf_op jit(solution)/shard_map/ppermute | solution.py:139
  16.8 6.9 %collective-permute-start.11 = (bf16[32,2176]{1,0:T(8,128)(2,1)S(1)}, bf16[32,2176]{1,0:T(8,128)(2,1)S(1)}, u32[]{:S(2)}, u32[]{:S(2)}) collective-permute-start(bf16[32,2176]{1,0:T(8,128)(2,1)S(1)} %get-tuple-element.26), channel_id=1, source_target_pairs={{0,3},{1,2},{2,1},{3,0},{4,7},{5,6},{6,5},{7,4},{8,11},{9,10},{10,... | collective-permute-start | bytes 417800 | tf_op jit(solution)/shard_map/ppermute | solution.py:139
  18.3 6.6 %collective-permute-start.9 = (bf16[32,2176]{1,0:T(8,128)(2,1)S(1)}, bf16[32,2176]{1,0:T(8,128)(2,1)S(1)}, u32[]{:S(2)}, u32[]{:S(2)}) collective-permute-start(bf16[32,2176]{1,0:T(8,128)(2,1)S(1)} %get-tuple-element.24), channel_id=1, source_target_pairs={{0,1},{1,0},{2,3},{3,2},{4,6},{5,7},{6,4},{7,5},{8,9},{9,8},{10,11... | collective-permute-start | bytes 417800 | tf_op jit(solution)/shard_map/ppermute | solution.py:139

commit v5 on v4

--- a/solution.py
+++ b/solution.py
@@ -45,21 +45,27 @@
     parts = [pl.ds(pl.multiple_of(c * blk, blk), blk) for c in columns]
     pos = jnp.concatenate([(row * n_col + c) * blk + sub for c in columns], axis=0)
     keep = jnp.where(key_pos <= pos, 1.0, 0.0).astype(jnp.float32)
-    for kv in range(kv_heads):
-        k_head = k_all[:, kv * HEAD : (kv + 1) * HEAD]
-        v_head = v_all[:, kv * HEAD : (kv + 1) * HEAD]
-        for h in range(kv * group, (kv + 1) * group):
-            q_head = jnp.concatenate([q_ref[p, h * HEAD : (h + 1) * HEAD] for p in parts], axis=0)
-            scores = lax.dot_general(
-                q_head, k_head, (((1,), (1,)), ((), ())), preferred_element_type=jnp.float32
-            )
-            capped = jnp.tanh(scores * (SCALE / CAP)) * (CAP / math.log(2.0))
-            weights = jnp.exp2(capped) * keep
-            denom = jnp.sum(weights, axis=1, keepdims=True)
-            numer = jnp.dot(
-                weights.astype(jnp.bfloat16), v_head, preferred_element_type=jnp.float32
-            )
-            emit(h, numer, denom)
+    scores = [
+        lax.dot_general(
+            jnp.concatenate([q_ref[p, h * HEAD : (h + 1) * HEAD] for p in parts], axis=0),
+            k_all[:, h // group * HEAD : (h // group + 1) * HEAD],
+            (((1,), (1,)), ((), ())),
+            preferred_element_type=jnp.float32,
+        )
+        for h in range(kv_heads * group)
+    ]
+    weights = []
+    for score in scores:
+        capped = jnp.tanh(score * (SCALE / CAP)) * (CAP / math.log(2.0))
+        weights.append(jnp.exp2(capped) * keep)
+    for h, weight in enumerate(weights):
+        denom = jnp.sum(weight, axis=1, keepdims=True)
+        numer = jnp.dot(
+            weight.astype(jnp.bfloat16),
+            v_all[:, h // group * HEAD : (h // group + 1) * HEAD],
+            preferred_element_type=jnp.float32,
+        )
+        emit(h, numer, denom)
 
 
 def chunks_of(n_col):
@@ -176,8 +182,8 @@
     far = split + once + near
     for mask in [0] + far:
         blocks[mask ^ 1] = [swap_row(x, 1) for x in blocks[mask]][::-1]
-    totals = sums(far, totals, False, "far_same_core")
-    messages = sums([m ^ 1 for m in [0] + far], totals, True, "far_other_core")
+    totals = sums([1] + far, totals, False, "far_same_core")
+    messages = sums([m ^ 1 for m in far], totals, True, "far_other_core")
     received = [messages[0]] + [swap_col(messages[j], j) for j in range(1, n_col)]
     return pl.pallas_call(
         combine_kernel,

time: 26 us -> 25.7 us (0.988)
  Pallas kernels: 2.89 us -> 2.17 us
  waiting for transfers between devices: 7.79 us -> 8.28 us
    pallas_call x3, Pallas kernels: 2.04 us -> 1.32 us  [sums(): pl.pallas_call(functools.partial(sums_kernel, masks, widths, len(before)...]
    ppermute x7, waiting for transfers between devices: 1.73 us -> 2.21 us  [swap_row(): return lax.ppermute(x, 'row', [(i, i ^ mask) for i in range(n_row)])]
  transfers between devices with their start and end apart: 12 -> 12, of which waited for: 7 -> 7; matrix products, arithmetic and copies ran while one was open for 0% -> 0% of each run, Pallas kernels for 5% -> 3%
where the time goes in v5:
time: 25.7 us; the launch traced here: 25.5 us
  starting transfers between devices  13 us (51%)
  waiting for transfers between devices  8.28 us (32%)
  Pallas kernels  2.17 us (8%)
  local copies, waits for them, and re-layouts  1.93 us (8%)
    ppermute x7, starting transfers between devices, swap_row(): return lax.ppermute(x, 'row', [(i, i ^ mask) for i in range(n_row)])  7.49 us
    ppermute x3, waiting for transfers between devices, swap_col(): return lax.ppermute(x, ('row', 'col'), pairs)  6.06 us
    ppermute x3, starting transfers between devices, swap_col(): return lax.ppermute(x, ('row', 'col'), pairs)  3.55 us
    ppermute x7, waiting for transfers between devices, swap_row(): return lax.ppermute(x, 'row', [(i, i ^ mask) for i in range(n_row)])  2.21 us
    ppermute x2, starting transfers between devices, send_up(): return lax.ppermute(x, ('row', 'col'), pairs)  1.99 us
    unnamed x5, local copies, waits for them, and re-layouts  1.92 us
    pallas_call x3, Pallas kernels, sums(): pl.pallas_call(functools.partial(sums_kernel, masks, widths, len(before)...  1.32 us
    pallas_call x1, Pallas kernels, per_device(): pl.pallas_call(combine_kernel, out_shape=jax.ShapeDtypeStruct((blk, feat_...  0.85 us
  transfers between devices with their start and end apart: 12, of which 7 were waited for; matrix products, arithmetic and copies ran while one was open for 0% of the time, Pallas kernels for 3%

profile of v5, /device:TPU:0, one launch (start us, length us, event | category | flops | bytes accessed | tf_op | source)
XLA Modules:
  0.0 25.5 jit_solution(12086511121558850659)
XLA Ops:
  0.0 0.9 %constant_dynamic-update-slice_fusion.1 = bf16[64,1024]{1,0:T(8,128)(2,1)S(1)} fusion(bf16[32,1024]{1,0:T(8,128)(2,1)} %param.4), kind=kLoop, calls=%fused_computation.1 | loop fusion | bytes 131072
  0.9 5.1 %collective-permute-start = (bf16[64,1024]{1,0:T(8,128)(2,1)S(1)}, bf16[64,1024]{1,0:T(8,128)(2,1)S(1)}, u32[]{:S(2)}, u32[]{:S(2)}) collective-permute-start(bf16[64,1024]{1,0:T(8,128)(2,1)S(1)} %constant_dynamic-update-slice_fusion.refs_0_), channel_id=1, source_target_pairs={{0,24},{4,28},{8,16},{12,20},{16,8},{20,12},{24,0},{28,4},{1,25},{... | collective-permute-start | bytes 393224 | tf_op jit(solution)/shard_map/ppermute | solution.py:130
  6.0 1.3 %collective-permute-start.2 = (bf16[64,1024]{1,0:T(8,128)(2,1)S(1)}, bf16[64,1024]{1,0:T(8,128)(2,1)S(1)}, u32[]{:S(2)}, u32[]{:S(2)}) collective-permute-start(bf16[64,1024]{1,0:T(8,128)(2,1)S(1)} %constant_dynamic-update-slice_fusion.refs_0_), channel_id=1, source_target_pairs={{0,16},{1,17},{2,18},{3,19},{8,24},{9,25},{10,26},{11,27}} | collective-permute-start | bytes 393224 | tf_op jit(solution)/shard_map/ppermute | solution.py:138
  7.3 1.2 %collective-permute-start.4 = (bf16[64,1024]{1,0:T(8,128)(2,1)S(1)}, bf16[64,1024]{1,0:T(8,128)(2,1)S(1)}, u32[]{:S(2)}, u32[]{:S(2)}) collective-permute-start(bf16[64,1024]{1,0:T(8,128)(2,1)S(1)} %constant_dynamic-update-slice_fusion.refs_0_), channel_id=1, source_target_pairs={{0,8},{4,12},{8,0},{12,4},{16,24},{20,28},{24,16},{28,20},{1,9},{5... | collective-permute-start | bytes 393224 | tf_op jit(solution)/shard_map/ppermute | solution.py:130
  8.6 1.0 %copy-done = bf16[128,2048]{1,0:T(8,128)(2,1)S(1)} copy-done((bf16[128,2048]{1,0:T(8,128)(2,1)S(1)}, bf16[128,2048]{1,0:T(8,128)(2,1)}, u32[]{:S(2)}) %copy-start) | copy-done | bytes 524312
  9.6 0.4 %own_block.1 = (f32[128,2048]{1,0:T(8,128)S(1)}, f32[128,128]{1,0:T(8,128)S(1)}) custom-call(bf16[128,2048]{1,0:T(8,128)(2,1)S(1)} %copy-done, bf16[64,1024]{1,0:T(8,128)(2,1)S(1)} %constant_dynamic-update-slice_fusion.refs_0_), custom_call_target="tpu_custom_call" | custom-call | tf_op jit(solution)/shard_map/own_block/pallas_call | solution.py:156
  10.0 0.3 %collective-permute-done.refs_5_ = bf16[64,1024]{1,0:T(8,128)(2,1)S(1)} collective-permute-done((bf16[64,1024]{1,0:T(8,128)(2,1)S(1)}, bf16[64,1024]{1,0:T(8,128)(2,1)S(1)}, u32[]{:S(2)}, u32[]{:S(2)}) %collective-permute-start) | collective-permute-done | bytes 131104 | tf_op jit(solution)/shard_map/ppermute | solution.py:130
  10.4 0.7 %collective-permute-start.3 = (bf16[64,1024]{1,0:T(8,128)(2,1)S(1)}, bf16[64,1024]{1,0:T(8,128)(2,1)S(1)}, u32[]{:S(2)}, u32[]{:S(2)}) collective-permute-start(bf16[64,1024]{1,0:T(8,128)(2,1)S(1)} %collective-permute-done.refs_5_), channel_id=1, source_target_pairs={{20,28},{21,29},{22,30},{23,31},{28,20},{29,21},{30,22},{31,23}} | collective-permute-start | bytes 393224 | tf_op jit(solution)/shard_map/ppermute | solution.py:138
  11.0 0.1 collective-permute-start.1
  11.1 0.5 %collective-permute-start.7 = (bf16[64,1024]{1,0:T(8,128)(2,1)S(1)}, bf16[64,1024]{1,0:T(8,128)(2,1)S(1)}, u32[]{:S(2)}, u32[]{:S(2)}) collective-permute-start(bf16[64,1024]{1,0:T(8,128)(2,1)S(1)} %collective-permute-done.refs_5_), channel_id=1, source_target_pairs={{0,4},{4,0},{8,12},{12,8},{16,20},{20,16},{24,28},{28,24},{1,5},{5... | collective-permute-start | bytes 393224 | tf_op jit(solution)/shard_map/ppermute | solution.py:130
  11.6 0.1 collective-permute-start.6
  11.7 1.3 %collective-permute-done.4.refs_6_ = bf16[64,1024]{1,0:T(8,128)(2,1)S(1)} collective-permute-done((bf16[64,1024]{1,0:T(8,128)(2,1)S(1)}, bf16[64,1024]{1,0:T(8,128)(2,1)S(1)}, u32[]{:S(2)}, u32[]{:S(2)}) %collective-permute-start.4) | collective-permute-done | bytes 131104 | tf_op jit(solution)/shard_map/ppermute | solution.py:130
  13.0 0.5 %collective-permute-start.5 = (bf16[64,1024]{1,0:T(8,128)(2,1)S(1)}, bf16[64,1024]{1,0:T(8,128)(2,1)S(1)}, u32[]{:S(2)}, u32[]{:S(2)}) collective-permute-start(bf16[64,1024]{1,0:T(8,128)(2,1)S(1)} %collective-permute-done.3.refs_4_), channel_id=1, source_target_pairs={{0,4},{4,0},{8,12},{12,8},{16,20},{20,16},{24,28},{28,24},{1,5},{5... | collective-permute-start | bytes 393224 | tf_op jit(solution)/shard_map/ppermute | solution.py:130
  13.5 0.5 %far_same_core.1 = (f32[128,2048]{1,0:T(8,128)S(1)}, f32[128,128]{1,0:T(8,128)S(1)}) custom-call(bf16[128,2048]{1,0:T(8,128)(2,1)S(1)} %copy-done, f32[128,2048]{1,0:T(8,128)S(1)} %get-tuple-element.18.refs_0_, f32[128,128]{1,0:T(8,128)S(1)} %get-tuple-element.19.refs_1_, bf16[64,1024]{1,0:T(8,128)(2,1)S(1)} %collective-permute-done.1.refs_2_, ...), custom_call_target="tpu_custom_call" | custom-call | tf_op jit(solution)/shard_map/far_same_core/pallas_call | solution.py:156
  14.0 0.4 %collective-permute-done.8.refs_5_ = bf16[64,1024]{1,0:T(8,128)(2,1)S(1)} collective-permute-done((bf16[64,1024]{1,0:T(8,128)(2,1)S(1)}, bf16[64,1024]{1,0:T(8,128)(2,1)S(1)}, u32[]{:S(2)}, u32[]{:S(2)}) %collective-permute-start.8) | collective-permute-done | bytes 131104 | tf_op jit(solution)/shard_map/ppermute | solution.py:130
  14.4 0.2 collective-permute-done.5.refs_2_
  14.6 0.5 %far_other_core.1 = (bf16[32,2176]{1,0:T(8,128)(2,1)S(1)}, bf16[32,2176]{1,0:T(8,128)(2,1)S(1)}, bf16[32,2176]{1,0:T(8,128)(2,1)S(1)}, bf16[32,2176]{1,0:T(8,128)(2,1)S(1)}) custom-call(bf16[128,2048]{1,0:T(8,128)(2,1)S(1)} %copy-done, f32[128,2048]{1,0:T(8,128)S(1)} %get-tuple-element.21.refs_0_, f32[128,128]{1,0:T(8,128)S(1)} %get-tuple-element.22.refs_1_, ...), custom_call_target="tpu_custom_call" | custom-call | tf_op jit(solution)/shard_map/far_other_core/pallas_call | solution.py:156
  15.0 1.6 %collective-permute-start.10 = (bf16[32,2176]{1,0:T(8,128)(2,1)S(1)}, bf16[32,2176]{1,0:T(8,128)(2,1)S(1)}, u32[]{:S(2)}, u32[]{:S(2)}) collective-permute-start(bf16[32,2176]{1,0:T(8,128)(2,1)S(1)} %get-tuple-element.25), channel_id=1, source_target_pairs={{0,2},{1,3},{2,0},{3,1},{4,5},{5,4},{6,7},{7,6},{8,10},{9,11},{10,... | collective-permute-start | bytes 417800 | tf_op jit(solution)/shard_map/ppermute | solution.py:145
  16.6 1.4 %collective-permute-start.11 = (bf16[32,2176]{1,0:T(8,128)(2,1)S(1)}, bf16[32,2176]{1,0:T(8,128)(2,1)S(1)}, u32[]{:S(2)}, u32[]{:S(2)}) collective-permute-start(bf16[32,2176]{1,0:T(8,128)(2,1)S(1)} %get-tuple-element.26), channel_id=1, source_target_pairs={{0,3},{1,2},{2,1},{3,0},{4,7},{5,6},{6,5},{7,4},{8,11},{9,10},{10,... | collective-permute-start | bytes 417800 | tf_op jit(solution)/shard_map/ppermute | solution.py:145
  18.0 0.5 %collective-permute-start.9 = (bf16[32,2176]{1,0:T(8,128)(2,1)S(1)}, bf16[32,2176]{1,0:T(8,128)(2,1)S(1)}, u32[]{:S(2)}, u32[]{:S(2)}) collective-permute-start(bf16[32,2176]{1,0:T(8,128)(2,1)S(1)} %get-tuple-element.24), channel_id=1, source_target_pairs={{0,1},{1,0},{2,3},{3,2},{4,6},{5,7},{6,4},{7,5},{8,9},{9,8},{10,11... | collective-permute-start | bytes 417800 | tf_op jit(solution)/shard_map/ppermute | solution.py:145
  18.6 4.2 %collective-permute-done.10.refs_2_ = bf16[32,2176]{1,0:T(8,128)(2,1)S(1)} collective-permute-done((bf16[32,2176]{1,0:T(8,128)(2,1)S(1)}, bf16[32,2176]{1,0:T(8,128)(2,1)S(1)}, u32[]{:S(2)}, u32[]{:S(2)}) %collective-permute-start.10) | collective-permute-done | bytes 139296 | tf_op jit(solution)/shard_map/ppermute | solution.py:145
  22.8 0.8 %collective-permute-done.11.refs_3_ = bf16[32,2176]{1,0:T(8,128)(2,1)S(1)} collective-permute-done((bf16[32,2176]{1,0:T(8,128)(2,1)S(1)}, bf16[32,2176]{1,0:T(8,128)(2,1)S(1)}, u32[]{:S(2)}, u32[]{:S(2)}) %collective-permute-start.11) | collective-permute-done | bytes 139296 | tf_op jit(solution)/shard_map/ppermute | solution.py:145
  23.5 1.1 %collective-permute-done.9.refs_1_ = bf16[32,2176]{1,0:T(8,128)(2,1)S(1)} collective-permute-done((bf16[32,2176]{1,0:T(8,128)(2,1)S(1)}, bf16[32,2176]{1,0:T(8,128)(2,1)S(1)}, u32[]{:S(2)}, u32[]{:S(2)}) %collective-permute-start.9) | collective-permute-done | bytes 139296 | tf_op jit(solution)/shard_map/ppermute | solution.py:145
  24.6 0.9 %combine.1 = bf16[32,2048]{1,0:T(8,128)(2,1)} custom-call(bf16[32,2176]{1,0:T(8,128)(2,1)S(1)} %get-tuple-element.23.refs_0_, bf16[32,2176]{1,0:T(8,128)(2,1)S(1)} %collective-permute-done.9.refs_1_, bf16[32,2176]{1,0:T(8,128)(2,1)S(1)} %collective-permute-done.10.refs_2_, bf16[32,2176]{1,0:T(8,128)(2,1)S(1)} %collective-permute-done.11.refs_3_), custom_call_target="tpu_custom_call" | custom-call | tf_op jit(solution)/shard_map/combine/pallas_call | solution.py:188
  (10 shorter events, 0.0 us)
Async XLA Ops:
  0.0 0.9 %copy-start.1 = (bf16[32,1024]{1,0:T(8,128)(2,1)S(1)}, bf16[32,1024]{1,0:T(8,128)(2,1)}, u32[]{:S(2)}) copy-start(bf16[32,1024]{1,0:T(8,128)(2,1)} %param.5) | copy-start | bytes 196612
  0.9 9.5 %collective-permute-start = (bf16[64,1024]{1,0:T(8,128)(2,1)S(1)}, bf16[64,1024]{1,0:T(8,128)(2,1)S(1)}, u32[]{:S(2)}, u32[]{:S(2)}) collective-permute-start(bf16[64,1024]{1,0:T(8,128)(2,1)S(1)} %constant_dynamic-update-slice_fusion.refs_0_), channel_id=1, source_target_pairs={{0,24},{4,28},{8,16},{12,20},{16,8},{20,12},{24,0},{28,4},{1,25},{... | collective-permute-start | bytes 393224 | tf_op jit(solution)/shard_map/ppermute | solution.py:130
  6.0 5.6 %collective-permute-start.2 = (bf16[64,1024]{1,0:T(8,128)(2,1)S(1)}, bf16[64,1024]{1,0:T(8,128)(2,1)S(1)}, u32[]{:S(2)}, u32[]{:S(2)}) collective-permute-start(bf16[64,1024]{1,0:T(8,128)(2,1)S(1)} %constant_dynamic-update-slice_fusion.refs_0_), channel_id=1, source_target_pairs={{0,16},{1,17},{2,18},{3,19},{8,24},{9,25},{10,26},{11,27}} | collective-permute-start | bytes 393224 | tf_op jit(solution)/shard_map/ppermute | solution.py:138
  7.3 5.7 %collective-permute-start.4 = (bf16[64,1024]{1,0:T(8,128)(2,1)S(1)}, bf16[64,1024]{1,0:T(8,128)(2,1)S(1)}, u32[]{:S(2)}, u32[]{:S(2)}) collective-permute-start(bf16[64,1024]{1,0:T(8,128)(2,1)S(1)} %constant_dynamic-update-slice_fusion.refs_0_), channel_id=1, source_target_pairs={{0,8},{4,12},{8,0},{12,4},{16,24},{20,28},{24,16},{28,20},{1,9},{5... | collective-permute-start | bytes 393224 | tf_op jit(solution)/shard_map/ppermute | solution.py:130
  8.6 1.0 %copy-start = (bf16[128,2048]{1,0:T(8,128)(2,1)S(1)}, bf16[128,2048]{1,0:T(8,128)(2,1)}, u32[]{:S(2)}) copy-start(bf16[128,2048]{1,0:T(8,128)(2,1)} %q_ref.5) | copy-start | bytes 1572868
  10.4 2.6 %collective-permute-start.3 = (bf16[64,1024]{1,0:T(8,128)(2,1)S(1)}, bf16[64,1024]{1,0:T(8,128)(2,1)S(1)}, u32[]{:S(2)}, u32[]{:S(2)}) collective-permute-start(bf16[64,1024]{1,0:T(8,128)(2,1)S(1)} %collective-permute-done.refs_5_), channel_id=1, source_target_pairs={{20,28},{21,29},{22,30},{23,31},{28,20},{29,21},{30,22},{31,23}} | collective-permute-start | bytes 393224 | tf_op jit(solution)/shard_map/ppermute | solution.py:138
  11.0 2.5 %collective-permute-start.1 = (bf16[64,1024]{1,0:T(8,128)(2,1)S(1)}, bf16[64,1024]{1,0:T(8,128)(2,1)S(1)}, u32[]{:S(2)}, u32[]{:S(2)}) collective-permute-start(bf16[64,1024]{1,0:T(8,128)(2,1)S(1)} %constant_dynamic-update-slice_fusion.refs_0_), channel_id=1, source_target_pairs={{0,4},{4,0},{8,12},{12,8},{16,20},{20,16},{24,28},{28,24},{1,5},{5... | collective-permute-start | bytes 393224 | tf_op jit(solution)/shard_map/ppermute | solution.py:130
  11.1 2.9 %collective-permute-start.7 = (bf16[64,1024]{1,0:T(8,128)(2,1)S(1)}, bf16[64,1024]{1,0:T(8,128)(2,1)S(1)}, u32[]{:S(2)}, u32[]{:S(2)}) collective-permute-start(bf16[64,1024]{1,0:T(8,128)(2,1)S(1)} %collective-permute-done.refs_5_), channel_id=1, source_target_pairs={{0,4},{4,0},{8,12},{12,8},{16,20},{20,16},{24,28},{28,24},{1,5},{5... | collective-permute-start | bytes 393224 | tf_op jit(solution)/shard_map/ppermute | solution.py:130
  11.6 2.4 %collective-permute-start.6 = (bf16[64,1024]{1,0:T(8,128)(2,1)S(1)}, bf16[64,1024]{1,0:T(8,128)(2,1)S(1)}, u32[]{:S(2)}, u32[]{:S(2)}) collective-permute-start(bf16[64,1024]{1,0:T(8,128)(2,1)S(1)} %collective-permute-done.2.refs_3_), channel_id=1, source_target_pairs={{0,4},{4,0},{8,12},{12,8},{16,20},{20,16},{24,28},{28,24},{1,5},{5... | collective-permute-start | bytes 393224 | tf_op jit(solution)/shard_map/ppermute | solution.py:130
  13.0 1.3 %collective-permute-start.8 = (bf16[64,1024]{1,0:T(8,128)(2,1)S(1)}, bf16[64,1024]{1,0:T(8,128)(2,1)S(1)}, u32[]{:S(2)}, u32[]{:S(2)}) collective-permute-start(bf16[64,1024]{1,0:T(8,128)(2,1)S(1)} %collective-permute-done.4.refs_6_), channel_id=1, source_target_pairs={{0,4},{4,0},{8,12},{12,8},{16,20},{20,16},{24,28},{28,24},{1,5},{5... | collective-permute-start | bytes 393224 | tf_op jit(solution)/shard_map/ppermute | solution.py:130
  13.0 1.5 %collective-permute-start.5 = (bf16[64,1024]{1,0:T(8,128)(2,1)S(1)}, bf16[64,1024]{1,0:T(8,128)(2,1)S(1)}, u32[]{:S(2)}, u32[]{:S(2)}) collective-permute-start(bf16[64,1024]{1,0:T(8,128)(2,1)S(1)} %collective-permute-done.3.refs_4_), channel_id=1, source_target_pairs={{0,4},{4,0},{8,12},{12,8},{16,20},{20,16},{24,28},{28,24},{1,5},{5... | collective-permute-start | bytes 393224 | tf_op jit(solution)/shard_map/ppermute | solution.py:130
  15.0 7.8 %collective-permute-start.10 = (bf16[32,2176]{1,0:T(8,128)(2,1)S(1)}, bf16[32,2176]{1,0:T(8,128)(2,1)S(1)}, u32[]{:S(2)}, u32[]{:S(2)}) collective-permute-start(bf16[32,2176]{1,0:T(8,128)(2,1)S(1)} %get-tuple-element.25), channel_id=1, source_target_pairs={{0,2},{1,3},{2,0},{3,1},{4,5},{5,4},{6,7},{7,6},{8,10},{9,11},{10,... | collective-permute-start | bytes 417800 | tf_op jit(solution)/shard_map/ppermute | solution.py:145
  16.6 6.9 %collective-permute-start.11 = (bf16[32,2176]{1,0:T(8,128)(2,1)S(1)}, bf16[32,2176]{1,0:T(8,128)(2,1)S(1)}, u32[]{:S(2)}, u32[]{:S(2)}) collective-permute-start(bf16[32,2176]{1,0:T(8,128)(2,1)S(1)} %get-tuple-element.26), channel_id=1, source_target_pairs={{0,3},{1,2},{2,1},{3,0},{4,7},{5,6},{6,5},{7,4},{8,11},{9,10},{10,... | collective-permute-start | bytes 417800 | tf_op jit(solution)/shard_map/ppermute | solution.py:145
  18.0 6.6 %collective-permute-start.9 = (bf16[32,2176]{1,0:T(8,128)(2,1)S(1)}, bf16[32,2176]{1,0:T(8,128)(2,1)S(1)}, u32[]{:S(2)}, u32[]{:S(2)}) collective-permute-start(bf16[32,2176]{1,0:T(8,128)(2,1)S(1)} %get-tuple-element.24), channel_id=1, source_target_pairs={{0,1},{1,0},{2,3},{3,2},{4,6},{5,7},{6,4},{7,5},{8,9},{9,8},{10,11... | collective-permute-start | bytes 417800 | tf_op jit(solution)/shard_map/ppermute | solution.py:145

commit v6 on v5

--- a/solution.py
+++ b/solution.py
@@ -94,30 +94,46 @@
             if last:
                 numer = numer.astype(jnp.bfloat16)
                 for i, d in enumerate(dests):
-                    outs[d][:, cut] = numer[i * blk : (i + 1) * blk]
+                    for t in range(HEAD // LANES):
+                        at = (h * HEAD // LANES + t) * blk
+                        outs[d][at : at + blk, :] = numer[
+                            i * blk : (i + 1) * blk, t * LANES : (t + 1) * LANES
+                        ]
             else:
                 outs[0][rows, cut] = numer
             total[0] = total[0] + jnp.where(lanes % (LANES // 2) == h, denom, 0.0)
 
         group_sums(masks, blk, n_col, dests, q_ref, k_all, v_all, emit)
         if last:
+            n_heads = feat_q // HEAD
             high = total[0].astype(jnp.bfloat16).astype(jnp.float32)
-            tail = jnp.where(lanes < LANES // 2, high, total[0] - high).astype(jnp.bfloat16)
+            tail = jnp.where(lanes < LANES // 2, high, total[0] - high)
+            tail = jnp.where(lanes % (LANES // 2) < n_heads, tail, 0.0)
             for i, d in enumerate(dests):
-                outs[d][:, feat_q:] = tail[i * blk : (i + 1) * blk]
+                packed = jnp.zeros((8, LANES), jnp.float32)
+                for k in range(blk // 8):
+                    eight = tail[i * blk + k * 8 : i * blk + k * 8 + 8]
+                    packed = packed + (pltpu.roll(eight, k * n_heads, 1) if k else eight)
+                packed = jnp.concatenate([packed, jnp.zeros_like(packed)], axis=0)
+                outs[d][blk * (feat_q // LANES) :, :] = packed.astype(jnp.bfloat16)
         else:
             outs[1][rows, :] = total[0]
 
 
 def combine_kernel(*refs):
     parts, out_ref = refs[:-1], refs[-1]
-    feat_q = out_ref.shape[1]
-    tail = sum(p[:, feat_q:].astype(jnp.float32) for p in parts)
+    blk, feat_q = out_ref.shape
+    n_heads = feat_q // HEAD
+    tail = sum(p[blk * (feat_q // LANES) :, :].astype(jnp.float32) for p in parts)[:8]
     inverse = 1.0 / (tail + pltpu.roll(tail, LANES // 2, 1))
-    for h in range(feat_q // HEAD):
-        cut = slice(h * HEAD, (h + 1) * HEAD)
-        numer = sum(p[:, cut].astype(jnp.float32) for p in parts)
-        out_ref[:, cut] = (numer * inverse[:, h : h + 1]).astype(jnp.bfloat16)
+    for h in range(n_heads):
+        lanes = [k * n_heads + h for k in range(blk // 8)]
+        scale = jnp.concatenate(
+            [jnp.broadcast_to(inverse[:, at : at + 1], (8, LANES)) for at in lanes], axis=0
+        )
+        for t in range(h * HEAD // LANES, (h + 1) * HEAD // LANES):
+            numer = sum(p[t * blk : (t + 1) * blk, :].astype(jnp.float32) for p in parts)
+            out_ref[:, t * LANES : (t + 1) * LANES] = (numer * scale).astype(jnp.bfloat16)
 
 
 def per_device(queries, keys, values):
@@ -145,7 +161,7 @@
         return lax.ppermute(x, ("row", "col"), pairs)
 
     def sums(masks, before, last, name):
-        message = jax.ShapeDtypeStruct((blk, feat_q + LANES), jnp.bfloat16)
+        message = jax.ShapeDtypeStruct((blk * (feat_q // LANES) + 16, LANES), jnp.bfloat16)
         totals = [
             jax.ShapeDtypeStruct((span, feat_q), jnp.float32),
             jax.ShapeDtypeStruct((span, LANES), jnp.float32),

time: 25.7 us -> 25.6 us (level)
  no operation moved by 1% of the time
where the time goes in v6:
time: 25.6 us; the launch traced here: 25.4 us
  starting transfers between devices  13 us (51%)
  waiting for transfers between devices  8.14 us (32%)
  Pallas kernels  2.22 us (9%)
  local copies, waits for them, and re-layouts  1.93 us (8%)
    ppermute x7, starting transfers between devices, swap_row(): return lax.ppermute(x, 'row', [(i, i ^ mask) for i in range(n_row)])  7.49 us
    ppermute x3, waiting for transfers between devices, swap_col(): return lax.ppermute(x, ('row', 'col'), pairs)  5.93 us
    ppermute x3, starting transfers between devices, swap_col(): return lax.ppermute(x, ('row', 'col'), pairs)  3.55 us
    ppermute x7, waiting for transfers between devices, swap_row(): return lax.ppermute(x, 'row', [(i, i ^ mask) for i in range(n_row)])  2.21 us
    ppermute x2, starting transfers between devices, send_up(): return lax.ppermute(x, ('row', 'col'), pairs)  1.99 us
    unnamed x5, local copies, waits for them, and re-layouts  1.92 us
    pallas_call x3, Pallas kernels, sums(): pl.pallas_call(functools.partial(sums_kernel, masks, widths, len(before)...  1.36 us
    pallas_call x1, Pallas kernels, per_device(): pl.pallas_call(combine_kernel, out_shape=jax.ShapeDtypeStruct((blk, feat_...  0.86 us
  transfers between devices with their start and end apart: 12, of which 7 were waited for; matrix products, arithmetic and copies ran while one was open for 0% of the time, Pallas kernels for 3%

profile of v6, /device:TPU:0, one launch (start us, length us, event | category | flops | bytes accessed | tf_op | source)
XLA Modules:
  0.0 25.4 jit_solution(11662823322003724280)
XLA Ops:
  0.0 0.9 %constant_dynamic-update-slice_fusion.1 = bf16[64,1024]{1,0:T(8,128)(2,1)S(1)} fusion(bf16[32,1024]{1,0:T(8,128)(2,1)} %param.4), kind=kLoop, calls=%fused_computation.1 | loop fusion | bytes 131072
  0.9 5.1 %collective-permute-start = (bf16[64,1024]{1,0:T(8,128)(2,1)S(1)}, bf16[64,1024]{1,0:T(8,128)(2,1)S(1)}, u32[]{:S(2)}, u32[]{:S(2)}) collective-permute-start(bf16[64,1024]{1,0:T(8,128)(2,1)S(1)} %constant_dynamic-update-slice_fusion.refs_0_), channel_id=1, source_target_pairs={{0,24},{4,28},{8,16},{12,20},{16,8},{20,12},{24,0},{28,4},{1,25},{... | collective-permute-start | bytes 393224 | tf_op jit(solution)/shard_map/ppermute | solution.py:146
  6.0 1.3 %collective-permute-start.2 = (bf16[64,1024]{1,0:T(8,128)(2,1)S(1)}, bf16[64,1024]{1,0:T(8,128)(2,1)S(1)}, u32[]{:S(2)}, u32[]{:S(2)}) collective-permute-start(bf16[64,1024]{1,0:T(8,128)(2,1)S(1)} %constant_dynamic-update-slice_fusion.refs_0_), channel_id=1, source_target_pairs={{0,16},{1,17},{2,18},{3,19},{8,24},{9,25},{10,26},{11,27}} | collective-permute-start | bytes 393224 | tf_op jit(solution)/shard_map/ppermute | solution.py:154
  7.3 1.2 %collective-permute-start.4 = (bf16[64,1024]{1,0:T(8,128)(2,1)S(1)}, bf16[64,1024]{1,0:T(8,128)(2,1)S(1)}, u32[]{:S(2)}, u32[]{:S(2)}) collective-permute-start(bf16[64,1024]{1,0:T(8,128)(2,1)S(1)} %constant_dynamic-update-slice_fusion.refs_0_), channel_id=1, source_target_pairs={{0,8},{4,12},{8,0},{12,4},{16,24},{20,28},{24,16},{28,20},{1,9},{5... | collective-permute-start | bytes 393224 | tf_op jit(solution)/shard_map/ppermute | solution.py:146
  8.6 1.0 %copy-done = bf16[128,2048]{1,0:T(8,128)(2,1)S(1)} copy-done((bf16[128,2048]{1,0:T(8,128)(2,1)S(1)}, bf16[128,2048]{1,0:T(8,128)(2,1)}, u32[]{:S(2)}) %copy-start) | copy-done | bytes 524312
  9.6 0.4 %own_block.1 = (f32[128,2048]{1,0:T(8,128)S(1)}, f32[128,128]{1,0:T(8,128)S(1)}) custom-call(bf16[128,2048]{1,0:T(8,128)(2,1)S(1)} %copy-done, bf16[64,1024]{1,0:T(8,128)(2,1)S(1)} %constant_dynamic-update-slice_fusion.refs_0_), custom_call_target="tpu_custom_call" | custom-call | tf_op jit(solution)/shard_map/own_block/pallas_call | solution.py:172
  10.0 0.3 %collective-permute-done.refs_5_ = bf16[64,1024]{1,0:T(8,128)(2,1)S(1)} collective-permute-done((bf16[64,1024]{1,0:T(8,128)(2,1)S(1)}, bf16[64,1024]{1,0:T(8,128)(2,1)S(1)}, u32[]{:S(2)}, u32[]{:S(2)}) %collective-permute-start) | collective-permute-done | bytes 131104 | tf_op jit(solution)/shard_map/ppermute | solution.py:146
  10.4 0.7 %collective-permute-start.3 = (bf16[64,1024]{1,0:T(8,128)(2,1)S(1)}, bf16[64,1024]{1,0:T(8,128)(2,1)S(1)}, u32[]{:S(2)}, u32[]{:S(2)}) collective-permute-start(bf16[64,1024]{1,0:T(8,128)(2,1)S(1)} %collective-permute-done.refs_5_), channel_id=1, source_target_pairs={{20,28},{21,29},{22,30},{23,31},{28,20},{29,21},{30,22},{31,23}} | collective-permute-start | bytes 393224 | tf_op jit(solution)/shard_map/ppermute | solution.py:154
  11.0 0.1 collective-permute-start.1
  11.1 0.5 %collective-permute-start.7 = (bf16[64,1024]{1,0:T(8,128)(2,1)S(1)}, bf16[64,1024]{1,0:T(8,128)(2,1)S(1)}, u32[]{:S(2)}, u32[]{:S(2)}) collective-permute-start(bf16[64,1024]{1,0:T(8,128)(2,1)S(1)} %collective-permute-done.refs_5_), channel_id=1, source_target_pairs={{0,4},{4,0},{8,12},{12,8},{16,20},{20,16},{24,28},{28,24},{1,5},{5... | collective-permute-start | bytes 393224 | tf_op jit(solution)/shard_map/ppermute | solution.py:146
  11.6 0.1 collective-permute-start.6
  11.7 1.3 %collective-permute-done.4.refs_6_ = bf16[64,1024]{1,0:T(8,128)(2,1)S(1)} collective-permute-done((bf16[64,1024]{1,0:T(8,128)(2,1)S(1)}, bf16[64,1024]{1,0:T(8,128)(2,1)S(1)}, u32[]{:S(2)}, u32[]{:S(2)}) %collective-permute-start.4) | collective-permute-done | bytes 131104 | tf_op jit(solution)/shard_map/ppermute | solution.py:146
  13.0 0.5 %collective-permute-start.5 = (bf16[64,1024]{1,0:T(8,128)(2,1)S(1)}, bf16[64,1024]{1,0:T(8,128)(2,1)S(1)}, u32[]{:S(2)}, u32[]{:S(2)}) collective-permute-start(bf16[64,1024]{1,0:T(8,128)(2,1)S(1)} %collective-permute-done.3.refs_4_), channel_id=1, source_target_pairs={{0,4},{4,0},{8,12},{12,8},{16,20},{20,16},{24,28},{28,24},{1,5},{5... | collective-permute-start | bytes 393224 | tf_op jit(solution)/shard_map/ppermute | solution.py:146
  13.5 0.5 %far_same_core.1 = (f32[128,2048]{1,0:T(8,128)S(1)}, f32[128,128]{1,0:T(8,128)S(1)}) custom-call(bf16[128,2048]{1,0:T(8,128)(2,1)S(1)} %copy-done, f32[128,2048]{1,0:T(8,128)S(1)} %get-tuple-element.18.refs_0_, f32[128,128]{1,0:T(8,128)S(1)} %get-tuple-element.19.refs_1_, bf16[64,1024]{1,0:T(8,128)(2,1)S(1)} %collective-permute-done.1.refs_2_, ...), custom_call_target="tpu_custom_call" | custom-call | tf_op jit(solution)/shard_map/far_same_core/pallas_call | solution.py:172
  14.0 0.4 %collective-permute-done.8.refs_5_ = bf16[64,1024]{1,0:T(8,128)(2,1)S(1)} collective-permute-done((bf16[64,1024]{1,0:T(8,128)(2,1)S(1)}, bf16[64,1024]{1,0:T(8,128)(2,1)S(1)}, u32[]{:S(2)}, u32[]{:S(2)}) %collective-permute-start.8) | collective-permute-done | bytes 131104 | tf_op jit(solution)/shard_map/ppermute | solution.py:146
  14.4 0.2 collective-permute-done.5.refs_2_
  14.6 0.5 %far_other_core.1 = (bf16[528,128]{1,0:T(8,128)(2,1)S(1)}, bf16[528,128]{1,0:T(8,128)(2,1)S(1)}, bf16[528,128]{1,0:T(8,128)(2,1)S(1)}, bf16[528,128]{1,0:T(8,128)(2,1)S(1)}) custom-call(bf16[128,2048]{1,0:T(8,128)(2,1)S(1)} %copy-done, f32[128,2048]{1,0:T(8,128)S(1)} %get-tuple-element.21.refs_0_, f32[128,128]{1,0:T(8,128)S(1)} %get-tuple-element.22.refs_1_, ...), custom_call_target="tpu_custom_call" | custom-call | tf_op jit(solution)/shard_map/far_other_core/pallas_call | solution.py:172
  15.0 1.6 %collective-permute-start.10 = (bf16[528,128]{1,0:T(8,128)(2,1)S(1)}, bf16[528,128]{1,0:T(8,128)(2,1)S(1)}, u32[]{:S(2)}, u32[]{:S(2)}) collective-permute-start(bf16[528,128]{1,0:T(8,128)(2,1)S(1)} %get-tuple-element.25), channel_id=1, source_target_pairs={{0,2},{1,3},{2,0},{3,1},{4,5},{5,4},{6,7},{7,6},{8,10},{9,11},{10,... | collective-permute-start | bytes 405512 | tf_op jit(solution)/shard_map/ppermute | solution.py:161
  16.6 1.4 %collective-permute-start.11 = (bf16[528,128]{1,0:T(8,128)(2,1)S(1)}, bf16[528,128]{1,0:T(8,128)(2,1)S(1)}, u32[]{:S(2)}, u32[]{:S(2)}) collective-permute-start(bf16[528,128]{1,0:T(8,128)(2,1)S(1)} %get-tuple-element.26), channel_id=1, source_target_pairs={{0,3},{1,2},{2,1},{3,0},{4,7},{5,6},{6,5},{7,4},{8,11},{9,10},{10,... | collective-permute-start | bytes 405512 | tf_op jit(solution)/shard_map/ppermute | solution.py:161
  18.1 0.5 %collective-permute-start.9 = (bf16[528,128]{1,0:T(8,128)(2,1)S(1)}, bf16[528,128]{1,0:T(8,128)(2,1)S(1)}, u32[]{:S(2)}, u32[]{:S(2)}) collective-permute-start(bf16[528,128]{1,0:T(8,128)(2,1)S(1)} %get-tuple-element.24), channel_id=1, source_target_pairs={{0,1},{1,0},{2,3},{3,2},{4,6},{5,7},{6,4},{7,5},{8,9},{9,8},{10,11... | collective-permute-start | bytes 405512 | tf_op jit(solution)/shard_map/ppermute | solution.py:161
  18.6 4.0 %collective-permute-done.10.refs_2_ = bf16[528,128]{1,0:T(8,128)(2,1)S(1)} collective-permute-done((bf16[528,128]{1,0:T(8,128)(2,1)S(1)}, bf16[528,128]{1,0:T(8,128)(2,1)S(1)}, u32[]{:S(2)}, u32[]{:S(2)}) %collective-permute-start.10) | collective-permute-done | bytes 135200 | tf_op jit(solution)/shard_map/ppermute | solution.py:161
  22.6 0.8 %collective-permute-done.11.refs_3_ = bf16[528,128]{1,0:T(8,128)(2,1)S(1)} collective-permute-done((bf16[528,128]{1,0:T(8,128)(2,1)S(1)}, bf16[528,128]{1,0:T(8,128)(2,1)S(1)}, u32[]{:S(2)}, u32[]{:S(2)}) %collective-permute-start.11) | collective-permute-done | bytes 135200 | tf_op jit(solution)/shard_map/ppermute | solution.py:161
  23.4 1.1 %collective-permute-done.9.refs_1_ = bf16[528,128]{1,0:T(8,128)(2,1)S(1)} collective-permute-done((bf16[528,128]{1,0:T(8,128)(2,1)S(1)}, bf16[528,128]{1,0:T(8,128)(2,1)S(1)}, u32[]{:S(2)}, u32[]{:S(2)}) %collective-permute-start.9) | collective-permute-done | bytes 135200 | tf_op jit(solution)/shard_map/ppermute | solution.py:161
  24.5 0.9 %combine.1 = bf16[32,2048]{1,0:T(8,128)(2,1)} custom-call(bf16[528,128]{1,0:T(8,128)(2,1)S(1)} %get-tuple-element.23.refs_0_, bf16[528,128]{1,0:T(8,128)(2,1)S(1)} %collective-permute-done.9.refs_1_, bf16[528,128]{1,0:T(8,128)(2,1)S(1)} %collective-permute-done.10.refs_2_, bf16[528,128]{1,0:T(8,128)(2,1)S(1)} %collective-permute-done.11.refs_3_), custom_call_target="tpu_custom_call" | custom-call | tf_op jit(solution)/shard_map/combine/pallas_call | solution.py:204
  (10 shorter events, 0.0 us)
Async XLA Ops:
  0.0 0.9 %copy-start.1 = (bf16[32,1024]{1,0:T(8,128)(2,1)S(1)}, bf16[32,1024]{1,0:T(8,128)(2,1)}, u32[]{:S(2)}) copy-start(bf16[32,1024]{1,0:T(8,128)(2,1)} %param.5) | copy-start | bytes 196612
  0.9 9.5 %collective-permute-start = (bf16[64,1024]{1,0:T(8,128)(2,1)S(1)}, bf16[64,1024]{1,0:T(8,128)(2,1)S(1)}, u32[]{:S(2)}, u32[]{:S(2)}) collective-permute-start(bf16[64,1024]{1,0:T(8,128)(2,1)S(1)} %constant_dynamic-update-slice_fusion.refs_0_), channel_id=1, source_target_pairs={{0,24},{4,28},{8,16},{12,20},{16,8},{20,12},{24,0},{28,4},{1,25},{... | collective-permute-start | bytes 393224 | tf_op jit(solution)/shard_map/ppermute | solution.py:146
  6.0 5.6 %collective-permute-start.2 = (bf16[64,1024]{1,0:T(8,128)(2,1)S(1)}, bf16[64,1024]{1,0:T(8,128)(2,1)S(1)}, u32[]{:S(2)}, u32[]{:S(2)}) collective-permute-start(bf16[64,1024]{1,0:T(8,128)(2,1)S(1)} %constant_dynamic-update-slice_fusion.refs_0_), channel_id=1, source_target_pairs={{0,16},{1,17},{2,18},{3,19},{8,24},{9,25},{10,26},{11,27}} | collective-permute-start | bytes 393224 | tf_op jit(solution)/shard_map/ppermute | solution.py:154
  7.3 5.7 %collective-permute-start.4 = (bf16[64,1024]{1,0:T(8,128)(2,1)S(1)}, bf16[64,1024]{1,0:T(8,128)(2,1)S(1)}, u32[]{:S(2)}, u32[]{:S(2)}) collective-permute-start(bf16[64,1024]{1,0:T(8,128)(2,1)S(1)} %constant_dynamic-update-slice_fusion.refs_0_), channel_id=1, source_target_pairs={{0,8},{4,12},{8,0},{12,4},{16,24},{20,28},{24,16},{28,20},{1,9},{5... | collective-permute-start | bytes 393224 | tf_op jit(solution)/shard_map/ppermute | solution.py:146
  8.6 1.0 %copy-start = (bf16[128,2048]{1,0:T(8,128)(2,1)S(1)}, bf16[128,2048]{1,0:T(8,128)(2,1)}, u32[]{:S(2)}) copy-start(bf16[128,2048]{1,0:T(8,128)(2,1)} %q_ref.5) | copy-start | bytes 1572868
  10.4 2.6 %collective-permute-start.3 = (bf16[64,1024]{1,0:T(8,128)(2,1)S(1)}, bf16[64,1024]{1,0:T(8,128)(2,1)S(1)}, u32[]{:S(2)}, u32[]{:S(2)}) collective-permute-start(bf16[64,1024]{1,0:T(8,128)(2,1)S(1)} %collective-permute-done.refs_5_), channel_id=1, source_target_pairs={{20,28},{21,29},{22,30},{23,31},{28,20},{29,21},{30,22},{31,23}} | collective-permute-start | bytes 393224 | tf_op jit(solution)/shard_map/ppermute | solution.py:154
  11.0 2.5 %collective-permute-start.1 = (bf16[64,1024]{1,0:T(8,128)(2,1)S(1)}, bf16[64,1024]{1,0:T(8,128)(2,1)S(1)}, u32[]{:S(2)}, u32[]{:S(2)}) collective-permute-start(bf16[64,1024]{1,0:T(8,128)(2,1)S(1)} %constant_dynamic-update-slice_fusion.refs_0_), channel_id=1, source_target_pairs={{0,4},{4,0},{8,12},{12,8},{16,20},{20,16},{24,28},{28,24},{1,5},{5... | collective-permute-start | bytes 393224 | tf_op jit(solution)/shard_map/ppermute | solution.py:146
  11.1 2.9 %collective-permute-start.7 = (bf16[64,1024]{1,0:T(8,128)(2,1)S(1)}, bf16[64,1024]{1,0:T(8,128)(2,1)S(1)}, u32[]{:S(2)}, u32[]{:S(2)}) collective-permute-start(bf16[64,1024]{1,0:T(8,128)(2,1)S(1)} %collective-permute-done.refs_5_), channel_id=1, source_target_pairs={{0,4},{4,0},{8,12},{12,8},{16,20},{20,16},{24,28},{28,24},{1,5},{5... | collective-permute-start | bytes 393224 | tf_op jit(solution)/shard_map/ppermute | solution.py:146
  11.6 2.4 %collective-permute-start.6 = (bf16[64,1024]{1,0:T(8,128)(2,1)S(1)}, bf16[64,1024]{1,0:T(8,128)(2,1)S(1)}, u32[]{:S(2)}, u32[]{:S(2)}) collective-permute-start(bf16[64,1024]{1,0:T(8,128)(2,1)S(1)} %collective-permute-done.2.refs_3_), channel_id=1, source_target_pairs={{0,4},{4,0},{8,12},{12,8},{16,20},{20,16},{24,28},{28,24},{1,5},{5... | collective-permute-start | bytes 393224 | tf_op jit(solution)/shard_map/ppermute | solution.py:146
  13.0 1.3 %collective-permute-start.8 = (bf16[64,1024]{1,0:T(8,128)(2,1)S(1)}, bf16[64,1024]{1,0:T(8,128)(2,1)S(1)}, u32[]{:S(2)}, u32[]{:S(2)}) collective-permute-start(bf16[64,1024]{1,0:T(8,128)(2,1)S(1)} %collective-permute-done.4.refs_6_), channel_id=1, source_target_pairs={{0,4},{4,0},{8,12},{12,8},{16,20},{20,16},{24,28},{28,24},{1,5},{5... | collective-permute-start | bytes 393224 | tf_op jit(solution)/shard_map/ppermute | solution.py:146
  13.0 1.5 %collective-permute-start.5 = (bf16[64,1024]{1,0:T(8,128)(2,1)S(1)}, bf16[64,1024]{1,0:T(8,128)(2,1)S(1)}, u32[]{:S(2)}, u32[]{:S(2)}) collective-permute-start(bf16[64,1024]{1,0:T(8,128)(2,1)S(1)} %collective-permute-done.3.refs_4_), channel_id=1, source_target_pairs={{0,4},{4,0},{8,12},{12,8},{16,20},{20,16},{24,28},{28,24},{1,5},{5... | collective-permute-start | bytes 393224 | tf_op jit(solution)/shard_map/ppermute | solution.py:146
  15.0 7.6 %collective-permute-start.10 = (bf16[528,128]{1,0:T(8,128)(2,1)S(1)}, bf16[528,128]{1,0:T(8,128)(2,1)S(1)}, u32[]{:S(2)}, u32[]{:S(2)}) collective-permute-start(bf16[528,128]{1,0:T(8,128)(2,1)S(1)} %get-tuple-element.25), channel_id=1, source_target_pairs={{0,2},{1,3},{2,0},{3,1},{4,5},{5,4},{6,7},{7,6},{8,10},{9,11},{10,... | collective-permute-start | bytes 405512 | tf_op jit(solution)/shard_map/ppermute | solution.py:161
  16.6 6.8 %collective-permute-start.11 = (bf16[528,128]{1,0:T(8,128)(2,1)S(1)}, bf16[528,128]{1,0:T(8,128)(2,1)S(1)}, u32[]{:S(2)}, u32[]{:S(2)}) collective-permute-start(bf16[528,128]{1,0:T(8,128)(2,1)S(1)} %get-tuple-element.26), channel_id=1, source_target_pairs={{0,3},{1,2},{2,1},{3,0},{4,7},{5,6},{6,5},{7,4},{8,11},{9,10},{10,... | collective-permute-start | bytes 405512 | tf_op jit(solution)/shard_map/ppermute | solution.py:161
  18.1 6.5 %collective-permute-start.9 = (bf16[528,128]{1,0:T(8,128)(2,1)S(1)}, bf16[528,128]{1,0:T(8,128)(2,1)S(1)}, u32[]{:S(2)}, u32[]{:S(2)}) collective-permute-start(bf16[528,128]{1,0:T(8,128)(2,1)S(1)} %get-tuple-element.24), channel_id=1, source_target_pairs={{0,1},{1,0},{2,3},{3,2},{4,6},{5,7},{6,4},{7,5},{8,9},{9,8},{10,11... | collective-permute-start | bytes 405512 | tf_op jit(solution)/shard_map/ppermute | solution.py:161

commit v7 on v6

--- a/solution.py
+++ b/solution.py
@@ -195,7 +195,7 @@
     blocks.update(zip(once, arrived))
     for mask in split:
         blocks[mask].append(send_up(blocks[mask ^ 2][0], mask, (None, 2)))
-    far = split + once + near
+    far = near + split + once
     for mask in [0] + far:
         blocks[mask ^ 1] = [swap_row(x, 1) for x in blocks[mask]][::-1]
     totals = sums([1] + far, totals, False, "far_same_core")

time: 25.6 us -> 25.6 us (level)
    ppermute x7, starting transfers between devices: 7.49 us -> 6.2 us  [swap_row(): return lax.ppermute(x, 'row', [(i, i ^ mask) for i in range(n_row)])]
    ppermute x2, starting transfers between devices: 1.99 us -> 3.2 us  [send_up(): return lax.ppermute(x, ('row', 'col'), pairs)]
    ppermute x2, waiting for transfers between devices: 0.01 us -> 0.61 us  [send_up(): return lax.ppermute(x, ('row', 'col'), pairs)]
    ppermute x7, waiting for transfers between devices: 2.21 us -> 1.69 us  [swap_row(): return lax.ppermute(x, 'row', [(i, i ^ mask) for i in range(n_row)])]
  transfers between devices with their start and end apart: 12 -> 12, of which waited for: 7 -> 8; matrix products, arithmetic and copies ran while one was open for 0% -> 0% of each run, Pallas kernels for 3% -> 3%
where the time goes in v7:
time: 25.6 us; the launch traced here: 25.4 us
  starting transfers between devices  12.9 us (50%)
  waiting for transfers between devices  8.23 us (32%)
  Pallas kernels  2.21 us (9%)
  local copies, waits for them, and re-layouts  1.92 us (8%)
    ppermute x7, starting transfers between devices, swap_row(): return lax.ppermute(x, 'row', [(i, i ^ mask) for i in range(n_row)])  6.2 us
    ppermute x3, waiting for transfers between devices, swap_col(): return lax.ppermute(x, ('row', 'col'), pairs)  5.92 us
    ppermute x3, starting transfers between devices, swap_col(): return lax.ppermute(x, ('row', 'col'), pairs)  3.55 us
    ppermute x2, starting transfers between devices, send_up(): return lax.ppermute(x, ('row', 'col'), pairs)  3.2 us
    unnamed x5, local copies, waits for them, and re-layouts  1.92 us
    ppermute x7, waiting for transfers between devices, swap_row(): return lax.ppermute(x, 'row', [(i, i ^ mask) for i in range(n_row)])  1.69 us
    pallas_call x3, Pallas kernels, sums(): pl.pallas_call(functools.partial(sums_kernel, masks, widths, len(before)...  1.35 us
    pallas_call x1, Pallas kernels, per_device(): pl.pallas_call(combine_kernel, out_shape=jax.ShapeDtypeStruct((blk, feat_...  0.86 us
  transfers between devices with their start and end apart: 12, of which 8 were waited for; matrix products, arithmetic and copies ran while one was open for 0% of the time, Pallas kernels for 3%

profile of v7, /device:TPU:0, one launch (start us, length us, event | category | flops | bytes accessed | tf_op | source)
XLA Modules:
  0.0 25.4 jit_solution(10397394397570218341)
XLA Ops:
  0.0 0.9 %constant_dynamic-update-slice_fusion.1 = bf16[64,1024]{1,0:T(8,128)(2,1)S(1)} fusion(bf16[32,1024]{1,0:T(8,128)(2,1)} %param.4), kind=kLoop, calls=%fused_computation.1 | loop fusion | bytes 131072
  0.9 5.1 %collective-permute-start = (bf16[64,1024]{1,0:T(8,128)(2,1)S(1)}, bf16[64,1024]{1,0:T(8,128)(2,1)S(1)}, u32[]{:S(2)}, u32[]{:S(2)}) collective-permute-start(bf16[64,1024]{1,0:T(8,128)(2,1)S(1)} %constant_dynamic-update-slice_fusion.refs_0_), channel_id=1, source_target_pairs={{0,24},{4,28},{8,16},{12,20},{16,8},{20,12},{24,0},{28,4},{1,25},{... | collective-permute-start | bytes 393224 | tf_op jit(solution)/shard_map/ppermute | solution.py:146
  6.0 2.5 %collective-permute-start.3 = (bf16[64,1024]{1,0:T(8,128)(2,1)S(1)}, bf16[64,1024]{1,0:T(8,128)(2,1)S(1)}, u32[]{:S(2)}, u32[]{:S(2)}) collective-permute-start(bf16[64,1024]{1,0:T(8,128)(2,1)S(1)} %constant_dynamic-update-slice_fusion.refs_0_), channel_id=1, source_target_pairs={{0,16},{1,17},{2,18},{3,19},{8,24},{9,25},{10,26},{11,27}} | collective-permute-start | bytes 393224 | tf_op jit(solution)/shard_map/ppermute | solution.py:154
  8.6 0.0 copy-start
  8.6 1.0 %copy-done = bf16[128,2048]{1,0:T(8,128)(2,1)S(1)} copy-done((bf16[128,2048]{1,0:T(8,128)(2,1)S(1)}, bf16[128,2048]{1,0:T(8,128)(2,1)}, u32[]{:S(2)}) %copy-start) | copy-done | bytes 524312
  9.6 0.4 %own_block.1 = (f32[128,2048]{1,0:T(8,128)S(1)}, f32[128,128]{1,0:T(8,128)S(1)}) custom-call(bf16[128,2048]{1,0:T(8,128)(2,1)S(1)} %copy-done, bf16[64,1024]{1,0:T(8,128)(2,1)S(1)} %constant_dynamic-update-slice_fusion.refs_0_), custom_call_target="tpu_custom_call" | custom-call | tf_op jit(solution)/shard_map/own_block/pallas_call | solution.py:172
  10.0 0.4 %collective-permute-done.refs_6_ = bf16[64,1024]{1,0:T(8,128)(2,1)S(1)} collective-permute-done((bf16[64,1024]{1,0:T(8,128)(2,1)S(1)}, bf16[64,1024]{1,0:T(8,128)(2,1)S(1)}, u32[]{:S(2)}, u32[]{:S(2)}) %collective-permute-start) | collective-permute-done | bytes 131104 | tf_op jit(solution)/shard_map/ppermute | solution.py:146
  10.4 0.7 %collective-permute-start.4 = (bf16[64,1024]{1,0:T(8,128)(2,1)S(1)}, bf16[64,1024]{1,0:T(8,128)(2,1)S(1)}, u32[]{:S(2)}, u32[]{:S(2)}) collective-permute-start(bf16[64,1024]{1,0:T(8,128)(2,1)S(1)} %collective-permute-done.refs_6_), channel_id=1, source_target_pairs={{20,28},{21,29},{22,30},{23,31},{28,20},{29,21},{30,22},{31,23}} | collective-permute-start | bytes 393224 | tf_op jit(solution)/shard_map/ppermute | solution.py:154
  11.0 0.1 collective-permute-start.1
  11.1 0.5 %collective-permute-start.8 = (bf16[64,1024]{1,0:T(8,128)(2,1)S(1)}, bf16[64,1024]{1,0:T(8,128)(2,1)S(1)}, u32[]{:S(2)}, u32[]{:S(2)}) collective-permute-start(bf16[64,1024]{1,0:T(8,128)(2,1)S(1)} %collective-permute-done.refs_6_), channel_id=1, source_target_pairs={{0,4},{4,0},{8,12},{12,8},{16,20},{20,16},{24,28},{28,24},{1,5},{5... | collective-permute-start | bytes 393224 | tf_op jit(solution)/shard_map/ppermute | solution.py:146
  11.6 0.8 %collective-permute-done.2.refs_3_ = bf16[64,1024]{1,0:T(8,128)(2,1)S(1)} collective-permute-done((bf16[64,1024]{1,0:T(8,128)(2,1)S(1)}, bf16[64,1024]{1,0:T(8,128)(2,1)S(1)}, u32[]{:S(2)}, u32[]{:S(2)}) %collective-permute-start.2) | collective-permute-done | bytes 131104 | tf_op jit(solution)/shard_map/ppermute | solution.py:146
  12.4 0.6 %collective-permute-done.3.refs_4_ = bf16[64,1024]{1,0:T(8,128)(2,1)S(1)} collective-permute-done((bf16[64,1024]{1,0:T(8,128)(2,1)S(1)}, bf16[64,1024]{1,0:T(8,128)(2,1)S(1)}, u32[]{:S(2)}, u32[]{:S(2)}) %collective-permute-start.3) | collective-permute-done | bytes 131104 | tf_op jit(solution)/shard_map/ppermute | solution.py:154
  13.0 0.5 %collective-permute-start.6 = (bf16[64,1024]{1,0:T(8,128)(2,1)S(1)}, bf16[64,1024]{1,0:T(8,128)(2,1)S(1)}, u32[]{:S(2)}, u32[]{:S(2)}) collective-permute-start(bf16[64,1024]{1,0:T(8,128)(2,1)S(1)} %collective-permute-done.4.refs_5_), channel_id=1, source_target_pairs={{0,4},{4,0},{8,12},{12,8},{16,20},{20,16},{24,28},{28,24},{1,5},{5... | collective-permute-start | bytes 393224 | tf_op jit(solution)/shard_map/ppermute | solution.py:146
  13.5 0.4 %far_same_core.1 = (f32[128,2048]{1,0:T(8,128)S(1)}, f32[128,128]{1,0:T(8,128)S(1)}) custom-call(bf16[128,2048]{1,0:T(8,128)(2,1)S(1)} %copy-done, f32[128,2048]{1,0:T(8,128)S(1)} %get-tuple-element.18.refs_0_, f32[128,128]{1,0:T(8,128)S(1)} %get-tuple-element.19.refs_1_, bf16[64,1024]{1,0:T(8,128)(2,1)S(1)} %collective-permute-done.1.refs_2_, ...), custom_call_target="tpu_custom_call" | custom-call | tf_op jit(solution)/shard_map/far_same_core/pallas_call | solution.py:172
  14.0 0.4 %collective-permute-done.7.refs_4_ = bf16[64,1024]{1,0:T(8,128)(2,1)S(1)} collective-permute-done((bf16[64,1024]{1,0:T(8,128)(2,1)S(1)}, bf16[64,1024]{1,0:T(8,128)(2,1)S(1)}, u32[]{:S(2)}, u32[]{:S(2)}) %collective-permute-start.7) | collective-permute-done | bytes 131104 | tf_op jit(solution)/shard_map/ppermute | solution.py:146
  14.4 0.2 collective-permute-done.6.refs_3_
  14.6 0.5 %far_other_core.1 = (bf16[528,128]{1,0:T(8,128)(2,1)S(1)}, bf16[528,128]{1,0:T(8,128)(2,1)S(1)}, bf16[528,128]{1,0:T(8,128)(2,1)S(1)}, bf16[528,128]{1,0:T(8,128)(2,1)S(1)}) custom-call(bf16[128,2048]{1,0:T(8,128)(2,1)S(1)} %copy-done, f32[128,2048]{1,0:T(8,128)S(1)} %get-tuple-element.21.refs_0_, f32[128,128]{1,0:T(8,128)S(1)} %get-tuple-element.22.refs_1_, ...), custom_call_target="tpu_custom_call" | custom-call | tf_op jit(solution)/shard_map/far_other_core/pallas_call | solution.py:172
  15.0 1.6 %collective-permute-start.10 = (bf16[528,128]{1,0:T(8,128)(2,1)S(1)}, bf16[528,128]{1,0:T(8,128)(2,1)S(1)}, u32[]{:S(2)}, u32[]{:S(2)}) collective-permute-start(bf16[528,128]{1,0:T(8,128)(2,1)S(1)} %get-tuple-element.25), channel_id=1, source_target_pairs={{0,2},{1,3},{2,0},{3,1},{4,5},{5,4},{6,7},{7,6},{8,10},{9,11},{10,... | collective-permute-start | bytes 405512 | tf_op jit(solution)/shard_map/ppermute | solution.py:161
  16.6 1.4 %collective-permute-start.11 = (bf16[528,128]{1,0:T(8,128)(2,1)S(1)}, bf16[528,128]{1,0:T(8,128)(2,1)S(1)}, u32[]{:S(2)}, u32[]{:S(2)}) collective-permute-start(bf16[528,128]{1,0:T(8,128)(2,1)S(1)} %get-tuple-element.26), channel_id=1, source_target_pairs={{0,3},{1,2},{2,1},{3,0},{4,7},{5,6},{6,5},{7,4},{8,11},{9,10},{10,... | collective-permute-start | bytes 405512 | tf_op jit(solution)/shard_map/ppermute | solution.py:161
  18.1 0.5 %collective-permute-start.9 = (bf16[528,128]{1,0:T(8,128)(2,1)S(1)}, bf16[528,128]{1,0:T(8,128)(2,1)S(1)}, u32[]{:S(2)}, u32[]{:S(2)}) collective-permute-start(bf16[528,128]{1,0:T(8,128)(2,1)S(1)} %get-tuple-element.24), channel_id=1, source_target_pairs={{0,1},{1,0},{2,3},{3,2},{4,6},{5,7},{6,4},{7,5},{8,9},{9,8},{10,11... | collective-permute-start | bytes 405512 | tf_op jit(solution)/shard_map/ppermute | solution.py:161
  18.6 4.0 %collective-permute-done.10.refs_2_ = bf16[528,128]{1,0:T(8,128)(2,1)S(1)} collective-permute-done((bf16[528,128]{1,0:T(8,128)(2,1)S(1)}, bf16[528,128]{1,0:T(8,128)(2,1)S(1)}, u32[]{:S(2)}, u32[]{:S(2)}) %collective-permute-start.10) | collective-permute-done | bytes 135200 | tf_op jit(solution)/shard_map/ppermute | solution.py:161
  22.6 0.8 %collective-permute-done.11.refs_3_ = bf16[528,128]{1,0:T(8,128)(2,1)S(1)} collective-permute-done((bf16[528,128]{1,0:T(8,128)(2,1)S(1)}, bf16[528,128]{1,0:T(8,128)(2,1)S(1)}, u32[]{:S(2)}, u32[]{:S(2)}) %collective-permute-start.11) | collective-permute-done | bytes 135200 | tf_op jit(solution)/shard_map/ppermute | solution.py:161
  23.4 1.1 %collective-permute-done.9.refs_1_ = bf16[528,128]{1,0:T(8,128)(2,1)S(1)} collective-permute-done((bf16[528,128]{1,0:T(8,128)(2,1)S(1)}, bf16[528,128]{1,0:T(8,128)(2,1)S(1)}, u32[]{:S(2)}, u32[]{:S(2)}) %collective-permute-start.9) | collective-permute-done | bytes 135200 | tf_op jit(solution)/shard_map/ppermute | solution.py:161
  24.5 0.9 %combine.1 = bf16[32,2048]{1,0:T(8,128)(2,1)} custom-call(bf16[528,128]{1,0:T(8,128)(2,1)S(1)} %get-tuple-element.23.refs_0_, bf16[528,128]{1,0:T(8,128)(2,1)S(1)} %collective-permute-done.9.refs_1_, bf16[528,128]{1,0:T(8,128)(2,1)S(1)} %collective-permute-done.10.refs_2_, bf16[528,128]{1,0:T(8,128)(2,1)S(1)} %collective-permute-done.11.refs_3_), custom_call_target="tpu_custom_call" | custom-call | tf_op jit(solution)/shard_map/combine/pallas_call | solution.py:204
  (10 shorter events, 0.0 us)
Async XLA Ops:
  0.0 0.9 %copy-start.1 = (bf16[32,1024]{1,0:T(8,128)(2,1)S(1)}, bf16[32,1024]{1,0:T(8,128)(2,1)}, u32[]{:S(2)}) copy-start(bf16[32,1024]{1,0:T(8,128)(2,1)} %param.5) | copy-start | bytes 196612
  0.9 9.5 %collective-permute-start = (bf16[64,1024]{1,0:T(8,128)(2,1)S(1)}, bf16[64,1024]{1,0:T(8,128)(2,1)S(1)}, u32[]{:S(2)}, u32[]{:S(2)}) collective-permute-start(bf16[64,1024]{1,0:T(8,128)(2,1)S(1)} %constant_dynamic-update-slice_fusion.refs_0_), channel_id=1, source_target_pairs={{0,24},{4,28},{8,16},{12,20},{16,8},{20,12},{24,0},{28,4},{1,25},{... | collective-permute-start | bytes 393224 | tf_op jit(solution)/shard_map/ppermute | solution.py:146
  6.0 6.4 %collective-permute-start.2 = (bf16[64,1024]{1,0:T(8,128)(2,1)S(1)}, bf16[64,1024]{1,0:T(8,128)(2,1)S(1)}, u32[]{:S(2)}, u32[]{:S(2)}) collective-permute-start(bf16[64,1024]{1,0:T(8,128)(2,1)S(1)} %constant_dynamic-update-slice_fusion.refs_0_), channel_id=1, source_target_pairs={{0,8},{4,12},{8,0},{12,4},{16,24},{20,28},{24,16},{28,20},{1,9},{5... | collective-permute-start | bytes 393224 | tf_op jit(solution)/shard_map/ppermute | solution.py:146
  6.0 7.0 %collective-permute-start.3 = (bf16[64,1024]{1,0:T(8,128)(2,1)S(1)}, bf16[64,1024]{1,0:T(8,128)(2,1)S(1)}, u32[]{:S(2)}, u32[]{:S(2)}) collective-permute-start(bf16[64,1024]{1,0:T(8,128)(2,1)S(1)} %constant_dynamic-update-slice_fusion.refs_0_), channel_id=1, source_target_pairs={{0,16},{1,17},{2,18},{3,19},{8,24},{9,25},{10,26},{11,27}} | collective-permute-start | bytes 393224 | tf_op jit(solution)/shard_map/ppermute | solution.py:154
  8.6 1.0 %copy-start = (bf16[128,2048]{1,0:T(8,128)(2,1)S(1)}, bf16[128,2048]{1,0:T(8,128)(2,1)}, u32[]{:S(2)}) copy-start(bf16[128,2048]{1,0:T(8,128)(2,1)} %q_ref.5) | copy-start | bytes 1572868
  10.4 2.7 %collective-permute-start.4 = (bf16[64,1024]{1,0:T(8,128)(2,1)S(1)}, bf16[64,1024]{1,0:T(8,128)(2,1)S(1)}, u32[]{:S(2)}, u32[]{:S(2)}) collective-permute-start(bf16[64,1024]{1,0:T(8,128)(2,1)S(1)} %collective-permute-done.refs_6_), channel_id=1, source_target_pairs={{20,28},{21,29},{22,30},{23,31},{28,20},{29,21},{30,22},{31,23}} | collective-permute-start | bytes 393224 | tf_op jit(solution)/shard_map/ppermute | solution.py:154
  11.0 2.5 %collective-permute-start.1 = (bf16[64,1024]{1,0:T(8,128)(2,1)S(1)}, bf16[64,1024]{1,0:T(8,128)(2,1)S(1)}, u32[]{:S(2)}, u32[]{:S(2)}) collective-permute-start(bf16[64,1024]{1,0:T(8,128)(2,1)S(1)} %constant_dynamic-update-slice_fusion.refs_0_), channel_id=1, source_target_pairs={{0,4},{4,0},{8,12},{12,8},{16,20},{20,16},{24,28},{28,24},{1,5},{5... | collective-permute-start | bytes 393224 | tf_op jit(solution)/shard_map/ppermute | solution.py:146
  11.1 2.9 %collective-permute-start.8 = (bf16[64,1024]{1,0:T(8,128)(2,1)S(1)}, bf16[64,1024]{1,0:T(8,128)(2,1)S(1)}, u32[]{:S(2)}, u32[]{:S(2)}) collective-permute-start(bf16[64,1024]{1,0:T(8,128)(2,1)S(1)} %collective-permute-done.refs_6_), channel_id=1, source_target_pairs={{0,4},{4,0},{8,12},{12,8},{16,20},{20,16},{24,28},{28,24},{1,5},{5... | collective-permute-start | bytes 393224 | tf_op jit(solution)/shard_map/ppermute | solution.py:146
  12.4 1.6 %collective-permute-start.5 = (bf16[64,1024]{1,0:T(8,128)(2,1)S(1)}, bf16[64,1024]{1,0:T(8,128)(2,1)S(1)}, u32[]{:S(2)}, u32[]{:S(2)}) collective-permute-start(bf16[64,1024]{1,0:T(8,128)(2,1)S(1)} %collective-permute-done.2.refs_3_), channel_id=1, source_target_pairs={{0,4},{4,0},{8,12},{12,8},{16,20},{20,16},{24,28},{28,24},{1,5},{5... | collective-permute-start | bytes 393224 | tf_op jit(solution)/shard_map/ppermute | solution.py:146
  13.0 1.3 %collective-permute-start.7 = (bf16[64,1024]{1,0:T(8,128)(2,1)S(1)}, bf16[64,1024]{1,0:T(8,128)(2,1)S(1)}, u32[]{:S(2)}, u32[]{:S(2)}) collective-permute-start(bf16[64,1024]{1,0:T(8,128)(2,1)S(1)} %collective-permute-done.3.refs_4_), channel_id=1, source_target_pairs={{0,4},{4,0},{8,12},{12,8},{16,20},{20,16},{24,28},{28,24},{1,5},{5... | collective-permute-start | bytes 393224 | tf_op jit(solution)/shard_map/ppermute | solution.py:146
  13.0 1.5 %collective-permute-start.6 = (bf16[64,1024]{1,0:T(8,128)(2,1)S(1)}, bf16[64,1024]{1,0:T(8,128)(2,1)S(1)}, u32[]{:S(2)}, u32[]{:S(2)}) collective-permute-start(bf16[64,1024]{1,0:T(8,128)(2,1)S(1)} %collective-permute-done.4.refs_5_), channel_id=1, source_target_pairs={{0,4},{4,0},{8,12},{12,8},{16,20},{20,16},{24,28},{28,24},{1,5},{5... | collective-permute-start | bytes 393224 | tf_op jit(solution)/shard_map/ppermute | solution.py:146
  15.0 7.6 %collective-permute-start.10 = (bf16[528,128]{1,0:T(8,128)(2,1)S(1)}, bf16[528,128]{1,0:T(8,128)(2,1)S(1)}, u32[]{:S(2)}, u32[]{:S(2)}) collective-permute-start(bf16[528,128]{1,0:T(8,128)(2,1)S(1)} %get-tuple-element.25), channel_id=1, source_target_pairs={{0,2},{1,3},{2,0},{3,1},{4,5},{5,4},{6,7},{7,6},{8,10},{9,11},{10,... | collective-permute-start | bytes 405512 | tf_op jit(solution)/shard_map/ppermute | solution.py:161
  16.6 6.8 %collective-permute-start.11 = (bf16[528,128]{1,0:T(8,128)(2,1)S(1)}, bf16[528,128]{1,0:T(8,128)(2,1)S(1)}, u32[]{:S(2)}, u32[]{:S(2)}) collective-permute-start(bf16[528,128]{1,0:T(8,128)(2,1)S(1)} %get-tuple-element.26), channel_id=1, source_target_pairs={{0,3},{1,2},{2,1},{3,0},{4,7},{5,6},{6,5},{7,4},{8,11},{9,10},{10,... | collective-permute-start | bytes 405512 | tf_op jit(solution)/shard_map/ppermute | solution.py:161
  18.1 6.5 %collective-permute-start.9 = (bf16[528,128]{1,0:T(8,128)(2,1)S(1)}, bf16[528,128]{1,0:T(8,128)(2,1)S(1)}, u32[]{:S(2)}, u32[]{:S(2)}) collective-permute-start(bf16[528,128]{1,0:T(8,128)(2,1)S(1)} %get-tuple-element.24), channel_id=1, source_target_pairs={{0,1},{1,0},{2,3},{3,2},{4,6},{5,7},{6,4},{7,5},{8,9},{9,8},{10,11... | collective-permute-start | bytes 405512 | tf_op jit(solution)/shard_map/ppermute | solution.py:161

commit v8 on v7

--- a/solution.py
+++ b/solution.py
@@ -198,8 +198,8 @@
     far = near + split + once
     for mask in [0] + far:
         blocks[mask ^ 1] = [swap_row(x, 1) for x in blocks[mask]][::-1]
-    totals = sums([1] + far, totals, False, "far_same_core")
-    messages = sums([m ^ 1 for m in far], totals, True, "far_other_core")
+    totals = sums([1] + far + [m ^ 1 for m in once], totals, False, "all_but_last")
+    messages = sums([m ^ 1 for m in split + near], totals, True, "last")
     received = [messages[0]] + [swap_col(messages[j], j) for j in range(1, n_col)]
     return pl.pallas_call(
         combine_kernel,

time: 25.6 us -> 25.9 us (1.012)
    ppermute x2, waiting for transfers between devices: 0.61 us -> 1.41 us  [send_up(): return lax.ppermute(x, ('row', 'col'), pairs)]
    ppermute x7, waiting for transfers between devices: 1.69 us -> 0.99 us  [swap_row(): return lax.ppermute(x, 'row', [(i, i ^ mask) for i in range(n_row)])]
  transfers between devices with their start and end apart: 12 -> 12, of which waited for: 8 -> 8; matrix products, arithmetic and copies ran while one was open for 0% -> 0% of each run, Pallas kernels for 3% -> 4%
where the time goes in v8:
time: 25.9 us; the launch traced here: 25.6 us
  starting transfers between devices  13 us (50%)
  waiting for transfers between devices  8.25 us (32%)
  Pallas kernels  2.4 us (9%)
  local copies, waits for them, and re-layouts  1.92 us (7%)
    ppermute x7, starting transfers between devices, swap_row(): return lax.ppermute(x, 'row', [(i, i ^ mask) for i in range(n_row)])  6.27 us
    ppermute x3, waiting for transfers between devices, swap_col(): return lax.ppermute(x, ('row', 'col'), pairs)  5.85 us
    ppermute x3, starting transfers between devices, swap_col(): return lax.ppermute(x, ('row', 'col'), pairs)  3.55 us
    ppermute x2, starting transfers between devices, send_up(): return lax.ppermute(x, ('row', 'col'), pairs)  3.2 us
    unnamed x5, local copies, waits for them, and re-layouts  1.92 us
    pallas_call x3, Pallas kernels, sums(): pl.pallas_call(functools.partial(sums_kernel, masks, widths, len(before)...  1.54 us
    ppermute x2, waiting for transfers between devices, send_up(): return lax.ppermute(x, ('row', 'col'), pairs)  1.41 us
    ppermute x7, waiting for transfers between devices, swap_row(): return lax.ppermute(x, 'row', [(i, i ^ mask) for i in range(n_row)])  0.99 us
  transfers between devices with their start and end apart: 12, of which 8 were waited for; matrix products, arithmetic and copies ran while one was open for 0% of the time, Pallas kernels for 4%

profile of v8, /device:TPU:0, one launch (start us, length us, event | category | flops | bytes accessed | tf_op | source)
XLA Modules:
  0.0 25.6 jit_solution(10843356185463710639)
XLA Ops:
  0.0 0.9 %constant_dynamic-update-slice_fusion.1 = bf16[64,1024]{1,0:T(8,128)(2,1)S(1)} fusion(bf16[32,1024]{1,0:T(8,128)(2,1)} %param.4), kind=kLoop, calls=%fused_computation.1 | loop fusion | bytes 131072
  0.9 5.1 %collective-permute-start = (bf16[64,1024]{1,0:T(8,128)(2,1)S(1)}, bf16[64,1024]{1,0:T(8,128)(2,1)S(1)}, u32[]{:S(2)}, u32[]{:S(2)}) collective-permute-start(bf16[64,1024]{1,0:T(8,128)(2,1)S(1)} %constant_dynamic-update-slice_fusion.refs_0_), channel_id=1, source_target_pairs={{0,24},{4,28},{8,16},{12,20},{16,8},{20,12},{24,0},{28,4},{1,25},{... | collective-permute-start | bytes 393224 | tf_op jit(solution)/shard_map/ppermute | solution.py:146
  6.0 2.5 %collective-permute-start.3 = (bf16[64,1024]{1,0:T(8,128)(2,1)S(1)}, bf16[64,1024]{1,0:T(8,128)(2,1)S(1)}, u32[]{:S(2)}, u32[]{:S(2)}) collective-permute-start(bf16[64,1024]{1,0:T(8,128)(2,1)S(1)} %constant_dynamic-update-slice_fusion.refs_0_), channel_id=1, source_target_pairs={{0,16},{1,17},{2,18},{3,19},{8,24},{9,25},{10,26},{11,27}} | collective-permute-start | bytes 393224 | tf_op jit(solution)/shard_map/ppermute | solution.py:154
  8.6 1.0 %copy-done = bf16[128,2048]{1,0:T(8,128)(2,1)S(1)} copy-done((bf16[128,2048]{1,0:T(8,128)(2,1)S(1)}, bf16[128,2048]{1,0:T(8,128)(2,1)}, u32[]{:S(2)}) %copy-start) | copy-done | bytes 524312
  9.6 0.4 %own_block.1 = (f32[128,2048]{1,0:T(8,128)S(1)}, f32[128,128]{1,0:T(8,128)S(1)}) custom-call(bf16[128,2048]{1,0:T(8,128)(2,1)S(1)} %copy-done, bf16[64,1024]{1,0:T(8,128)(2,1)S(1)} %constant_dynamic-update-slice_fusion.refs_0_), custom_call_target="tpu_custom_call" | custom-call | tf_op jit(solution)/shard_map/own_block/pallas_call | solution.py:172
  10.0 0.4 %collective-permute-done.refs_6_ = bf16[64,1024]{1,0:T(8,128)(2,1)S(1)} collective-permute-done((bf16[64,1024]{1,0:T(8,128)(2,1)S(1)}, bf16[64,1024]{1,0:T(8,128)(2,1)S(1)}, u32[]{:S(2)}, u32[]{:S(2)}) %collective-permute-start) | collective-permute-done | bytes 131104 | tf_op jit(solution)/shard_map/ppermute | solution.py:146
  10.4 0.7 %collective-permute-start.4 = (bf16[64,1024]{1,0:T(8,128)(2,1)S(1)}, bf16[64,1024]{1,0:T(8,128)(2,1)S(1)}, u32[]{:S(2)}, u32[]{:S(2)}) collective-permute-start(bf16[64,1024]{1,0:T(8,128)(2,1)S(1)} %collective-permute-done.refs_6_), channel_id=1, source_target_pairs={{20,28},{21,29},{22,30},{23,31},{28,20},{29,21},{30,22},{31,23}} | collective-permute-start | bytes 393224 | tf_op jit(solution)/shard_map/ppermute | solution.py:154
  11.0 0.1 collective-permute-start.1
  11.1 0.5 %collective-permute-start.5 = (bf16[64,1024]{1,0:T(8,128)(2,1)S(1)}, bf16[64,1024]{1,0:T(8,128)(2,1)S(1)}, u32[]{:S(2)}, u32[]{:S(2)}) collective-permute-start(bf16[64,1024]{1,0:T(8,128)(2,1)S(1)} %collective-permute-done.refs_6_), channel_id=1, source_target_pairs={{0,4},{4,0},{8,12},{12,8},{16,20},{20,16},{24,28},{28,24},{1,5},{5... | collective-permute-start | bytes 393224 | tf_op jit(solution)/shard_map/ppermute | solution.py:146
  11.6 1.4 %collective-permute-done.3.refs_4_ = bf16[64,1024]{1,0:T(8,128)(2,1)S(1)} collective-permute-done((bf16[64,1024]{1,0:T(8,128)(2,1)S(1)}, bf16[64,1024]{1,0:T(8,128)(2,1)S(1)}, u32[]{:S(2)}, u32[]{:S(2)}) %collective-permute-start.3) | collective-permute-done | bytes 131104 | tf_op jit(solution)/shard_map/ppermute | solution.py:154
  13.0 0.5 %collective-permute-start.8 = (bf16[64,1024]{1,0:T(8,128)(2,1)S(1)}, bf16[64,1024]{1,0:T(8,128)(2,1)S(1)}, u32[]{:S(2)}, u32[]{:S(2)}) collective-permute-start(bf16[64,1024]{1,0:T(8,128)(2,1)S(1)} %collective-permute-done.2.refs_3_), channel_id=1, source_target_pairs={{0,4},{4,0},{8,12},{12,8},{16,20},{20,16},{24,28},{28,24},{1,5},{5... | collective-permute-start | bytes 393224 | tf_op jit(solution)/shard_map/ppermute | solution.py:146
  13.5 0.1 collective-permute-start.6
  13.6 0.6 %all_but_last.1 = (f32[128,2048]{1,0:T(8,128)S(1)}, f32[128,128]{1,0:T(8,128)S(1)}) custom-call(bf16[128,2048]{1,0:T(8,128)(2,1)S(1)} %copy-done, f32[128,2048]{1,0:T(8,128)S(1)} %get-tuple-element.18.refs_0_, f32[128,128]{1,0:T(8,128)S(1)} %get-tuple-element.19.refs_1_, bf16[64,1024]{1,0:T(8,128)(2,1)S(1)} %collective-permute-done.1.refs_2_, ...), custom_call_target="tpu_custom_call" | custom-call | tf_op jit(solution)/shard_map/all_but_last/pallas_call | solution.py:172
  14.3 0.1 collective-permute-done.7.refs_3_
  14.4 0.2 collective-permute-done.8.refs_4_
  14.6 0.3 %collective-permute-done.6.refs_2_ = bf16[64,1024]{1,0:T(8,128)(2,1)S(1)} collective-permute-done((bf16[64,1024]{1,0:T(8,128)(2,1)S(1)}, bf16[64,1024]{1,0:T(8,128)(2,1)S(1)}, u32[]{:S(2)}, u32[]{:S(2)}) %collective-permute-start.6) | collective-permute-done | bytes 131104 | tf_op jit(solution)/shard_map/ppermute | solution.py:146
  14.9 0.5 %last.1 = (bf16[528,128]{1,0:T(8,128)(2,1)S(1)}, bf16[528,128]{1,0:T(8,128)(2,1)S(1)}, bf16[528,128]{1,0:T(8,128)(2,1)S(1)}, bf16[528,128]{1,0:T(8,128)(2,1)S(1)}) custom-call(bf16[128,2048]{1,0:T(8,128)(2,1)S(1)} %copy-done, f32[128,2048]{1,0:T(8,128)S(1)} %get-tuple-element.21.refs_0_, f32[128,128]{1,0:T(8,128)S(1)} %get-tuple-element.22.refs_1_, ...), custom_call_target="tpu_custom_call" | custom-call | tf_op jit(solution)/shard_map/last/pallas_call | solution.py:172
  15.4 1.6 %collective-permute-start.10 = (bf16[528,128]{1,0:T(8,128)(2,1)S(1)}, bf16[528,128]{1,0:T(8,128)(2,1)S(1)}, u32[]{:S(2)}, u32[]{:S(2)}) collective-permute-start(bf16[528,128]{1,0:T(8,128)(2,1)S(1)} %get-tuple-element.25), channel_id=1, source_target_pairs={{0,2},{1,3},{2,0},{3,1},{4,5},{5,4},{6,7},{7,6},{8,10},{9,11},{10,... | collective-permute-start | bytes 405512 | tf_op jit(solution)/shard_map/ppermute | solution.py:161
  16.9 1.4 %collective-permute-start.11 = (bf16[528,128]{1,0:T(8,128)(2,1)S(1)}, bf16[528,128]{1,0:T(8,128)(2,1)S(1)}, u32[]{:S(2)}, u32[]{:S(2)}) collective-permute-start(bf16[528,128]{1,0:T(8,128)(2,1)S(1)} %get-tuple-element.26), channel_id=1, source_target_pairs={{0,3},{1,2},{2,1},{3,0},{4,7},{5,6},{6,5},{7,4},{8,11},{9,10},{10,... | collective-permute-start | bytes 405512 | tf_op jit(solution)/shard_map/ppermute | solution.py:161
  18.4 0.5 %collective-permute-start.9 = (bf16[528,128]{1,0:T(8,128)(2,1)S(1)}, bf16[528,128]{1,0:T(8,128)(2,1)S(1)}, u32[]{:S(2)}, u32[]{:S(2)}) collective-permute-start(bf16[528,128]{1,0:T(8,128)(2,1)S(1)} %get-tuple-element.24), channel_id=1, source_target_pairs={{0,1},{1,0},{2,3},{3,2},{4,6},{5,7},{6,4},{7,5},{8,9},{9,8},{10,11... | collective-permute-start | bytes 405512 | tf_op jit(solution)/shard_map/ppermute | solution.py:161
  18.9 4.3 %collective-permute-done.10.refs_2_ = bf16[528,128]{1,0:T(8,128)(2,1)S(1)} collective-permute-done((bf16[528,128]{1,0:T(8,128)(2,1)S(1)}, bf16[528,128]{1,0:T(8,128)(2,1)S(1)}, u32[]{:S(2)}, u32[]{:S(2)}) %collective-permute-start.10) | collective-permute-done | bytes 135200 | tf_op jit(solution)/shard_map/ppermute | solution.py:161
  23.2 0.4 %collective-permute-done.11.refs_3_ = bf16[528,128]{1,0:T(8,128)(2,1)S(1)} collective-permute-done((bf16[528,128]{1,0:T(8,128)(2,1)S(1)}, bf16[528,128]{1,0:T(8,128)(2,1)S(1)}, u32[]{:S(2)}, u32[]{:S(2)}) %collective-permute-start.11) | collective-permute-done | bytes 135200 | tf_op jit(solution)/shard_map/ppermute | solution.py:161
  23.6 1.2 %collective-permute-done.9.refs_1_ = bf16[528,128]{1,0:T(8,128)(2,1)S(1)} collective-permute-done((bf16[528,128]{1,0:T(8,128)(2,1)S(1)}, bf16[528,128]{1,0:T(8,128)(2,1)S(1)}, u32[]{:S(2)}, u32[]{:S(2)}) %collective-permute-start.9) | collective-permute-done | bytes 135200 | tf_op jit(solution)/shard_map/ppermute | solution.py:161
  24.8 0.9 %combine.1 = bf16[32,2048]{1,0:T(8,128)(2,1)} custom-call(bf16[528,128]{1,0:T(8,128)(2,1)S(1)} %get-tuple-element.23.refs_0_, bf16[528,128]{1,0:T(8,128)(2,1)S(1)} %collective-permute-done.9.refs_1_, bf16[528,128]{1,0:T(8,128)(2,1)S(1)} %collective-permute-done.10.refs_2_, bf16[528,128]{1,0:T(8,128)(2,1)S(1)} %collective-permute-done.11.refs_3_), custom_call_target="tpu_custom_call" | custom-call | tf_op jit(solution)/shard_map/combine/pallas_call | solution.py:204
  (10 shorter events, 0.0 us)
Async XLA Ops:
  0.0 0.9 %copy-start.1 = (bf16[32,1024]{1,0:T(8,128)(2,1)S(1)}, bf16[32,1024]{1,0:T(8,128)(2,1)}, u32[]{:S(2)}) copy-start(bf16[32,1024]{1,0:T(8,128)(2,1)} %param.5) | copy-start | bytes 196612
  0.9 9.5 %collective-permute-start = (bf16[64,1024]{1,0:T(8,128)(2,1)S(1)}, bf16[64,1024]{1,0:T(8,128)(2,1)S(1)}, u32[]{:S(2)}, u32[]{:S(2)}) collective-permute-start(bf16[64,1024]{1,0:T(8,128)(2,1)S(1)} %constant_dynamic-update-slice_fusion.refs_0_), channel_id=1, source_target_pairs={{0,24},{4,28},{8,16},{12,20},{16,8},{20,12},{24,0},{28,4},{1,25},{... | collective-permute-start | bytes 393224 | tf_op jit(solution)/shard_map/ppermute | solution.py:146
  6.0 7.0 %collective-permute-start.2 = (bf16[64,1024]{1,0:T(8,128)(2,1)S(1)}, bf16[64,1024]{1,0:T(8,128)(2,1)S(1)}, u32[]{:S(2)}, u32[]{:S(2)}) collective-permute-start(bf16[64,1024]{1,0:T(8,128)(2,1)S(1)} %constant_dynamic-update-slice_fusion.refs_0_), channel_id=1, source_target_pairs={{0,8},{4,12},{8,0},{12,4},{16,24},{20,28},{24,16},{28,20},{1,9},{5... | collective-permute-start | bytes 393224 | tf_op jit(solution)/shard_map/ppermute | solution.py:146
  6.0 7.0 %collective-permute-start.3 = (bf16[64,1024]{1,0:T(8,128)(2,1)S(1)}, bf16[64,1024]{1,0:T(8,128)(2,1)S(1)}, u32[]{:S(2)}, u32[]{:S(2)}) collective-permute-start(bf16[64,1024]{1,0:T(8,128)(2,1)S(1)} %constant_dynamic-update-slice_fusion.refs_0_), channel_id=1, source_target_pairs={{0,16},{1,17},{2,18},{3,19},{8,24},{9,25},{10,26},{11,27}} | collective-permute-start | bytes 393224 | tf_op jit(solution)/shard_map/ppermute | solution.py:154
  8.6 1.0 %copy-start = (bf16[128,2048]{1,0:T(8,128)(2,1)S(1)}, bf16[128,2048]{1,0:T(8,128)(2,1)}, u32[]{:S(2)}) copy-start(bf16[128,2048]{1,0:T(8,128)(2,1)} %q_ref.5) | copy-start | bytes 1572868
  10.4 3.2 %collective-permute-start.4 = (bf16[64,1024]{1,0:T(8,128)(2,1)S(1)}, bf16[64,1024]{1,0:T(8,128)(2,1)S(1)}, u32[]{:S(2)}, u32[]{:S(2)}) collective-permute-start(bf16[64,1024]{1,0:T(8,128)(2,1)S(1)} %collective-permute-done.refs_6_), channel_id=1, source_target_pairs={{20,28},{21,29},{22,30},{23,31},{28,20},{29,21},{30,22},{31,23}} | collective-permute-start | bytes 393224 | tf_op jit(solution)/shard_map/ppermute | solution.py:154
  11.0 2.6 %collective-permute-start.1 = (bf16[64,1024]{1,0:T(8,128)(2,1)S(1)}, bf16[64,1024]{1,0:T(8,128)(2,1)S(1)}, u32[]{:S(2)}, u32[]{:S(2)}) collective-permute-start(bf16[64,1024]{1,0:T(8,128)(2,1)S(1)} %constant_dynamic-update-slice_fusion.refs_0_), channel_id=1, source_target_pairs={{0,4},{4,0},{8,12},{12,8},{16,20},{20,16},{24,28},{28,24},{1,5},{5... | collective-permute-start | bytes 393224 | tf_op jit(solution)/shard_map/ppermute | solution.py:146
  11.1 2.5 %collective-permute-start.5 = (bf16[64,1024]{1,0:T(8,128)(2,1)S(1)}, bf16[64,1024]{1,0:T(8,128)(2,1)S(1)}, u32[]{:S(2)}, u32[]{:S(2)}) collective-permute-start(bf16[64,1024]{1,0:T(8,128)(2,1)S(1)} %collective-permute-done.refs_6_), channel_id=1, source_target_pairs={{0,4},{4,0},{8,12},{12,8},{16,20},{20,16},{24,28},{28,24},{1,5},{5... | collective-permute-start | bytes 393224 | tf_op jit(solution)/shard_map/ppermute | solution.py:146
  13.0 1.3 %collective-permute-start.7 = (bf16[64,1024]{1,0:T(8,128)(2,1)S(1)}, bf16[64,1024]{1,0:T(8,128)(2,1)S(1)}, u32[]{:S(2)}, u32[]{:S(2)}) collective-permute-start(bf16[64,1024]{1,0:T(8,128)(2,1)S(1)} %collective-permute-done.3.refs_4_), channel_id=1, source_target_pairs={{0,4},{4,0},{8,12},{12,8},{16,20},{20,16},{24,28},{28,24},{1,5},{5... | collective-permute-start | bytes 393224 | tf_op jit(solution)/shard_map/ppermute | solution.py:146
  13.0 1.5 %collective-permute-start.8 = (bf16[64,1024]{1,0:T(8,128)(2,1)S(1)}, bf16[64,1024]{1,0:T(8,128)(2,1)S(1)}, u32[]{:S(2)}, u32[]{:S(2)}) collective-permute-start(bf16[64,1024]{1,0:T(8,128)(2,1)S(1)} %collective-permute-done.2.refs_3_), channel_id=1, source_target_pairs={{0,4},{4,0},{8,12},{12,8},{16,20},{20,16},{24,28},{28,24},{1,5},{5... | collective-permute-start | bytes 393224 | tf_op jit(solution)/shard_map/ppermute | solution.py:146
  13.5 1.3 %collective-permute-start.6 = (bf16[64,1024]{1,0:T(8,128)(2,1)S(1)}, bf16[64,1024]{1,0:T(8,128)(2,1)S(1)}, u32[]{:S(2)}, u32[]{:S(2)}) collective-permute-start(bf16[64,1024]{1,0:T(8,128)(2,1)S(1)} %collective-permute-done.4.refs_5_), channel_id=1, source_target_pairs={{0,4},{4,0},{8,12},{12,8},{16,20},{20,16},{24,28},{28,24},{1,5},{5... | collective-permute-start | bytes 393224 | tf_op jit(solution)/shard_map/ppermute | solution.py:146
  15.4 7.9 %collective-permute-start.10 = (bf16[528,128]{1,0:T(8,128)(2,1)S(1)}, bf16[528,128]{1,0:T(8,128)(2,1)S(1)}, u32[]{:S(2)}, u32[]{:S(2)}) collective-permute-start(bf16[528,128]{1,0:T(8,128)(2,1)S(1)} %get-tuple-element.25), channel_id=1, source_target_pairs={{0,2},{1,3},{2,0},{3,1},{4,5},{5,4},{6,7},{7,6},{8,10},{9,11},{10,... | collective-permute-start | bytes 405512 | tf_op jit(solution)/shard_map/ppermute | solution.py:161
  16.9 6.7 %collective-permute-start.11 = (bf16[528,128]{1,0:T(8,128)(2,1)S(1)}, bf16[528,128]{1,0:T(8,128)(2,1)S(1)}, u32[]{:S(2)}, u32[]{:S(2)}) collective-permute-start(bf16[528,128]{1,0:T(8,128)(2,1)S(1)} %get-tuple-element.26), channel_id=1, source_target_pairs={{0,3},{1,2},{2,1},{3,0},{4,7},{5,6},{6,5},{7,4},{8,11},{9,10},{10,... | collective-permute-start | bytes 405512 | tf_op jit(solution)/shard_map/ppermute | solution.py:161
  18.4 6.4 %collective-permute-start.9 = (bf16[528,128]{1,0:T(8,128)(2,1)S(1)}, bf16[528,128]{1,0:T(8,128)(2,1)S(1)}, u32[]{:S(2)}, u32[]{:S(2)}) collective-permute-start(bf16[528,128]{1,0:T(8,128)(2,1)S(1)} %get-tuple-element.24), channel_id=1, source_target_pairs={{0,1},{1,0},{2,3},{3,2},{4,6},{5,7},{6,4},{7,5},{8,9},{9,8},{10,11... | collective-permute-start | bytes 405512 | tf_op jit(solution)/shard_map/ppermute | solution.py:161

commit v9 on v6

--- a/solution.py
+++ b/solution.py
@@ -186,6 +186,7 @@
     once = [m for m in range(top, n_row, 2) if m & 2]
     split = [m for m in range(top, n_row, 2) if not m & 2]
     blocks = {0: [own]}
+    partner = swap_row(own, 1)
     for mask in once + near:
         blocks[mask] = [swap_row(own, mask)]
     totals = sums([0], [], False, "own_block")
@@ -196,7 +197,8 @@
     for mask in split:
         blocks[mask].append(send_up(blocks[mask ^ 2][0], mask, (None, 2)))
     far = split + once + near
-    for mask in [0] + far:
+    blocks[1] = [partner]
+    for mask in far:
         blocks[mask ^ 1] = [swap_row(x, 1) for x in blocks[mask]][::-1]
     totals = sums([1] + far, totals, False, "far_same_core")
     messages = sums([m ^ 1 for m in far], totals, True, "far_other_core")

time: 25.6 us -> 25.6 us (level)
  no operation moved by 1% of the time
where the time goes in v9:
time: 25.6 us; the launch traced here: 25.4 us
  starting transfers between devices  13 us (51%)
  waiting for transfers between devices  8.14 us (32%)
  Pallas kernels  2.22 us (9%)
  local copies, waits for them, and re-layouts  1.93 us (8%)
    ppermute x7, starting transfers between devices, swap_row(): return lax.ppermute(x, 'row', [(i, i ^ mask) for i in range(n_row)])  7.49 us
    ppermute x3, waiting for transfers between devices, swap_col(): return lax.ppermute(x, ('row', 'col'), pairs)  5.93 us
    ppermute x3, starting transfers between devices, swap_col(): return lax.ppermute(x, ('row', 'col'), pairs)  3.55 us
    ppermute x7, waiting for transfers between devices, swap_row(): return lax.ppermute(x, 'row', [(i, i ^ mask) for i in range(n_row)])  2.21 us
    ppermute x2, starting transfers between devices, send_up(): return lax.ppermute(x, ('row', 'col'), pairs)  1.99 us
    unnamed x5, local copies, waits for them, and re-layouts  1.92 us
    pallas_call x3, Pallas kernels, sums(): pl.pallas_call(functools.partial(sums_kernel, masks, widths, len(before)...  1.36 us
    pallas_call x1, Pallas kernels, per_device(): pl.pallas_call(combine_kernel, out_shape=jax.ShapeDtypeStruct((blk, feat_...  0.86 us
  transfers between devices with their start and end apart: 12, of which 7 were waited for; matrix products, arithmetic and copies ran while one was open for 0% of the time, Pallas kernels for 3%

profile of v9, /device:TPU:0, one launch (start us, length us, event | category | flops | bytes accessed | tf_op | source)
XLA Modules:
  0.0 25.4 jit_solution(11662823322003724280)
XLA Ops:
  0.0 0.9 %constant_dynamic-update-slice_fusion.1 = bf16[64,1024]{1,0:T(8,128)(2,1)S(1)} fusion(bf16[32,1024]{1,0:T(8,128)(2,1)} %param.4), kind=kLoop, calls=%fused_computation.1 | loop fusion | bytes 131072
  0.9 5.1 %collective-permute-start = (bf16[64,1024]{1,0:T(8,128)(2,1)S(1)}, bf16[64,1024]{1,0:T(8,128)(2,1)S(1)}, u32[]{:S(2)}, u32[]{:S(2)}) collective-permute-start(bf16[64,1024]{1,0:T(8,128)(2,1)S(1)} %constant_dynamic-update-slice_fusion.refs_0_), channel_id=1, source_target_pairs={{0,24},{4,28},{8,16},{12,20},{16,8},{20,12},{24,0},{28,4},{1,25},{... | collective-permute-start | bytes 393224 | tf_op jit(solution)/shard_map/ppermute | solution.py:146
  6.0 1.3 %collective-permute-start.2 = (bf16[64,1024]{1,0:T(8,128)(2,1)S(1)}, bf16[64,1024]{1,0:T(8,128)(2,1)S(1)}, u32[]{:S(2)}, u32[]{:S(2)}) collective-permute-start(bf16[64,1024]{1,0:T(8,128)(2,1)S(1)} %constant_dynamic-update-slice_fusion.refs_0_), channel_id=1, source_target_pairs={{0,16},{1,17},{2,18},{3,19},{8,24},{9,25},{10,26},{11,27}} | collective-permute-start | bytes 393224 | tf_op jit(solution)/shard_map/ppermute | solution.py:154
  7.3 1.2 %collective-permute-start.4 = (bf16[64,1024]{1,0:T(8,128)(2,1)S(1)}, bf16[64,1024]{1,0:T(8,128)(2,1)S(1)}, u32[]{:S(2)}, u32[]{:S(2)}) collective-permute-start(bf16[64,1024]{1,0:T(8,128)(2,1)S(1)} %constant_dynamic-update-slice_fusion.refs_0_), channel_id=1, source_target_pairs={{0,8},{4,12},{8,0},{12,4},{16,24},{20,28},{24,16},{28,20},{1,9},{5... | collective-permute-start | bytes 393224 | tf_op jit(solution)/shard_map/ppermute | solution.py:146
  8.6 1.0 %copy-done = bf16[128,2048]{1,0:T(8,128)(2,1)S(1)} copy-done((bf16[128,2048]{1,0:T(8,128)(2,1)S(1)}, bf16[128,2048]{1,0:T(8,128)(2,1)}, u32[]{:S(2)}) %copy-start) | copy-done | bytes 524312
  9.6 0.4 %own_block.1 = (f32[128,2048]{1,0:T(8,128)S(1)}, f32[128,128]{1,0:T(8,128)S(1)}) custom-call(bf16[128,2048]{1,0:T(8,128)(2,1)S(1)} %copy-done, bf16[64,1024]{1,0:T(8,128)(2,1)S(1)} %constant_dynamic-update-slice_fusion.refs_0_), custom_call_target="tpu_custom_call" | custom-call | tf_op jit(solution)/shard_map/own_block/pallas_call | solution.py:172
  10.0 0.3 %collective-permute-done.refs_5_ = bf16[64,1024]{1,0:T(8,128)(2,1)S(1)} collective-permute-done((bf16[64,1024]{1,0:T(8,128)(2,1)S(1)}, bf16[64,1024]{1,0:T(8,128)(2,1)S(1)}, u32[]{:S(2)}, u32[]{:S(2)}) %collective-permute-start) | collective-permute-done | bytes 131104 | tf_op jit(solution)/shard_map/ppermute | solution.py:146
  10.4 0.7 %collective-permute-start.3 = (bf16[64,1024]{1,0:T(8,128)(2,1)S(1)}, bf16[64,1024]{1,0:T(8,128)(2,1)S(1)}, u32[]{:S(2)}, u32[]{:S(2)}) collective-permute-start(bf16[64,1024]{1,0:T(8,128)(2,1)S(1)} %collective-permute-done.refs_5_), channel_id=1, source_target_pairs={{20,28},{21,29},{22,30},{23,31},{28,20},{29,21},{30,22},{31,23}} | collective-permute-start | bytes 393224 | tf_op jit(solution)/shard_map/ppermute | solution.py:154
  11.0 0.1 collective-permute-start.1
  11.1 0.5 %collective-permute-start.7 = (bf16[64,1024]{1,0:T(8,128)(2,1)S(1)}, bf16[64,1024]{1,0:T(8,128)(2,1)S(1)}, u32[]{:S(2)}, u32[]{:S(2)}) collective-permute-start(bf16[64,1024]{1,0:T(8,128)(2,1)S(1)} %collective-permute-done.refs_5_), channel_id=1, source_target_pairs={{0,4},{4,0},{8,12},{12,8},{16,20},{20,16},{24,28},{28,24},{1,5},{5... | collective-permute-start | bytes 393224 | tf_op jit(solution)/shard_map/ppermute | solution.py:146
  11.6 0.1 collective-permute-start.6
  11.7 1.3 %collective-permute-done.4.refs_6_ = bf16[64,1024]{1,0:T(8,128)(2,1)S(1)} collective-permute-done((bf16[64,1024]{1,0:T(8,128)(2,1)S(1)}, bf16[64,1024]{1,0:T(8,128)(2,1)S(1)}, u32[]{:S(2)}, u32[]{:S(2)}) %collective-permute-start.4) | collective-permute-done | bytes 131104 | tf_op jit(solution)/shard_map/ppermute | solution.py:146
  13.0 0.5 %collective-permute-start.5 = (bf16[64,1024]{1,0:T(8,128)(2,1)S(1)}, bf16[64,1024]{1,0:T(8,128)(2,1)S(1)}, u32[]{:S(2)}, u32[]{:S(2)}) collective-permute-start(bf16[64,1024]{1,0:T(8,128)(2,1)S(1)} %collective-permute-done.3.refs_4_), channel_id=1, source_target_pairs={{0,4},{4,0},{8,12},{12,8},{16,20},{20,16},{24,28},{28,24},{1,5},{5... | collective-permute-start | bytes 393224 | tf_op jit(solution)/shard_map/ppermute | solution.py:146
  13.5 0.5 %far_same_core.1 = (f32[128,2048]{1,0:T(8,128)S(1)}, f32[128,128]{1,0:T(8,128)S(1)}) custom-call(bf16[128,2048]{1,0:T(8,128)(2,1)S(1)} %copy-done, f32[128,2048]{1,0:T(8,128)S(1)} %get-tuple-element.18.refs_0_, f32[128,128]{1,0:T(8,128)S(1)} %get-tuple-element.19.refs_1_, bf16[64,1024]{1,0:T(8,128)(2,1)S(1)} %collective-permute-done.1.refs_2_, ...), custom_call_target="tpu_custom_call" | custom-call | tf_op jit(solution)/shard_map/far_same_core/pallas_call | solution.py:172
  14.0 0.4 %collective-permute-done.8.refs_5_ = bf16[64,1024]{1,0:T(8,128)(2,1)S(1)} collective-permute-done((bf16[64,1024]{1,0:T(8,128)(2,1)S(1)}, bf16[64,1024]{1,0:T(8,128)(2,1)S(1)}, u32[]{:S(2)}, u32[]{:S(2)}) %collective-permute-start.8) | collective-permute-done | bytes 131104 | tf_op jit(solution)/shard_map/ppermute | solution.py:146
  14.4 0.2 collective-permute-done.5.refs_2_
  14.6 0.5 %far_other_core.1 = (bf16[528,128]{1,0:T(8,128)(2,1)S(1)}, bf16[528,128]{1,0:T(8,128)(2,1)S(1)}, bf16[528,128]{1,0:T(8,128)(2,1)S(1)}, bf16[528,128]{1,0:T(8,128)(2,1)S(1)}) custom-call(bf16[128,2048]{1,0:T(8,128)(2,1)S(1)} %copy-done, f32[128,2048]{1,0:T(8,128)S(1)} %get-tuple-element.21.refs_0_, f32[128,128]{1,0:T(8,128)S(1)} %get-tuple-element.22.refs_1_, ...), custom_call_target="tpu_custom_call" | custom-call | tf_op jit(solution)/shard_map/far_other_core/pallas_call | solution.py:172
  15.0 1.6 %collective-permute-start.10 = (bf16[528,128]{1,0:T(8,128)(2,1)S(1)}, bf16[528,128]{1,0:T(8,128)(2,1)S(1)}, u32[]{:S(2)}, u32[]{:S(2)}) collective-permute-start(bf16[528,128]{1,0:T(8,128)(2,1)S(1)} %get-tuple-element.25), channel_id=1, source_target_pairs={{0,2},{1,3},{2,0},{3,1},{4,5},{5,4},{6,7},{7,6},{8,10},{9,11},{10,... | collective-permute-start | bytes 405512 | tf_op jit(solution)/shard_map/ppermute | solution.py:161
  16.6 1.4 %collective-permute-start.11 = (bf16[528,128]{1,0:T(8,128)(2,1)S(1)}, bf16[528,128]{1,0:T(8,128)(2,1)S(1)}, u32[]{:S(2)}, u32[]{:S(2)}) collective-permute-start(bf16[528,128]{1,0:T(8,128)(2,1)S(1)} %get-tuple-element.26), channel_id=1, source_target_pairs={{0,3},{1,2},{2,1},{3,0},{4,7},{5,6},{6,5},{7,4},{8,11},{9,10},{10,... | collective-permute-start | bytes 405512 | tf_op jit(solution)/shard_map/ppermute | solution.py:161
  18.1 0.5 %collective-permute-start.9 = (bf16[528,128]{1,0:T(8,128)(2,1)S(1)}, bf16[528,128]{1,0:T(8,128)(2,1)S(1)}, u32[]{:S(2)}, u32[]{:S(2)}) collective-permute-start(bf16[528,128]{1,0:T(8,128)(2,1)S(1)} %get-tuple-element.24), channel_id=1, source_target_pairs={{0,1},{1,0},{2,3},{3,2},{4,6},{5,7},{6,4},{7,5},{8,9},{9,8},{10,11... | collective-permute-start | bytes 405512 | tf_op jit(solution)/shard_map/ppermute | solution.py:161
  18.6 4.0 %collective-permute-done.10.refs_2_ = bf16[528,128]{1,0:T(8,128)(2,1)S(1)} collective-permute-done((bf16[528,128]{1,0:T(8,128)(2,1)S(1)}, bf16[528,128]{1,0:T(8,128)(2,1)S(1)}, u32[]{:S(2)}, u32[]{:S(2)}) %collective-permute-start.10) | collective-permute-done | bytes 135200 | tf_op jit(solution)/shard_map/ppermute | solution.py:161
  22.6 0.8 %collective-permute-done.11.refs_3_ = bf16[528,128]{1,0:T(8,128)(2,1)S(1)} collective-permute-done((bf16[528,128]{1,0:T(8,128)(2,1)S(1)}, bf16[528,128]{1,0:T(8,128)(2,1)S(1)}, u32[]{:S(2)}, u32[]{:S(2)}) %collective-permute-start.11) | collective-permute-done | bytes 135200 | tf_op jit(solution)/shard_map/ppermute | solution.py:161
  23.4 1.1 %collective-permute-done.9.refs_1_ = bf16[528,128]{1,0:T(8,128)(2,1)S(1)} collective-permute-done((bf16[528,128]{1,0:T(8,128)(2,1)S(1)}, bf16[528,128]{1,0:T(8,128)(2,1)S(1)}, u32[]{:S(2)}, u32[]{:S(2)}) %collective-permute-start.9) | collective-permute-done | bytes 135200 | tf_op jit(solution)/shard_map/ppermute | solution.py:161
  24.5 0.9 %combine.1 = bf16[32,2048]{1,0:T(8,128)(2,1)} custom-call(bf16[528,128]{1,0:T(8,128)(2,1)S(1)} %get-tuple-element.23.refs_0_, bf16[528,128]{1,0:T(8,128)(2,1)S(1)} %collective-permute-done.9.refs_1_, bf16[528,128]{1,0:T(8,128)(2,1)S(1)} %collective-permute-done.10.refs_2_, bf16[528,128]{1,0:T(8,128)(2,1)S(1)} %collective-permute-done.11.refs_3_), custom_call_target="tpu_custom_call" | custom-call | tf_op jit(solution)/shard_map/combine/pallas_call | solution.py:206
  (10 shorter events, 0.0 us)
Async XLA Ops:
  0.0 0.9 %copy-start.1 = (bf16[32,1024]{1,0:T(8,128)(2,1)S(1)}, bf16[32,1024]{1,0:T(8,128)(2,1)}, u32[]{:S(2)}) copy-start(bf16[32,1024]{1,0:T(8,128)(2,1)} %param.5) | copy-start | bytes 196612
  0.9 9.5 %collective-permute-start = (bf16[64,1024]{1,0:T(8,128)(2,1)S(1)}, bf16[64,1024]{1,0:T(8,128)(2,1)S(1)}, u32[]{:S(2)}, u32[]{:S(2)}) collective-permute-start(bf16[64,1024]{1,0:T(8,128)(2,1)S(1)} %constant_dynamic-update-slice_fusion.refs_0_), channel_id=1, source_target_pairs={{0,24},{4,28},{8,16},{12,20},{16,8},{20,12},{24,0},{28,4},{1,25},{... | collective-permute-start | bytes 393224 | tf_op jit(solution)/shard_map/ppermute | solution.py:146
  6.0 5.6 %collective-permute-start.2 = (bf16[64,1024]{1,0:T(8,128)(2,1)S(1)}, bf16[64,1024]{1,0:T(8,128)(2,1)S(1)}, u32[]{:S(2)}, u32[]{:S(2)}) collective-permute-start(bf16[64,1024]{1,0:T(8,128)(2,1)S(1)} %constant_dynamic-update-slice_fusion.refs_0_), channel_id=1, source_target_pairs={{0,16},{1,17},{2,18},{3,19},{8,24},{9,25},{10,26},{11,27}} | collective-permute-start | bytes 393224 | tf_op jit(solution)/shard_map/ppermute | solution.py:154
  7.3 5.7 %collective-permute-start.4 = (bf16[64,1024]{1,0:T(8,128)(2,1)S(1)}, bf16[64,1024]{1,0:T(8,128)(2,1)S(1)}, u32[]{:S(2)}, u32[]{:S(2)}) collective-permute-start(bf16[64,1024]{1,0:T(8,128)(2,1)S(1)} %constant_dynamic-update-slice_fusion.refs_0_), channel_id=1, source_target_pairs={{0,8},{4,12},{8,0},{12,4},{16,24},{20,28},{24,16},{28,20},{1,9},{5... | collective-permute-start | bytes 393224 | tf_op jit(solution)/shard_map/ppermute | solution.py:146
  8.6 1.0 %copy-start = (bf16[128,2048]{1,0:T(8,128)(2,1)S(1)}, bf16[128,2048]{1,0:T(8,128)(2,1)}, u32[]{:S(2)}) copy-start(bf16[128,2048]{1,0:T(8,128)(2,1)} %q_ref.5) | copy-start | bytes 1572868
  10.4 2.6 %collective-permute-start.3 = (bf16[64,1024]{1,0:T(8,128)(2,1)S(1)}, bf16[64,1024]{1,0:T(8,128)(2,1)S(1)}, u32[]{:S(2)}, u32[]{:S(2)}) collective-permute-start(bf16[64,1024]{1,0:T(8,128)(2,1)S(1)} %collective-permute-done.refs_5_), channel_id=1, source_target_pairs={{20,28},{21,29},{22,30},{23,31},{28,20},{29,21},{30,22},{31,23}} | collective-permute-start | bytes 393224 | tf_op jit(solution)/shard_map/ppermute | solution.py:154
  11.0 2.5 %collective-permute-start.1 = (bf16[64,1024]{1,0:T(8,128)(2,1)S(1)}, bf16[64,1024]{1,0:T(8,128)(2,1)S(1)}, u32[]{:S(2)}, u32[]{:S(2)}) collective-permute-start(bf16[64,1024]{1,0:T(8,128)(2,1)S(1)} %constant_dynamic-update-slice_fusion.refs_0_), channel_id=1, source_target_pairs={{0,4},{4,0},{8,12},{12,8},{16,20},{20,16},{24,28},{28,24},{1,5},{5... | collective-permute-start | bytes 393224 | tf_op jit(solution)/shard_map/ppermute | solution.py:146
  11.1 2.9 %collective-permute-start.7 = (bf16[64,1024]{1,0:T(8,128)(2,1)S(1)}, bf16[64,1024]{1,0:T(8,128)(2,1)S(1)}, u32[]{:S(2)}, u32[]{:S(2)}) collective-permute-start(bf16[64,1024]{1,0:T(8,128)(2,1)S(1)} %collective-permute-done.refs_5_), channel_id=1, source_target_pairs={{0,4},{4,0},{8,12},{12,8},{16,20},{20,16},{24,28},{28,24},{1,5},{5... | collective-permute-start | bytes 393224 | tf_op jit(solution)/shard_map/ppermute | solution.py:146
  11.6 2.4 %collective-permute-start.6 = (bf16[64,1024]{1,0:T(8,128)(2,1)S(1)}, bf16[64,1024]{1,0:T(8,128)(2,1)S(1)}, u32[]{:S(2)}, u32[]{:S(2)}) collective-permute-start(bf16[64,1024]{1,0:T(8,128)(2,1)S(1)} %collective-permute-done.2.refs_3_), channel_id=1, source_target_pairs={{0,4},{4,0},{8,12},{12,8},{16,20},{20,16},{24,28},{28,24},{1,5},{5... | collective-permute-start | bytes 393224 | tf_op jit(solution)/shard_map/ppermute | solution.py:146
  13.0 1.3 %collective-permute-start.8 = (bf16[64,1024]{1,0:T(8,128)(2,1)S(1)}, bf16[64,1024]{1,0:T(8,128)(2,1)S(1)}, u32[]{:S(2)}, u32[]{:S(2)}) collective-permute-start(bf16[64,1024]{1,0:T(8,128)(2,1)S(1)} %collective-permute-done.4.refs_6_), channel_id=1, source_target_pairs={{0,4},{4,0},{8,12},{12,8},{16,20},{20,16},{24,28},{28,24},{1,5},{5... | collective-permute-start | bytes 393224 | tf_op jit(solution)/shard_map/ppermute | solution.py:146
  13.0 1.5 %collective-permute-start.5 = (bf16[64,1024]{1,0:T(8,128)(2,1)S(1)}, bf16[64,1024]{1,0:T(8,128)(2,1)S(1)}, u32[]{:S(2)}, u32[]{:S(2)}) collective-permute-start(bf16[64,1024]{1,0:T(8,128)(2,1)S(1)} %collective-permute-done.3.refs_4_), channel_id=1, source_target_pairs={{0,4},{4,0},{8,12},{12,8},{16,20},{20,16},{24,28},{28,24},{1,5},{5... | collective-permute-start | bytes 393224 | tf_op jit(solution)/shard_map/ppermute | solution.py:146
  15.0 7.6 %collective-permute-start.10 = (bf16[528,128]{1,0:T(8,128)(2,1)S(1)}, bf16[528,128]{1,0:T(8,128)(2,1)S(1)}, u32[]{:S(2)}, u32[]{:S(2)}) collective-permute-start(bf16[528,128]{1,0:T(8,128)(2,1)S(1)} %get-tuple-element.25), channel_id=1, source_target_pairs={{0,2},{1,3},{2,0},{3,1},{4,5},{5,4},{6,7},{7,6},{8,10},{9,11},{10,... | collective-permute-start | bytes 405512 | tf_op jit(solution)/shard_map/ppermute | solution.py:161
  16.6 6.8 %collective-permute-start.11 = (bf16[528,128]{1,0:T(8,128)(2,1)S(1)}, bf16[528,128]{1,0:T(8,128)(2,1)S(1)}, u32[]{:S(2)}, u32[]{:S(2)}) collective-permute-start(bf16[528,128]{1,0:T(8,128)(2,1)S(1)} %get-tuple-element.26), channel_id=1, source_target_pairs={{0,3},{1,2},{2,1},{3,0},{4,7},{5,6},{6,5},{7,4},{8,11},{9,10},{10,... | collective-permute-start | bytes 405512 | tf_op jit(solution)/shard_map/ppermute | solution.py:161
  18.1 6.5 %collective-permute-start.9 = (bf16[528,128]{1,0:T(8,128)(2,1)S(1)}, bf16[528,128]{1,0:T(8,128)(2,1)S(1)}, u32[]{:S(2)}, u32[]{:S(2)}) collective-permute-start(bf16[528,128]{1,0:T(8,128)(2,1)S(1)} %get-tuple-element.24), channel_id=1, source_target_pairs={{0,1},{1,0},{2,3},{3,2},{4,6},{5,7},{6,4},{7,5},{8,9},{9,8},{10,11... | collective-permute-start | bytes 405512 | tf_op jit(solution)/shard_map/ppermute | solution.py:161
